TPU v7x, 32 devices: a whole 2x2x4 slice. The times are simulated.
32 devices in a mesh: replica: 4 (over z), tensor: 4 (over y, x), section: 2 (over core).
Axes of the slice: x: 2, y: 2, z: 4, core: 2. Of those that a mesh axis runs over, the one named last changes fastest.
Arguments:
- grads: bfloat16 [4, 2, 1024, 1024], P('replica', 'section', None, 'tensor'), may hold values from -250 to 250
- errors: bfloat16 [4, 2, 1024, 1024], P('replica', 'section', None, 'tensor'), may hold values from -3 to 3
- q_start: float32 [2, 1024, 32], P('section', 'tensor'), may hold values from -6 to 6
- momentum: float32 [2, 1024, 1024], P('section', 'replica', 'tensor'), may hold values from -6 to 6
- vec_grads: float32 [4, 2, 1024], P('replica', 'section', 'tensor'), may hold values from -6 to 6
- vec_momentum: float32 [2, 1024], P('section', 'tensor'), may hold values from -6 to 6
Outputs:
- new_errors: bfloat16 [4, 2, 1024, 1024], P('replica', 'section', None, 'tensor')
- new_momentum: float32 [2, 1024, 1024], P('section', 'replica', 'tensor')
- new_vec_momentum: float32 [2, 1024], P('section', 'tensor')
All inputs are finite; a program needn't handle non-finite values.
Results may differ from a plain program's by a relative error of at most 0.0034.
The roundings to bfloat16 on the way count: a program that leaves them out, or rounds other values in their place, can miss the bound.
Values may be sent and summed in bfloat16 or wider, within the bound.
No kernel may reach another device: no remote copies, remote signals or barrier semaphores. Data moves between devices by JAX's collectives and lax.ppermute only.
A program may use at most 64 MiB of HBM per device.

v0:
```python
import jax
import jax.numpy as jnp
from jax import lax
from jax.sharding import PartitionSpec as P

ROUNDS = 2


def solve_rows(factor, p_rows):

    def solve_one(lower, matrix):
        return jax.scipy.linalg.solve_triangular(lower, matrix.T, lower=True).T

    return jax.vmap(solve_one)(factor, p_rows)


def body(grads, errors, q_start, momentum, vec_grads, vec_momentum):
    replicas = lax.axis_size("replica")
    merged = (grads[0].astype(jnp.float32) + errors[0].astype(jnp.float32)).astype(jnp.bfloat16)
    q_lo = q_start.astype(jnp.bfloat16)
    vec_sum = None
    vec_sum = lax.psum(vec_grads[0], "replica")
    p_lo = None
    for round_no in range(ROUNDS):
        p_part = jnp.einsum("bdc,bcr->bdr", merged, q_lo, preferred_element_type=jnp.float32)
        p_sum = lax.psum(p_part, ("replica", "tensor")) / replicas
        gram_mat = jnp.einsum("bdr,bds->brs", p_sum, p_sum, precision=lax.Precision.HIGHEST)
        factor = jnp.linalg.cholesky(gram_mat)
        p_lo = solve_rows(factor, p_sum).astype(jnp.bfloat16)
        q_part = jnp.einsum("bdc,bdr->bcr", merged, p_lo, preferred_element_type=jnp.float32)
        q_total = lax.psum(q_part, "replica")
        q_lo = (q_total / replicas).astype(jnp.bfloat16)
    approx = jnp.einsum("bdr,bcr->bdc", p_lo, q_lo, preferred_element_type=jnp.float32)
    new_errors = (merged.astype(jnp.float32) - approx).astype(jnp.bfloat16)[None]
    own_rows = momentum.shape[1]
    first_row = lax.axis_index("replica") * own_rows
    p_mine = lax.dynamic_slice_in_dim(p_lo, first_row, own_rows, 1)
    approx_mine = jnp.einsum("bdr,bcr->bdc", p_mine, q_lo, preferred_element_type=jnp.float32)
    new_momentum = 0.9 * momentum + approx_mine
    new_vec_momentum = 0.9 * vec_momentum + vec_sum / replicas
    return (new_errors, new_momentum, new_vec_momentum)


def solution(mesh):
    placed = (
        P("replica", "section", None, "tensor"),
        P("replica", "section", None, "tensor"),
        P("section", "tensor", None),
        P("section", "replica", "tensor"),
        P("replica", "section", "tensor"),
        P("section", "tensor"),
    )
    return jax.shard_map(
        body,
        mesh=mesh,
        in_specs=placed,
        out_specs=(
            P("replica", "section", None, "tensor"),
            P("section", "replica", "tensor"),
            P("section", "tensor"),
        ),
        check_vma=False,
    )
```

profile of v0, /device:TPU:0, one launch (start us, length us, event | category | flops | bytes accessed | tf_op | source)
XLA Modules:
  0.0 288.0 jit_solution(7557517772357898132)
XLA Ops:
  7.2 0.0 copy-start.3
  7.2 0.0 all-reduce.4.cloned.1.call-start
  7.2 1.3 fusion.6
  8.6 0.0 copy-done.3
  8.6 0.9 convolution_bitcast_fusion.2
  9.5 0.0 all-reduce.4.cloned.1.call-update
  9.5 0.0 all-reduce.6.cloned.1.call-start
  9.6 111.4 %all-reduce.4.cloned.1.call-done = f32[1,1024,32]{1,2,0:T(8,128)} async-done(((f32[1,1024,32]{1,2,0:T(8,128)}), f32[1,1024,32]{1,2,0:T(8,128)}) %all-reduce.4.cloned.1.call-update) | async-done | bytes 131088 | tf_op jit(solution)/shard_map/psum | solution.py:26
  121.0 0.0 copy-start.1
  121.0 1.3 fusion.11
  122.3 0.1 copy.10
  122.4 2.9 %custom-call.8 = f32[1,32,32]{2,1,0:T(8,128)S(1)} custom-call(f32[1,32,32]{2,1,0:T(8,128)S(1)} %fusion.30), custom_call_target="Cholesky" | custom-call | tf_op jit(solution)/shard_map/jit(cholesky)/cholesky | solution.py:28
  125.3 0.6 compare_reduce_fusion.1
  126.0 0.7 fusion.23
  126.6 2.4 custom-call.9
  129.1 0.0 copy-done.1
  129.1 0.3 fusion.5
  129.4 0.2 convolution_bitcast_fusion.6
  129.6 18.0 %psum.36 = f32[1,256,32]{1,2,0:T(8,128)S(1)} all-reduce(f32[1,256,32]{1,2,0:T(8,128)S(1)} %convolution_bitcast_fusion.6), channel_id=1, replica_groups=mesh['replica'=4,'tensor'=4,'section'=2] {'replica'}, use_global_device_ids=true, to_apply=%region_3.0 | all-reduce | flops 8192 | bytes 65536 | tf_op jit(solution)/shard_map/psum | solution.py:31
  147.6 0.9 convolution_bitcast_fusion.1
  148.5 0.0 all-reduce.6.cloned.1.call-update
  148.6 101.7 %all-reduce.6.cloned.1.call-done = f32[1,1024,32]{1,2,0:T(8,128)} async-done(((f32[1,1024,32]{1,2,0:T(8,128)}), f32[1,1024,32]{1,2,0:T(8,128)}) %all-reduce.6.cloned.1.call-update) | async-done | bytes 131088 | tf_op jit(solution)/shard_map/psum | solution.py:26
  250.2 0.0 copy-start
  250.2 1.3 fusion.9
  251.5 0.1 copy.12
  251.6 2.9 %custom-call.10 = f32[1,32,32]{2,1,0:T(8,128)S(1)} custom-call(f32[1,32,32]{2,1,0:T(8,128)S(1)} %fusion.29), custom_call_target="Cholesky" | custom-call | tf_op jit(solution)/shard_map/jit(cholesky)/cholesky | solution.py:28
  254.6 0.6 compare_reduce_fusion
  255.2 0.7 fusion.24
  255.9 2.4 custom-call.11
  258.3 0.0 copy-done
  258.3 0.3 fusion.4
  258.7 0.2 convolution_bitcast_fusion.5
  258.8 0.0 copy-start.4
  258.9 0.7 copy-done.4
  259.5 18.3 %all-reduce = (f32[1,256,32]{1,2,0:T(8,128)S(1)}, f32[1,256]{1,0:T(1,128)S(1)}) all-reduce(f32[1,256,32]{1,2,0:T(8,128)S(1)} %convolution_bitcast_fusion.5, f32[1,256]{1,0:T(1,128)S(1)} %bitcast.98), channel_id=1, replica_groups=mesh['replica'=4,'tensor'=4,'section'=2] {'replica'}, use_global_device_ids=true, to_apply=%region_5.8 | all-reduce | flops 8448 | bytes 67584 | tf_op jit(solution)/shard_map/psum | solution.py:31
  277.9 0.0 copy-start.2
  277.9 1.1 fusion.1
  279.0 0.0 copy-start.5
  279.0 0.7 copy-done.5
  279.7 0.6 multiply_add_fusion
  280.3 0.0 copy-done.2
  280.3 0.9 fusion.2
  (4 shorter events, 0.1 us)
Async XLA Ops:
  7.2 1.4 copy-start.3
  7.2 113.8 %all-reduce.4.cloned.1.call-start = ((), (), s32[]{:S(2)}) async-start(), calls=%async_computation | async-start | bytes 262144 | tf_op jit(solution)/shard_map/psum | solution.py:26
  9.5 240.7 %all-reduce.6.cloned.1.call-start = ((), (), s32[]{:S(2)}) async-start(), calls=%async_computation.1 | async-start | bytes 262144 | tf_op jit(solution)/shard_map/psum | solution.py:26
  121.0 8.1 %copy-start.1 = (f32[1,1024,32]{1,2,0:T(8,128)S(1)}, f32[1,1024,32]{1,2,0:T(8,128)}, u32[]{:S(2)}) copy-start(f32[1,1024,32]{1,2,0:T(8,128)} %all-reduce.4.cloned.1.call-done) | copy-start | bytes 393220
  250.2 8.1 %copy-start = (f32[1,1024,32]{1,2,0:T(8,128)S(1)}, f32[1,1024,32]{1,2,0:T(8,128)}, u32[]{:S(2)}) copy-start(f32[1,1024,32]{1,2,0:T(8,128)} %all-reduce.6.cloned.1.call-done) | copy-start | bytes 393220
  258.8 0.7 copy-start.4
  277.9 2.4 copy-start.2
  279.0 0.7 copy-start.5
Sparse Core Ops, SparseCore 0:
  14.0 106.9 all-reduce.3
  148.7 101.5 all-reduce.5
where the time goes:
time: 288 us
  waiting for transfers between devices  213 us (74%)
  blocking collectives  36.4 us (13%)
  other arithmetic  15.3 us (5%)
  between operations  14.1 us (5%)
  matrix products  7.53 us (3%)
    psum x2, waiting for transfers between devices, body(): p_sum = lax.psum(p_part, ('replica', 'tensor')) / replicas  213 us
    psum x2, blocking collectives, body(): q_total = lax.psum(q_part, 'replica')  36.4 us
    another operation x6, other arithmetic, body(): factor = jnp.linalg.cholesky(gram_mat)  7.19 us
    another operation x4, other arithmetic, solve_one(): return jax.scipy.linalg.solve_triangular(lower, matrix.T, lower=True).T  6.17 us
  transfers between devices with their start and end apart: 2, of which 2 were waited for; matrix products, arithmetic and copies ran while one was open for 0% of the time, Pallas kernels for 0%

commit v1 on v0

v1 whole, which is shorter than its diff:
```python
import functools

import jax
import jax.numpy as jnp
from jax import lax
from jax.experimental import pallas as pl
from jax.experimental.pallas import tpu as pltpu
from jax.sharding import PartitionSpec as P

ROUNDS = 2
GATHER_MAX = 8
PAD = 16
STEP = 8
HIGHEST = lax.Precision.HIGHEST
F32, BF16 = jnp.float32, jnp.bfloat16
VMEM = pl.BlockSpec(memory_space=pltpu.VMEM)


def dot(a, b, ca, cb, precision=None):
    return lax.dot_general(a, b, (((ca,), (cb,)), ((), ())), precision=precision, preferred_element_type=F32)


def call(kernel, outs, *args, flops=0, scratch=()):
    size = sum(a.size * a.dtype.itemsize for a in (*args, *outs))
    return pl.pallas_call(
        kernel,
        out_shape=outs,
        in_specs=[VMEM] * len(args),
        out_specs=[VMEM] * len(outs),
        scratch_shapes=scratch,
        compiler_params=pltpu.CompilerParams(vmem_limit_bytes=32 * 1024 * 1024),
        cost_estimate=pl.CostEstimate(flops=flops, bytes_accessed=size, transcendentals=0),
    )(*args)


def three_parts(x):
    hi = x.astype(BF16).astype(F32)
    mid = (x - hi).astype(BF16).astype(F32)
    lo = (x - hi - mid).astype(BF16).astype(F32)
    return hi, mid, lo


def tree(values):
    values = list(values)
    while len(values) > 1:
        values = [a + b for a, b in zip(values[::2], values[1::2])] + values[len(values) & ~1 :]
    return values[0]


def inverse_factor(gram):
    n = gram.shape[0]
    wide = max(128, 2 * n)
    eye = (lax.broadcasted_iota(jnp.int32, (n, n), 0) == lax.broadcasted_iota(jnp.int32, (n, n), 1)).astype(F32)
    row = lax.broadcasted_iota(jnp.int32, (n, wide), 0)
    both = jnp.concatenate([gram, eye, jnp.zeros((n, wide - 2 * n), F32)], axis=1)
    scale = jnp.zeros((n, wide), F32)
    for first in range(0, n, STEP):
        columns = [jnp.broadcast_to(both[:, k : k + 1], (n, wide)) for k in range(first, first + STEP)]
        for j in range(STEP):
            k = first + j
            inverse = 1.0 / jnp.broadcast_to(columns[j][k : k + 1, :], (n, wide))
            scale = jnp.where(row == k, inverse, scale)
            factor = jnp.where(row > k, columns[j] * inverse, 0.0)
            for i in range(j + 1, STEP):
                columns[i] = columns[i] - factor * columns[i][k : k + 1, :]
            both = both - factor * both[k : k + 1, :]
    return both[:, n : 2 * n] * jnp.sqrt(scale[:, :n])


def merge_kernel(grads, errors, q, vec, merged, p_part):
    rows, cols = grads.shape
    total = (grads[...].astype(F32) + errors[...].astype(F32)).astype(BF16)
    merged[:rows, :] = total
    parts = three_parts(vec[...])
    merged[rows:, :] = jnp.concatenate([*parts, jnp.zeros((PAD - 3, cols), F32)], axis=0).astype(BF16)
    p_part[...] = dot(q[...].T.astype(BF16), total, 1, 1)


def add_kernel(*refs):
    refs[-1][...] = tree([r[...] for r in refs[:-1]])


def factor_kernel(n_p, replicas, last, *refs):
    p_parts, merged, out = refs[:n_p], refs[n_p:-1], refs[-1]
    rows, cols = merged[0].shape[0] - PAD, merged[0].shape[1]
    p_sum = tree([p[...] for p in p_parts]) * (1.0 / replicas)
    inverse = inverse_factor(dot(p_sum, p_sum, 1, 1, HIGHEST))
    p_lo = dot(inverse, p_sum, 1, 0, HIGHEST).astype(BF16)
    q_sum = tree([dot(p_lo, m[:rows, :], 1, 0) for m in merged])
    q_lo = (q_sum * (1.0 / replicas)).astype(BF16)
    if not last:
        out[...] = tree([dot(q_lo, m[:rows, :], 1, 1) for m in merged])
        return
    out[:, :rows] = p_lo
    out[:, rows : rows + cols] = q_lo
    vec = tree([jnp.sum(m[rows:, :].astype(F32), axis=0, keepdims=True) for m in merged]) * (1.0 / replicas)
    parts = three_parts(vec)
    out[:, rows + cols :] = jnp.concatenate([*parts, jnp.zeros((out.shape[0] - 3, cols), F32)], axis=0).astype(BF16)


def final_kernel(owners, *refs):
    place, own, *received = refs[: -9]
    merged, momentum, vec_momentum, new_errors, new_momentum, new_vec, pack, p_rows, unused = refs[-9:]
    del unused
    rows, cols = new_errors.shape
    own_rows = momentum.shape[0]
    is_owner = place[1] == 1

    @pl.when(is_owner)
    def _():
        pack[...] = own[...]

    @pl.when(jnp.logical_not(is_owner))
    def _():
        pack[...] = sum(r[...].astype(F32) for r in received).astype(BF16)

    p_rows[...] = pack[:, :rows].T
    q_lo = pack[:, rows : rows + cols]
    approx = dot(p_rows[...], q_lo, 1, 0)
    new_errors[...] = (merged[:rows, :].astype(F32) - approx).astype(BF16)
    first = pl.multiple_of(place[0] * own_rows, own_rows)
    mine = dot(p_rows[pl.ds(first, own_rows), :], q_lo, 1, 0)
    new_momentum[...] = 0.9 * momentum[...] + mine
    vec = jnp.sum(pack[:, rows + cols :].astype(F32), axis=0, keepdims=True)
    new_vec[...] = 0.9 * vec_momentum[...] + vec


def gathered(grads, errors, q_start, momentum, vec_grads, vec_momentum):
    replicas, tensors, sections = (lax.axis_size(a) for a in ("replica", "tensor", "section"))
    rows, cols = grads.shape[2:]
    rank = q_start.shape[2]
    middle = (replicas - 1) // 2
    owner = [middle + s % min(2, replicas) for s in range(sections)]
    sources = [sorted((z for z in range(replicas) if z != o), key=lambda z, o=o: -abs(z - o)) for o in owner]
    inward = [
        [(sources[s][j] * sections + s, owner[s] * sections + s) for s in range(sections)] for j in range(replicas - 1)
    ]
    outward = [[(b, a) for a, b in pairs] for pairs in inward]

    def along(x, perms):
        return [lax.ppermute(x, ("replica", "section"), p) for p in perms]

    def across(x):
        return [x] + [lax.ppermute(x, "tensor", [(i, i ^ k) for i in range(tensors)]) for k in range(1, tensors)]

    p_shape = jax.ShapeDtypeStruct((rank, rows), F32)
    work = 2 * rows * cols * rank
    merged, p_part = call(
        merge_kernel,
        [jax.ShapeDtypeStruct((rows + PAD, cols), BF16), p_shape],
        grads[0, 0],
        errors[0, 0],
        q_start[0],
        vec_grads[0],
        flops=work,
    )
    p_in = along(p_part, inward)
    m_in = along(merged, inward)
    p_part = call(add_kernel, [p_shape], p_part, *p_in)[0]
    for round_no in range(ROUNDS):
        last = round_no == ROUNDS - 1
        shape = jax.ShapeDtypeStruct((rank, rows + 2 * cols), BF16) if last else p_shape
        parts = across(p_part)
        p_part = call(
            functools.partial(factor_kernel, len(parts), replicas, last),
            [shape],
            *parts,
            merged,
            *m_in,
            flops=2 * replicas * work,
        )[0]
    received = along(p_part, outward)
    z, s = lax.axis_index("replica"), lax.axis_index("section")
    place = jnp.stack([z, (z == jnp.asarray(owner)[s]).astype(jnp.int32)])
    outs = [
        jax.ShapeDtypeStruct((rows, cols), BF16),
        jax.ShapeDtypeStruct(momentum.shape[1:], F32),
        jax.ShapeDtypeStruct((1, cols), F32),
    ]
    args = [place, p_part, *received, merged, momentum[0], vec_momentum]
    errors_out, momentum_out, vec_out = pl.pallas_call(
        functools.partial(final_kernel, owner),
        out_shape=outs,
        in_specs=[pl.BlockSpec(memory_space=pltpu.SMEM)] + [VMEM] * (len(args) - 1),
        out_specs=[VMEM] * 3,
        scratch_shapes=[
            pltpu.VMEM(p_part.shape, BF16),
            pltpu.VMEM((rows, rank), BF16),
            pltpu.VMEM((8, 128), F32),
        ],
        compiler_params=pltpu.CompilerParams(vmem_limit_bytes=32 * 1024 * 1024),
    )(*args)
    return errors_out[None, None], momentum_out[None], vec_out


def reduced(grads, errors, q_start, momentum, vec_grads, vec_momentum):
    replicas = lax.axis_size("replica")
    merged = (grads[0].astype(F32) + errors[0].astype(F32)).astype(BF16)
    q_lo = q_start.astype(BF16)
    vec_sum = lax.psum(vec_grads[0], "replica")
    p_lo = None
    for _ in range(ROUNDS):
        p_part = jnp.einsum("bdc,bcr->brd", merged, q_lo, preferred_element_type=F32)
        p_sum = lax.psum(p_part, ("replica", "tensor")) / replicas
        gram = jnp.einsum("brd,bsd->brs", p_sum, p_sum, precision=HIGHEST)
        inverse = jnp.stack([inverse_factor(g) for g in gram])
        p_lo = jnp.einsum("brs,bsd->brd", inverse, p_sum, precision=HIGHEST).astype(BF16)
        q_part = jnp.einsum("bdc,brd->bcr", merged, p_lo, preferred_element_type=F32)
        q_lo = (lax.psum(q_part, "replica") / replicas).astype(BF16)
    approx = jnp.einsum("brd,bcr->bdc", p_lo, q_lo, preferred_element_type=F32)
    new_errors = (merged.astype(F32) - approx).astype(BF16)[None]
    own_rows = momentum.shape[1]
    mine = lax.dynamic_slice_in_dim(approx, lax.axis_index("replica") * own_rows, own_rows, 1)
    return new_errors, 0.9 * momentum + mine, 0.9 * vec_momentum + vec_sum / replicas


def solution(mesh):
    few = mesh.shape["replica"] <= GATHER_MAX
    wide = P("replica", "section", None, "tensor")
    outs = (wide, P("section", "replica", "tensor"), P("section", "tensor"))
    return jax.shard_map(
        gathered if few else reduced,
        mesh=mesh,
        in_specs=(wide, wide, P("section", "tensor", None), outs[1], P("replica", "section", "tensor"), outs[2]),
        out_specs=outs,
        check_vma=False,
    )
```

time: 288 us -> 65.8 us (0.23)
  waiting for transfers between devices: 213 us -> 29.7 us
  blocking collectives: 36.4 us -> 0 us
  starting transfers between devices: 0.08 us -> 22.4 us
  other arithmetic: 15.3 us -> 0.08 us
  between operations: 14.1 us -> 1.42 us
  matrix products: 7.53 us -> 0 us
  Pallas kernels: 0 us -> 6.84 us
  local copies, waits for them, and re-layouts: 1.52 us -> 4.86 us
    psum x2 -> x0, waiting for transfers between devices: 213 us -> none  [body(): p_sum = lax.psum(p_part, ('replica', 'tensor')) / replicas]
    psum x2 -> x0, blocking collectives: 36.4 us -> none  [body(): q_total = lax.psum(q_part, 'replica')]
    ppermute x0 -> x15, waiting for transfers between devices: none -> 29.7 us  [the longest x9 21.8 us: along(): return [lax.ppermute(x, ('replica', 'section'), p) for p in perms]]
    ppermute x0 -> x15, starting transfers between devices: none -> 22.4 us  [the longest x9 13.4 us: along(): return [lax.ppermute(x, ('replica', 'section'), p) for p in perms]]
    another operation x10 -> x1, other arithmetic: 13.4 us -> 0.08 us  [gathered(): place = jnp.stack([z, (z == jnp.asarray(owner)[s]).astype(jnp.int32)])]
    dot_general x8 -> x0, matrix products: 6.85 us -> none  [the longest x2 2.59 us: body(): jnp.einsum('bdr,bds->brs', p_sum, p_sum, precision=lax.Precision.HIGHEST)]
    pallas_call x0 -> x5, Pallas kernels: none -> 6.84 us  [the longest x4 4.99 us: call(): pl.pallas_call(kernel, out_shape=outs, in_specs=[VMEM] * len(args), out_s...]
    unnamed x12 -> x13, local copies, waits for them, and re-layouts: 1.38 us -> 4.28 us
  transfers between devices with their start and end apart: 2 -> 15, of which waited for: 2 -> 6; matrix products, arithmetic and copies ran while one was open for 0% -> 1% of each run, Pallas kernels for 0% -> 0%
where the time goes in v1:
time: 65.8 us; the launch traced here: 65.4 us
  waiting for transfers between devices  29.7 us (45%)
  starting transfers between devices  22.4 us (34%)
  Pallas kernels  6.84 us (10%)
  local copies, waits for them, and re-layouts  4.86 us (7%)
  between operations  1.42 us (2%)
    ppermute x9, waiting for transfers between devices, along(): return [lax.ppermute(x, ('replica', 'section'), p) for p in perms]  21.8 us
    ppermute x9, starting transfers between devices, along(): return [lax.ppermute(x, ('replica', 'section'), p) for p in perms]  13.4 us
    ppermute x6, starting transfers between devices, across(): lax.ppermute(x, 'tensor', [(i, i ^ k) for i in range(tensors)])  9.04 us
    ppermute x6, waiting for transfers between devices, across(): lax.ppermute(x, 'tensor', [(i, i ^ k) for i in range(tensors)])  7.9 us
    pallas_call x4, Pallas kernels, call(): pl.pallas_call(kernel, out_shape=outs, in_specs=[VMEM] * len(args), out_s...  4.99 us
    unnamed x13, local copies, waits for them, and re-layouts  4.28 us
    pallas_call x1, Pallas kernels, gathered(): pl.pallas_call(functools.partial(final_kernel, owner), out_shape=outs, in...  1.85 us
  transfers between devices with their start and end apart: 15, of which 6 were waited for; matrix products, arithmetic and copies ran while one was open for 1% of the time, Pallas kernels for 0%

profile of v1, /device:TPU:0, one launch (start us, length us, event | category | flops | bytes accessed | tf_op | source)
XLA Modules:
  0.0 65.4 jit_solution(3400094962252089227)
XLA Ops:
  0.6 0.9 %copy.10 = f32[1,256,32]{2,1,0:T(8,128)S(1)} copy(f32[1,256,32]{1,2,0:T(8,128)} %param.9) | data formatting | bytes 65536 | tf_op args[2]
  1.5 0.0 copy-start.4
  1.5 0.7 %copy-done.4 = f32[1,1,256]{2,1,0:T(1,128)S(1)} copy-done((f32[1,1,256]{2,1,0:T(1,128)S(1)}, f32[1,1,256]{2,1,0:T(1,128)}, u32[]{:S(2)}) %copy-start.4) | copy-done | bytes 1048
  2.2 0.0 copy-start
  2.2 1.0 %copy-done = bf16[1,1,1024,256]{3,2,1,0:T(8,128)(2,1)S(1)} copy-done((bf16[1,1,1024,256]{3,2,1,0:T(8,128)(2,1)S(1)}, bf16[1,1,1024,256]{3,2,1,0:T(8,128)(2,1)}, u32[]{:S(2)}) %copy-start) | copy-done | bytes 524312
  3.2 0.0 copy-start.1
  3.2 1.0 %copy-done.1 = bf16[1,1,1024,256]{3,2,1,0:T(8,128)(2,1)S(1)} copy-done((bf16[1,1,1024,256]{3,2,1,0:T(8,128)(2,1)S(1)}, bf16[1,1,1024,256]{3,2,1,0:T(8,128)(2,1)}, u32[]{:S(2)}) %copy-start.1) | copy-done | bytes 524312
  4.3 0.3 shard_map.94
  4.5 0.7 %collective-permute-start.6 = (bf16[1040,256]{1,0:T(8,128)(2,1)S(1)}, bf16[1040,256]{1,0:T(8,128)(2,1)S(1)}, u32[]{:S(2)}, u32[]{:S(2)}) collective-permute-start(bf16[1040,256]{1,0:T(8,128)(2,1)S(1)} %get-tuple-element.9.refs_4_.refs_5_), channel_id=1, source_target_pairs={{24,8},{1,17},{26,10},{3,19},{28,12},{5,21},{30,14},{7,23}} | collective-permute-start | bytes 1597448 | tf_op jit(solution)/shard_map/ppermute | solution.py:141
  5.2 5.6 %collective-permute-start.7 = (bf16[1040,256]{1,0:T(8,128)(2,1)S(1)}, bf16[1040,256]{1,0:T(8,128)(2,1)S(1)}, u32[]{:S(2)}, u32[]{:S(2)}) collective-permute-start(bf16[1040,256]{1,0:T(8,128)(2,1)S(1)} %get-tuple-element.9.refs_4_.refs_5_), channel_id=1, source_target_pairs={{0,8},{9,17},{2,10},{11,19},{4,12},{13,21},{6,14},{15,23}} | collective-permute-start | bytes 1597448 | tf_op jit(solution)/shard_map/ppermute | solution.py:141
  10.8 0.7 %collective-permute-start.8 = (bf16[1040,256]{1,0:T(8,128)(2,1)S(1)}, bf16[1040,256]{1,0:T(8,128)(2,1)S(1)}, u32[]{:S(2)}, u32[]{:S(2)}) collective-permute-start(bf16[1040,256]{1,0:T(8,128)(2,1)S(1)} %get-tuple-element.9.refs_4_.refs_5_), channel_id=1, source_target_pairs={{16,8},{25,17},{18,10},{27,19},{20,12},{29,21},{22,14},{31,23}} | collective-permute-start | bytes 1597448 | tf_op jit(solution)/shard_map/ppermute | solution.py:141
  11.5 0.7 %collective-permute-start = (f32[32,1024]{1,0:T(8,128)S(1)}, f32[32,1024]{1,0:T(8,128)S(1)}, u32[]{:S(2)}, u32[]{:S(2)}) collective-permute-start(f32[32,1024]{1,0:T(8,128)S(1)} %get-tuple-element.8.refs_0_), channel_id=1, source_target_pairs={{24,8},{1,17},{26,10},{3,19},{28,12},{5,21},{30,14},{7,23}} | collective-permute-start | bytes 393224 | tf_op jit(solution)/shard_map/ppermute | solution.py:141
  12.2 2.5 %collective-permute-start.1 = (f32[32,1024]{1,0:T(8,128)S(1)}, f32[32,1024]{1,0:T(8,128)S(1)}, u32[]{:S(2)}, u32[]{:S(2)}) collective-permute-start(f32[32,1024]{1,0:T(8,128)S(1)} %get-tuple-element.8.refs_0_), channel_id=1, source_target_pairs={{0,8},{9,17},{2,10},{11,19},{4,12},{13,21},{6,14},{15,23}} | collective-permute-start | bytes 393224 | tf_op jit(solution)/shard_map/ppermute | solution.py:141
  14.7 0.0 collective-permute-done.refs_1_
  14.7 0.7 %collective-permute-start.2 = (f32[32,1024]{1,0:T(8,128)S(1)}, f32[32,1024]{1,0:T(8,128)S(1)}, u32[]{:S(2)}, u32[]{:S(2)}) collective-permute-start(f32[32,1024]{1,0:T(8,128)S(1)} %get-tuple-element.8.refs_0_), channel_id=1, source_target_pairs={{16,8},{25,17},{18,10},{27,19},{20,12},{29,21},{22,14},{31,23}} | collective-permute-start | bytes 393224 | tf_op jit(solution)/shard_map/ppermute | solution.py:141
  15.4 9.3 %collective-permute-done.1.refs_2_ = f32[32,1024]{1,0:T(8,128)S(1)} collective-permute-done((f32[32,1024]{1,0:T(8,128)S(1)}, f32[32,1024]{1,0:T(8,128)S(1)}, u32[]{:S(2)}, u32[]{:S(2)}) %collective-permute-start.1) | collective-permute-done | bytes 131104 | tf_op jit(solution)/shard_map/ppermute | solution.py:141
  24.6 0.0 collective-permute-done.2.refs_3_
  24.7 1.6 %collective-permute-start.3 = (f32[32,1024]{1,0:T(8,128)S(1)}, f32[32,1024]{1,0:T(8,128)S(1)}, u32[]{:S(2)}, u32[]{:S(2)}) collective-permute-start(f32[32,1024]{1,0:T(8,128)S(1)} %shard_map.95.refs_0_), channel_id=1, source_target_pairs={{0,2},{2,0},{4,6},{6,4},{1,3},{3,1},{5,7},{7,5},{8,10},{10,8},{12,... | collective-permute-start | bytes 393224 | tf_op jit(solution)/shard_map/ppermute | solution.py:144
  26.2 1.5 %collective-permute-start.4 = (f32[32,1024]{1,0:T(8,128)S(1)}, f32[32,1024]{1,0:T(8,128)S(1)}, u32[]{:S(2)}, u32[]{:S(2)}) collective-permute-start(f32[32,1024]{1,0:T(8,128)S(1)} %shard_map.95.refs_0_), channel_id=1, source_target_pairs={{0,4},{2,6},{4,0},{6,2},{1,5},{3,7},{5,1},{7,3},{8,12},{10,14},{12... | collective-permute-start | bytes 393224 | tf_op jit(solution)/shard_map/ppermute | solution.py:144
  27.7 2.0 %collective-permute-done.3.refs_1_ = f32[32,1024]{1,0:T(8,128)S(1)} collective-permute-done((f32[32,1024]{1,0:T(8,128)S(1)}, f32[32,1024]{1,0:T(8,128)S(1)}, u32[]{:S(2)}, u32[]{:S(2)}) %collective-permute-start.3) | collective-permute-done | bytes 131104 | tf_op jit(solution)/shard_map/ppermute | solution.py:144
  29.7 2.4 %collective-permute-start.5 = (f32[32,1024]{1,0:T(8,128)S(1)}, f32[32,1024]{1,0:T(8,128)S(1)}, u32[]{:S(2)}, u32[]{:S(2)}) collective-permute-start(f32[32,1024]{1,0:T(8,128)S(1)} %shard_map.95.refs_0_), channel_id=1, source_target_pairs={{0,6},{2,4},{4,2},{6,0},{1,7},{3,5},{5,3},{7,1},{8,14},{10,12},{12... | collective-permute-start | bytes 393224 | tf_op jit(solution)/shard_map/ppermute | solution.py:144
  32.1 0.0 collective-permute-done.4.refs_2_
  32.1 3.4 %collective-permute-done.5.refs_3_ = f32[32,1024]{1,0:T(8,128)S(1)} collective-permute-done((f32[32,1024]{1,0:T(8,128)S(1)}, f32[32,1024]{1,0:T(8,128)S(1)}, u32[]{:S(2)}, u32[]{:S(2)}) %collective-permute-start.5) | collective-permute-done | bytes 131104 | tf_op jit(solution)/shard_map/ppermute | solution.py:144
  35.6 0.0 collective-permute-done.6.refs_5_
  35.6 0.0 collective-permute-done.7.refs_6_
  35.6 0.0 collective-permute-done.8.refs_7_
  35.6 2.9 %shard_map.96.refs_0_ = f32[32,1024]{1,0:T(8,128)S(1)} custom-call(f32[32,1024]{1,0:T(8,128)S(1)} %shard_map.95.refs_0_, f32[32,1024]{1,0:T(8,128)S(1)} %collective-permute-done.3.refs_1_, f32[32,1024]{1,0:T(8,128)S(1)} %collective-permute-done.4.refs_2_, f32[32,1024]{1,0:T(8,128)S(1)} %collective-permute-done.5.refs_3_, ...), custom_call_target="tpu_custom_call" | custom-call | flops 134217728 | bytes 2785280 | tf_op jit(solution)/shard_map/pallas_call | solution.py:25
  38.5 1.6 %collective-permute-start.10 = (f32[32,1024]{1,0:T(8,128)S(1)}, f32[32,1024]{1,0:T(8,128)S(1)}, u32[]{:S(2)}, u32[]{:S(2)}) collective-permute-start(f32[32,1024]{1,0:T(8,128)S(1)} %shard_map.96.refs_0_), channel_id=1, source_target_pairs={{0,4},{2,6},{4,0},{6,2},{1,5},{3,7},{5,1},{7,3},{8,12},{10,14},{12... | collective-permute-start | bytes 393224 | tf_op jit(solution)/shard_map/ppermute | solution.py:144
  40.0 1.4 %collective-permute-start.11 = (f32[32,1024]{1,0:T(8,128)S(1)}, f32[32,1024]{1,0:T(8,128)S(1)}, u32[]{:S(2)}, u32[]{:S(2)}) collective-permute-start(f32[32,1024]{1,0:T(8,128)S(1)} %shard_map.96.refs_0_), channel_id=1, source_target_pairs={{0,6},{2,4},{4,2},{6,0},{1,7},{3,5},{5,3},{7,1},{8,14},{10,12},{12... | collective-permute-start | bytes 393224 | tf_op jit(solution)/shard_map/ppermute | solution.py:144
  41.5 0.5 collective-permute-start.9
  42.0 0.0 copy-start.5
  42.0 0.7 copy-done.5
  42.7 0.6 dynamic_slice.3
  43.9 0.0 copy-start.2
  43.9 0.0 collective-permute-done.10.refs_2_
  43.9 2.0 %collective-permute-done.11.refs_3_ = f32[32,1024]{1,0:T(8,128)S(1)} collective-permute-done((f32[32,1024]{1,0:T(8,128)S(1)}, f32[32,1024]{1,0:T(8,128)S(1)}, u32[]{:S(2)}, u32[]{:S(2)}) %collective-permute-start.11) | collective-permute-done | bytes 131104 | tf_op jit(solution)/shard_map/ppermute | solution.py:144
  45.9 0.5 collective-permute-done.9.refs_1_
  46.4 1.8 %shard_map.97.refs_1_ = bf16[32,1536]{1,0:T(8,128)(2,1)S(1)} custom-call(f32[32,1024]{1,0:T(8,128)S(1)} %shard_map.96.refs_0_, f32[32,1024]{1,0:T(8,128)S(1)} %collective-permute-done.9.refs_1_, f32[32,1024]{1,0:T(8,128)S(1)} %collective-permute-done.10.refs_2_, f32[32,1024]{1,0:T(8,128)S(1)} %collective-permute-done.11.refs_3_, ...), custom_call_target="tpu_custom_call" | custom-call | flops 134217728 | bytes 2752512 | tf_op jit(solution)/shard_map/pallas_call | solution.py:25
  48.2 0.7 %collective-permute-start.12 = (bf16[32,1536]{1,0:T(8,128)(2,1)S(1)}, bf16[32,1536]{1,0:T(8,128)(2,1)S(1)}, u32[]{:S(2)}, u32[]{:S(2)}) collective-permute-start(bf16[32,1536]{1,0:T(8,128)(2,1)S(1)} %shard_map.97.refs_1_), channel_id=1, source_target_pairs={{8,24},{17,1},{10,26},{19,3},{12,28},{21,5},{14,30},{23,7}} | collective-permute-start | bytes 294920 | tf_op jit(solution)/shard_map/ppermute | solution.py:141
  48.9 1.3 %collective-permute-start.13 = (bf16[32,1536]{1,0:T(8,128)(2,1)S(1)}, bf16[32,1536]{1,0:T(8,128)(2,1)S(1)}, u32[]{:S(2)}, u32[]{:S(2)}) collective-permute-start(bf16[32,1536]{1,0:T(8,128)(2,1)S(1)} %shard_map.97.refs_1_), channel_id=1, source_target_pairs={{8,0},{17,9},{10,2},{19,11},{12,4},{21,13},{14,6},{23,15}} | collective-permute-start | bytes 294920 | tf_op jit(solution)/shard_map/ppermute | solution.py:141
  50.2 0.7 %collective-permute-start.14 = (bf16[32,1536]{1,0:T(8,128)(2,1)S(1)}, bf16[32,1536]{1,0:T(8,128)(2,1)S(1)}, u32[]{:S(2)}, u32[]{:S(2)}) collective-permute-start(bf16[32,1536]{1,0:T(8,128)(2,1)S(1)} %shard_map.97.refs_1_), channel_id=1, source_target_pairs={{8,16},{17,25},{10,18},{19,27},{12,20},{21,29},{14,22},{23,31}} | collective-permute-start | bytes 294920 | tf_op jit(solution)/shard_map/ppermute | solution.py:141
  50.9 0.1 pad_add_fusion.refs_0_
  51.0 0.0 collective-permute-done.12.refs_2_
  51.0 12.5 %collective-permute-done.13.refs_3_ = bf16[32,1536]{1,0:T(8,128)(2,1)S(1)} collective-permute-done((bf16[32,1536]{1,0:T(8,128)(2,1)S(1)}, bf16[32,1536]{1,0:T(8,128)(2,1)S(1)}, u32[]{:S(2)}, u32[]{:S(2)}) %collective-permute-start.13) | collective-permute-done | bytes 98336 | tf_op jit(solution)/shard_map/ppermute | solution.py:141
  63.5 0.0 collective-permute-done.14.refs_4_
  63.5 0.0 copy-done.2
  63.5 0.0 copy-done.3
  63.5 1.8 %shard_map.98 = (bf16[1024,256]{1,0:T(8,128)(2,1)}, f32[256,256]{1,0:T(8,128)}, f32[1,256]{1,0:T(1,128)}) custom-call(s32[2]{0:T(128)S(1)} %pad_add_fusion.refs_0_, bf16[32,1536]{1,0:T(8,128)(2,1)S(1)} %shard_map.97.refs_1_, bf16[32,1536]{1,0:T(8,128)(2,1)S(1)} %collective-permute-done.12.refs_2_, bf16[32,1536]{1,0:T(8,128)(2,1)S(1)} %collective-permute-done.13.refs_3_, ...), custom_call_target="tpu_custom_call" | custom-call | tf_op jit(solution)/shard_map/pallas_call | solution.py:181
  (2 shorter events, 0.0 us)
Async XLA Ops:
  1.5 0.7 %copy-start.4 = (f32[1,1,256]{2,1,0:T(1,128)S(1)}, f32[1,1,256]{2,1,0:T(1,128)}, u32[]{:S(2)}) copy-start(f32[1,1,256]{2,1,0:T(1,128)} %param.11) | copy-start | bytes 3076
  2.2 1.0 %copy-start = (bf16[1,1,1024,256]{3,2,1,0:T(8,128)(2,1)S(1)}, bf16[1,1,1024,256]{3,2,1,0:T(8,128)(2,1)}, u32[]{:S(2)}) copy-start(bf16[1,1,1024,256]{3,2,1,0:T(8,128)(2,1)} %param.7) | copy-start | bytes 1572868
  3.2 1.0 %copy-start.1 = (bf16[1,1,1024,256]{3,2,1,0:T(8,128)(2,1)S(1)}, bf16[1,1,1024,256]{3,2,1,0:T(8,128)(2,1)}, u32[]{:S(2)}) copy-start(bf16[1,1,1024,256]{3,2,1,0:T(8,128)(2,1)} %param.8) | copy-start | bytes 1572868
  4.5 31.0 %collective-permute-start.6 = (bf16[1040,256]{1,0:T(8,128)(2,1)S(1)}, bf16[1040,256]{1,0:T(8,128)(2,1)S(1)}, u32[]{:S(2)}, u32[]{:S(2)}) collective-permute-start(bf16[1040,256]{1,0:T(8,128)(2,1)S(1)} %get-tuple-element.9.refs_4_.refs_5_), channel_id=1, source_target_pairs={{24,8},{1,17},{26,10},{3,19},{28,12},{5,21},{30,14},{7,23}} | collective-permute-start | bytes 1597448 | tf_op jit(solution)/shard_map/ppermute | solution.py:141
  5.2 30.3 %collective-permute-start.7 = (bf16[1040,256]{1,0:T(8,128)(2,1)S(1)}, bf16[1040,256]{1,0:T(8,128)(2,1)S(1)}, u32[]{:S(2)}, u32[]{:S(2)}) collective-permute-start(bf16[1040,256]{1,0:T(8,128)(2,1)S(1)} %get-tuple-element.9.refs_4_.refs_5_), channel_id=1, source_target_pairs={{0,8},{9,17},{2,10},{11,19},{4,12},{13,21},{6,14},{15,23}} | collective-permute-start | bytes 1597448 | tf_op jit(solution)/shard_map/ppermute | solution.py:141
  10.8 24.8 %collective-permute-start.8 = (bf16[1040,256]{1,0:T(8,128)(2,1)S(1)}, bf16[1040,256]{1,0:T(8,128)(2,1)S(1)}, u32[]{:S(2)}, u32[]{:S(2)}) collective-permute-start(bf16[1040,256]{1,0:T(8,128)(2,1)S(1)} %get-tuple-element.9.refs_4_.refs_5_), channel_id=1, source_target_pairs={{16,8},{25,17},{18,10},{27,19},{20,12},{29,21},{22,14},{31,23}} | collective-permute-start | bytes 1597448 | tf_op jit(solution)/shard_map/ppermute | solution.py:141
  11.5 3.2 %collective-permute-start = (f32[32,1024]{1,0:T(8,128)S(1)}, f32[32,1024]{1,0:T(8,128)S(1)}, u32[]{:S(2)}, u32[]{:S(2)}) collective-permute-start(f32[32,1024]{1,0:T(8,128)S(1)} %get-tuple-element.8.refs_0_), channel_id=1, source_target_pairs={{24,8},{1,17},{26,10},{3,19},{28,12},{5,21},{30,14},{7,23}} | collective-permute-start | bytes 393224 | tf_op jit(solution)/shard_map/ppermute | solution.py:141
  12.2 12.4 %collective-permute-start.1 = (f32[32,1024]{1,0:T(8,128)S(1)}, f32[32,1024]{1,0:T(8,128)S(1)}, u32[]{:S(2)}, u32[]{:S(2)}) collective-permute-start(f32[32,1024]{1,0:T(8,128)S(1)} %get-tuple-element.8.refs_0_), channel_id=1, source_target_pairs={{0,8},{9,17},{2,10},{11,19},{4,12},{13,21},{6,14},{15,23}} | collective-permute-start | bytes 393224 | tf_op jit(solution)/shard_map/ppermute | solution.py:141
  14.7 9.9 %collective-permute-start.2 = (f32[32,1024]{1,0:T(8,128)S(1)}, f32[32,1024]{1,0:T(8,128)S(1)}, u32[]{:S(2)}, u32[]{:S(2)}) collective-permute-start(f32[32,1024]{1,0:T(8,128)S(1)} %get-tuple-element.8.refs_0_), channel_id=1, source_target_pairs={{16,8},{25,17},{18,10},{27,19},{20,12},{29,21},{22,14},{31,23}} | collective-permute-start | bytes 393224 | tf_op jit(solution)/shard_map/ppermute | solution.py:141
  24.7 5.0 %collective-permute-start.3 = (f32[32,1024]{1,0:T(8,128)S(1)}, f32[32,1024]{1,0:T(8,128)S(1)}, u32[]{:S(2)}, u32[]{:S(2)}) collective-permute-start(f32[32,1024]{1,0:T(8,128)S(1)} %shard_map.95.refs_0_), channel_id=1, source_target_pairs={{0,2},{2,0},{4,6},{6,4},{1,3},{3,1},{5,7},{7,5},{8,10},{10,8},{12,... | collective-permute-start | bytes 393224 | tf_op jit(solution)/shard_map/ppermute | solution.py:144
  26.2 5.9 %collective-permute-start.4 = (f32[32,1024]{1,0:T(8,128)S(1)}, f32[32,1024]{1,0:T(8,128)S(1)}, u32[]{:S(2)}, u32[]{:S(2)}) collective-permute-start(f32[32,1024]{1,0:T(8,128)S(1)} %shard_map.95.refs_0_), channel_id=1, source_target_pairs={{0,4},{2,6},{4,0},{6,2},{1,5},{3,7},{5,1},{7,3},{8,12},{10,14},{12... | collective-permute-start | bytes 393224 | tf_op jit(solution)/shard_map/ppermute | solution.py:144
  29.7 5.9 %collective-permute-start.5 = (f32[32,1024]{1,0:T(8,128)S(1)}, f32[32,1024]{1,0:T(8,128)S(1)}, u32[]{:S(2)}, u32[]{:S(2)}) collective-permute-start(f32[32,1024]{1,0:T(8,128)S(1)} %shard_map.95.refs_0_), channel_id=1, source_target_pairs={{0,6},{2,4},{4,2},{6,0},{1,7},{3,5},{5,3},{7,1},{8,14},{10,12},{12... | collective-permute-start | bytes 393224 | tf_op jit(solution)/shard_map/ppermute | solution.py:144
  38.5 5.4 %collective-permute-start.10 = (f32[32,1024]{1,0:T(8,128)S(1)}, f32[32,1024]{1,0:T(8,128)S(1)}, u32[]{:S(2)}, u32[]{:S(2)}) collective-permute-start(f32[32,1024]{1,0:T(8,128)S(1)} %shard_map.96.refs_0_), channel_id=1, source_target_pairs={{0,4},{2,6},{4,0},{6,2},{1,5},{3,7},{5,1},{7,3},{8,12},{10,14},{12... | collective-permute-start | bytes 393224 | tf_op jit(solution)/shard_map/ppermute | solution.py:144
  40.0 5.9 %collective-permute-start.11 = (f32[32,1024]{1,0:T(8,128)S(1)}, f32[32,1024]{1,0:T(8,128)S(1)}, u32[]{:S(2)}, u32[]{:S(2)}) collective-permute-start(f32[32,1024]{1,0:T(8,128)S(1)} %shard_map.96.refs_0_), channel_id=1, source_target_pairs={{0,6},{2,4},{4,2},{6,0},{1,7},{3,5},{5,3},{7,1},{8,14},{10,12},{12... | collective-permute-start | bytes 393224 | tf_op jit(solution)/shard_map/ppermute | solution.py:144
  41.5 5.0 %collective-permute-start.9 = (f32[32,1024]{1,0:T(8,128)S(1)}, f32[32,1024]{1,0:T(8,128)S(1)}, u32[]{:S(2)}, u32[]{:S(2)}) collective-permute-start(f32[32,1024]{1,0:T(8,128)S(1)} %shard_map.96.refs_0_), channel_id=1, source_target_pairs={{0,2},{2,0},{4,6},{6,4},{1,3},{3,1},{5,7},{7,5},{8,10},{10,8},{12,... | collective-permute-start | bytes 393224 | tf_op jit(solution)/shard_map/ppermute | solution.py:144
  42.0 0.7 %copy-start.5 = (s32[2]{0:T(128)S(1)}, s32[2]{0:T(128)}, u32[]{:S(2)}) copy-start(s32[2]{0:T(128)} %constant.15.clone) | copy-start | bytes 28
  43.9 19.6 %copy-start.2 = (f32[1,256,256]{2,1,0:T(8,128)S(1)}, f32[1,256,256]{2,1,0:T(8,128)}, u32[]{:S(2)}) copy-start(f32[1,256,256]{2,1,0:T(8,128)} %param.10) | copy-start | bytes 786436
  48.2 2.7 %collective-permute-start.12 = (bf16[32,1536]{1,0:T(8,128)(2,1)S(1)}, bf16[32,1536]{1,0:T(8,128)(2,1)S(1)}, u32[]{:S(2)}, u32[]{:S(2)}) collective-permute-start(bf16[32,1536]{1,0:T(8,128)(2,1)S(1)} %shard_map.97.refs_1_), channel_id=1, source_target_pairs={{8,24},{17,1},{10,26},{19,3},{12,28},{21,5},{14,30},{23,7}} | collective-permute-start | bytes 294920 | tf_op jit(solution)/shard_map/ppermute | solution.py:141
  48.9 14.6 %collective-permute-start.13 = (bf16[32,1536]{1,0:T(8,128)(2,1)S(1)}, bf16[32,1536]{1,0:T(8,128)(2,1)S(1)}, u32[]{:S(2)}, u32[]{:S(2)}) collective-permute-start(bf16[32,1536]{1,0:T(8,128)(2,1)S(1)} %shard_map.97.refs_1_), channel_id=1, source_target_pairs={{8,0},{17,9},{10,2},{19,11},{12,4},{21,13},{14,6},{23,15}} | collective-permute-start | bytes 294920 | tf_op jit(solution)/shard_map/ppermute | solution.py:141
  50.2 13.3 %collective-permute-start.14 = (bf16[32,1536]{1,0:T(8,128)(2,1)S(1)}, bf16[32,1536]{1,0:T(8,128)(2,1)S(1)}, u32[]{:S(2)}, u32[]{:S(2)}) collective-permute-start(bf16[32,1536]{1,0:T(8,128)(2,1)S(1)} %shard_map.97.refs_1_), channel_id=1, source_target_pairs={{8,16},{17,25},{10,18},{19,27},{12,20},{21,29},{14,22},{23,31}} | collective-permute-start | bytes 294920 | tf_op jit(solution)/shard_map/ppermute | solution.py:141
  50.9 12.6 %copy-start.3 = (f32[1,256]{1,0:T(1,128)S(1)}, f32[1,256]{1,0:T(1,128)}, u32[]{:S(2)}) copy-start(f32[1,256]{1,0:T(1,128)} %refs_7_.1) | copy-start | bytes 3076

commit v2 on v1

--- a/solution.py
+++ b/solution.py
@@ -10,26 +10,28 @@
 ROUNDS = 2
 GATHER_MAX = 8
 PAD = 16
+CHUNKS = 4
 STEP = 8
 HIGHEST = lax.Precision.HIGHEST
 F32, BF16 = jnp.float32, jnp.bfloat16
 VMEM = pl.BlockSpec(memory_space=pltpu.VMEM)
+HBM = pl.BlockSpec(memory_space=pltpu.MemorySpace.HBM)
 
 
 def dot(a, b, ca, cb, precision=None):
     return lax.dot_general(a, b, (((ca,), (cb,)), ((), ())), precision=precision, preferred_element_type=F32)
 
 
-def call(kernel, outs, *args, flops=0, scratch=()):
+def call(kernel, outs, *args, flops=0, in_specs=None, out_specs=None, scratch=(), limit=32, cost=None):
     size = sum(a.size * a.dtype.itemsize for a in (*args, *outs))
     return pl.pallas_call(
         kernel,
         out_shape=outs,
-        in_specs=[VMEM] * len(args),
-        out_specs=[VMEM] * len(outs),
+        in_specs=in_specs or [VMEM] * len(args),
+        out_specs=out_specs or [VMEM] * len(outs),
         scratch_shapes=scratch,
-        compiler_params=pltpu.CompilerParams(vmem_limit_bytes=32 * 1024 * 1024),
-        cost_estimate=pl.CostEstimate(flops=flops, bytes_accessed=size, transcendentals=0),
+        compiler_params=pltpu.CompilerParams(vmem_limit_bytes=limit * 1024 * 1024),
+        cost_estimate=pl.CostEstimate(flops=flops, bytes_accessed=cost or size, transcendentals=0),
     )(*args)
 
 
@@ -67,13 +69,31 @@
     return both[:, n : 2 * n] * jnp.sqrt(scale[:, :n])
 
 
-def merge_kernel(grads, errors, q, vec, merged, p_part):
+def merge_kernel(grads, errors, q, vec, merged, p_part, grads_in, errors_in, q_in, vec_in, sems):
     rows, cols = grads.shape
-    total = (grads[...].astype(F32) + errors[...].astype(F32)).astype(BF16)
-    merged[:rows, :] = total
-    parts = three_parts(vec[...])
+    step = rows // CHUNKS
+    small = [pltpu.make_async_copy(a, b, sems.at[2, i]) for i, (a, b) in enumerate([(q, q_in), (vec, vec_in)])]
+    large = [
+        [
+            pltpu.make_async_copy(a.at[pl.ds(i * step, step)], b.at[pl.ds(i * step, step)], sems.at[j, i])
+            for j, (a, b) in enumerate([(grads, grads_in), (errors, errors_in)])
+        ]
+        for i in range(CHUNKS)
+    ]
+    for copy in small + sum(large, []):
+        copy.start()
+    for copy in small:
+        copy.wait()
+    q_lo = q_in[...].astype(BF16)
+    parts = three_parts(vec_in[...])
     merged[rows:, :] = jnp.concatenate([*parts, jnp.zeros((PAD - 3, cols), F32)], axis=0).astype(BF16)
-    p_part[...] = dot(q[...].T.astype(BF16), total, 1, 1)
+    for i in range(CHUNKS):
+        for copy in large[i]:
+            copy.wait()
+        here = slice(i * step, (i + 1) * step)
+        total = (grads_in[here, :].astype(F32) + errors_in[here, :].astype(F32)).astype(BF16)
+        merged[here, :] = total
+        p_part[:, here] = dot(q_lo, total, 1, 1)
 
 
 def add_kernel(*refs):
@@ -98,31 +118,51 @@
     out[:, rows + cols :] = jnp.concatenate([*parts, jnp.zeros((out.shape[0] - 3, cols), F32)], axis=0).astype(BF16)
 
 
-def final_kernel(owners, *refs):
-    place, own, *received = refs[: -9]
-    merged, momentum, vec_momentum, new_errors, new_momentum, new_vec, pack, p_rows, unused = refs[-9:]
-    del unused
+def final_kernel(place, merged, momentum, vec_momentum, *refs):
+    packs = refs[:-9]
+    new_errors, new_momentum, new_vec, pack, p_rows, errors_out, momentum_out, vec_out, sems = refs[-9:]
     rows, cols = new_errors.shape
     own_rows = momentum.shape[0]
-    is_owner = place[1] == 1
-
-    @pl.when(is_owner)
-    def _():
-        pack[...] = own[...]
-
-    @pl.when(jnp.logical_not(is_owner))
-    def _():
-        pack[...] = sum(r[...].astype(F32) for r in received).astype(BF16)
+    for i, candidate in enumerate(packs):
+
+        @pl.when(place[1] == i)
+        def _(candidate=candidate):
+            pack[...] = candidate[...]
 
     p_rows[...] = pack[:, :rows].T
     q_lo = pack[:, rows : rows + cols]
-    approx = dot(p_rows[...], q_lo, 1, 0)
-    new_errors[...] = (merged[:rows, :].astype(F32) - approx).astype(BF16)
+    copies = []
+    step = rows // CHUNKS
+    for i in range(CHUNKS):
+        here = pl.ds(i * step, step)
+        approx = dot(p_rows[here, :], q_lo, 1, 0)
+        errors_out[here, :] = (merged[here, :].astype(F32) - approx).astype(BF16)
+        copies.append(pltpu.make_async_copy(errors_out.at[here], new_errors.at[here], sems.at[i]))
+        copies[-1].start()
     first = pl.multiple_of(place[0] * own_rows, own_rows)
     mine = dot(p_rows[pl.ds(first, own_rows), :], q_lo, 1, 0)
-    new_momentum[...] = 0.9 * momentum[...] + mine
+    momentum_out[...] = 0.9 * momentum[...] + mine
+    copies.append(pltpu.make_async_copy(momentum_out, new_momentum, sems.at[CHUNKS]))
+    copies[-1].start()
     vec = jnp.sum(pack[:, rows + cols :].astype(F32), axis=0, keepdims=True)
-    new_vec[...] = 0.9 * vec_momentum[...] + vec
+    vec_out[...] = 0.9 * vec_momentum[...] + vec
+    copies.append(pltpu.make_async_copy(vec_out, new_vec, sems.at[CHUNKS + 1]))
+    copies[-1].start()
+    for copy in copies:
+        copy.wait()
+
+
+def completed(needed, places):
+    needed = list(needed)
+    sources = [p for p in places if p not in [a for a, _ in needed]]
+    targets = [p for p in places if p not in [b for _, b in needed]]
+    far = {(a, b): (a == b, 2 * abs(a[0] - b[0]) + (a[1] != b[1]), a, b) for a in sources for b in targets}
+    for a, b in sorted(far, key=far.get):
+        if a in sources and b in targets:
+            sources.remove(a)
+            targets.remove(b)
+            needed.append((a, b))
+    return needed
 
 
 def gathered(grads, errors, q_start, momentum, vec_grads, vec_momentum):
@@ -131,36 +171,59 @@
     rank = q_start.shape[2]
     middle = (replicas - 1) // 2
     owner = [middle + s % min(2, replicas) for s in range(sections)]
-    sources = [sorted((z for z in range(replicas) if z != o), key=lambda z, o=o: -abs(z - o)) for o in owner]
+    sources = [sorted((z for z in range(replicas) if z != o), key=lambda z, o=o: (-abs(z - o), abs(2 * z - replicas + 1))) for o in owner]
+    places = [(z, s) for z in range(replicas) for s in range(sections)]
     inward = [
-        [(sources[s][j] * sections + s, owner[s] * sections + s) for s in range(sections)] for j in range(replicas - 1)
+        completed([((sources[s][j], s), (owner[s], s)) for s in range(sections)], places) for j in range(replicas - 1)
     ]
     outward = [[(b, a) for a, b in pairs] for pairs in inward]
+    number = lambda place: place[0] * sections + place[1]
 
     def along(x, perms):
-        return [lax.ppermute(x, ("replica", "section"), p) for p in perms]
-
-    def across(x):
-        return [x] + [lax.ppermute(x, "tensor", [(i, i ^ k) for i in range(tensors)]) for k in range(1, tensors)]
+        return [lax.ppermute(x, ("replica", "section"), [(number(a), number(b)) for a, b in p]) for p in perms]
+
+    def across(x, hold):
+        parts = [x]
+        for k in range(1, tensors):
+            if k == tensors - 1 and hold is not None:
+                x = lax.optimization_barrier((x, hold))[0]
+            needed = [((owner[s], i, s), (owner[s], i ^ k, s)) for s in range(sections) for i in range(tensors)]
+            idle = [p for p in places if p[0] != owner[p[1]]]
+            pairs = needed + [((a[0], i, a[1]), (b[0], i, b[1])) for a, b in completed([], idle) for i in range(tensors)]
+            order = [((a[0] * tensors + a[1]) * sections + a[2], (b[0] * tensors + b[1]) * sections + b[2]) for a, b in pairs]
+            parts.append(lax.ppermute(x, ("replica", "tensor", "section"), order))
+        return parts
 
     p_shape = jax.ShapeDtypeStruct((rank, rows), F32)
     work = 2 * rows * cols * rank
+    block = (rows, cols)
+    merged_shape = jax.ShapeDtypeStruct((rows + PAD, cols), BF16)
     merged, p_part = call(
         merge_kernel,
-        [jax.ShapeDtypeStruct((rows + PAD, cols), BF16), p_shape],
+        [merged_shape, p_shape],
         grads[0, 0],
         errors[0, 0],
-        q_start[0],
+        q_start[0].T,
         vec_grads[0],
         flops=work,
+        in_specs=[HBM] * 4, limit=60,
+        scratch=[
+            pltpu.VMEM(block, BF16),
+            pltpu.VMEM(block, BF16),
+            pltpu.VMEM((rank, cols), F32),
+            pltpu.VMEM((1, cols), F32),
+            pltpu.SemaphoreType.DMA((3, CHUNKS)),
+        ],
     )
     p_in = along(p_part, inward)
-    m_in = along(merged, inward)
+    m_near = along(merged, inward[1:])
     p_part = call(add_kernel, [p_shape], p_part, *p_in)[0]
+    held = lax.optimization_barrier((merged, p_part))[0]
+    m_in = along(held, inward[:1]) + m_near
     for round_no in range(ROUNDS):
         last = round_no == ROUNDS - 1
         shape = jax.ShapeDtypeStruct((rank, rows + 2 * cols), BF16) if last else p_shape
-        parts = across(p_part)
+        parts = across(p_part, None if round_no else m_in[-1])
         p_part = call(
             functools.partial(factor_kernel, len(parts), replicas, last),
             [shape],
@@ -171,26 +234,35 @@
         )[0]
     received = along(p_part, outward)
     z, s = lax.axis_index("replica"), lax.axis_index("section")
-    place = jnp.stack([z, (z == jnp.asarray(owner)[s]).astype(jnp.int32)])
-    outs = [
-        jax.ShapeDtypeStruct((rows, cols), BF16),
-        jax.ShapeDtypeStruct(momentum.shape[1:], F32),
-        jax.ShapeDtypeStruct((1, cols), F32),
-    ]
-    args = [place, p_part, *received, merged, momentum[0], vec_momentum]
-    errors_out, momentum_out, vec_out = pl.pallas_call(
-        functools.partial(final_kernel, owner),
-        out_shape=outs,
-        in_specs=[pl.BlockSpec(memory_space=pltpu.SMEM)] + [VMEM] * (len(args) - 1),
-        out_specs=[VMEM] * 3,
-        scratch_shapes=[
+    came = sum(
+        jnp.where((z == sources[i][j]) & (s == i), j + 1, 0) for i in range(sections) for j in range(replicas - 1)
+    )
+    new_errors, new_momentum, new_vec = call(
+        final_kernel,
+        [
+            jax.ShapeDtypeStruct(block, BF16),
+            jax.ShapeDtypeStruct(momentum.shape[1:], F32),
+            jax.ShapeDtypeStruct((1, cols), F32),
+        ],
+        jnp.stack([z, came]).astype(jnp.int32),
+        merged,
+        momentum[0],
+        vec_momentum,
+        p_part,
+        *received,
+        flops=2 * work,
+        in_specs=[pl.BlockSpec(memory_space=pltpu.SMEM)] + [VMEM] * (replicas + 3),
+        out_specs=[HBM] * 3,
+        scratch=[
             pltpu.VMEM(p_part.shape, BF16),
             pltpu.VMEM((rows, rank), BF16),
-            pltpu.VMEM((8, 128), F32),
+            pltpu.VMEM(block, BF16),
+            pltpu.VMEM(momentum.shape[1:], F32),
+            pltpu.VMEM((1, cols), F32),
+            pltpu.SemaphoreType.DMA((CHUNKS + 2,)),
         ],
-        compiler_params=pltpu.CompilerParams(vmem_limit_bytes=32 * 1024 * 1024),
-    )(*args)
-    return errors_out[None, None], momentum_out[None], vec_out
+    )
+    return new_errors[None, None], new_momentum[None], new_vec
 
 
 def reduced(grads, errors, q_start, momentum, vec_grads, vec_momentum):

time: 65.8 us -> 48.1 us (0.73)
  waiting for transfers between devices: 29.7 us -> 15.7 us
  local copies, waits for them, and re-layouts: 4.86 us -> 0.92 us
  Pallas kernels: 6.84 us -> 9.04 us
  starting transfers between devices: 22.4 us -> 21.5 us
  between operations: 1.42 us -> 0.7 us
    ppermute x15, waiting for transfers between devices: 29.7 us -> 15.7 us  [the longest x9 13.1 us: along(): lax.ppermute(x, ('replica', 'section'), [(number(a), number(b)) for a, b...]
    unnamed x13 -> x8, local copies, waits for them, and re-layouts: 4.28 us -> 0.92 us
    pallas_call x5, Pallas kernels: 6.84 us -> 9.04 us  [call(): pl.pallas_call(kernel, out_shape=outs, in_specs=in_specs or [VMEM] * len(...]
    ppermute x15, starting transfers between devices: 22.4 us -> 21.5 us  [the longest x9 18.5 us: along(): lax.ppermute(x, ('replica', 'section'), [(number(a), number(b)) for a, b...]
  transfers between devices with their start and end apart: 15 -> 15, of which waited for: 6 -> 10; matrix products, arithmetic and copies ran while one was open for 1% -> 0% of each run, Pallas kernels for 0% -> 0%
where the time goes in v2:
time: 48.1 us; the launch traced here: 48 us
  starting transfers between devices  21.5 us (45%)
  waiting for transfers between devices  15.7 us (33%)
  Pallas kernels  9.04 us (19%)
  local copies, waits for them, and re-layouts  0.92 us (2%)
  between operations  0.7 us (1%)
    ppermute x9, starting transfers between devices, along(): lax.ppermute(x, ('replica', 'section'), [(number(a), number(b)) for a, b...  18.5 us
    ppermute x9, waiting for transfers between devices, along(): lax.ppermute(x, ('replica', 'section'), [(number(a), number(b)) for a, b...  13.1 us
    pallas_call x5, Pallas kernels, call(): pl.pallas_call(kernel, out_shape=outs, in_specs=in_specs or [VMEM] * len(...  9.04 us
    ppermute x6, starting transfers between devices, across(): parts.append(lax.ppermute(x, ('replica', 'tensor', 'section'), order))  3.04 us
    ppermute x6, waiting for transfers between devices, across(): parts.append(lax.ppermute(x, ('replica', 'tensor', 'section'), order))  2.6 us
  transfers between devices with their start and end apart: 15, of which 10 were waited for; matrix products, arithmetic and copies ran while one was open for 0% of the time, Pallas kernels for 0%

profile of v2, /device:TPU:0, one launch (start us, length us, event | category | flops | bytes accessed | tf_op | source)
XLA Modules:
  0.0 48.0 jit_solution(6481449882519596988)
XLA Ops:
  0.6 2.6 %shard_map.85 = (bf16[1040,256]{1,0:T(8,128)(2,1)}, f32[32,1024]{1,0:T(8,128)}) custom-call(bf16[1024,256]{1,0:T(8,128)(2,1)} %bitcast.12, bf16[1024,256]{1,0:T(8,128)(2,1)} %bitcast.13, f32[32,256]{1,0:T(8,128)} %bitcast.14, f32[1,256]{1,0:T(1,128)} %bitcast.15), custom_call_target="tpu_custom_call" | custom-call | flops 16777216 | bytes 1745920 | tf_op jit(solution)/shard_map/pallas_call | solution.py:27
  3.2 0.0 copy-start
  3.2 0.5 %collective-permute-start = (f32[32,1024]{1,0:T(8,128)}, f32[32,1024]{1,0:T(8,128)S(1)}, u32[]{:S(2)}, u32[]{:S(2)}) collective-permute-start(f32[32,1024]{1,0:T(8,128)} %get-tuple-element.11.refs_0_), channel_id=1, source_target_pairs={{24,8},{1,17},{0,1},{8,9},{17,16},{25,24},{9,0},{16,25},{26,10},{3... | collective-permute-start | bytes 393224 | tf_op jit(solution)/shard_map/ppermute | solution.py:183
  3.7 3.1 %collective-permute-start.1 = (f32[32,1024]{1,0:T(8,128)}, f32[32,1024]{1,0:T(8,128)S(1)}, u32[]{:S(2)}, u32[]{:S(2)}) collective-permute-start(f32[32,1024]{1,0:T(8,128)} %get-tuple-element.11.refs_0_), channel_id=1, source_target_pairs={{16,8},{9,17},{0,1},{1,0},{8,9},{17,16},{24,25},{25,24},{18,10},{1... | collective-permute-start | bytes 393224 | tf_op jit(solution)/shard_map/ppermute | solution.py:183
  6.9 0.0 collective-permute-start.2
  6.9 1.2 %collective-permute-start.5 = (bf16[1040,256]{1,0:T(8,128)(2,1)}, bf16[1040,256]{1,0:T(8,128)(2,1)S(1)}, u32[]{:S(2)}, u32[]{:S(2)}) collective-permute-start(bf16[1040,256]{1,0:T(8,128)(2,1)} %get-tuple-element.13.refs_4_.merged), channel_id=1, source_target_pairs={{0,8},{25,17},{1,0},{8,9},{17,16},{24,25},{9,1},{16,24},{2,10},{27... | collective-permute-start | bytes 1597448 | tf_op jit(solution)/shard_map/ppermute | solution.py:183
  8.1 0.0 collective-permute-start.8
  8.1 0.5 %collective-permute-done.refs_1_ = f32[32,1024]{1,0:T(8,128)S(1)} collective-permute-done((f32[32,1024]{1,0:T(8,128)}, f32[32,1024]{1,0:T(8,128)S(1)}, u32[]{:S(2)}, u32[]{:S(2)}) %collective-permute-start) | collective-permute-done | bytes 131104 | tf_op jit(solution)/shard_map/ppermute | solution.py:183
  8.6 0.0 collective-permute-done.1.refs_2_
  8.6 1.8 %collective-permute-done.2.refs_3_ = f32[32,1024]{1,0:T(8,128)S(1)} collective-permute-done((f32[32,1024]{1,0:T(8,128)}, f32[32,1024]{1,0:T(8,128)S(1)}, u32[]{:S(2)}, u32[]{:S(2)}) %collective-permute-start.2) | collective-permute-done | bytes 131104 | tf_op jit(solution)/shard_map/ppermute | solution.py:183
  10.4 0.0 copy-start.2
  10.4 0.9 %copy-done.2 = f32[32,1024]{1,0:T(8,128)S(1)} copy-done((f32[32,1024]{1,0:T(8,128)S(1)}, f32[32,1024]{1,0:T(8,128)}, u32[]{:S(2)}) %copy-start.2) | copy-done | bytes 131096
  11.3 0.0 copy-done
  11.3 0.6 %collective-permute-start.7 = (bf16[1040,256]{1,0:T(8,128)(2,1)S(1)}, bf16[1040,256]{1,0:T(8,128)(2,1)S(1)}, u32[]{:S(2)}, u32[]{:S(2)}) collective-permute-start(bf16[1040,256]{1,0:T(8,128)(2,1)S(1)} %copy-done), channel_id=1, source_target_pairs={{24,8},{1,17},{0,1},{8,9},{17,16},{25,24},{9,0},{16,25},{26,10},{3... | collective-permute-start | bytes 1597448 | tf_op jit(solution)/shard_map/ppermute | solution.py:183
  11.9 2.4 %collective-permute-start.3 = (f32[32,1024]{1,0:T(8,128)S(1)}, f32[32,1024]{1,0:T(8,128)S(1)}, u32[]{:S(2)}, u32[]{:S(2)}) collective-permute-start(f32[32,1024]{1,0:T(8,128)S(1)} %shard_map.86.refs_0_), channel_id=1, source_target_pairs={{8,10},{10,8},{12,14},{14,12},{17,19},{19,17},{21,23},{23,21},{0,1... | collective-permute-start | bytes 393224 | tf_op jit(solution)/shard_map/ppermute | solution.py:194
  14.3 0.0 collective-permute-start.4
  14.3 3.0 %collective-permute-done.5.refs_7_ = bf16[1040,256]{1,0:T(8,128)(2,1)S(1)} collective-permute-done((bf16[1040,256]{1,0:T(8,128)(2,1)}, bf16[1040,256]{1,0:T(8,128)(2,1)S(1)}, u32[]{:S(2)}, u32[]{:S(2)}) %collective-permute-start.5) | collective-permute-done | bytes 532512 | tf_op jit(solution)/shard_map/ppermute | solution.py:183
  17.3 0.0 collective-permute-start.6
  17.3 0.0 collective-permute-done.3.refs_1_
  17.3 0.0 collective-permute-done.4.refs_2_
  17.3 0.0 collective-permute-done.8.refs_6_
  17.3 1.3 %collective-permute-done.6.refs_3_ = f32[32,1024]{1,0:T(8,128)S(1)} collective-permute-done((f32[32,1024]{1,0:T(8,128)S(1)}, f32[32,1024]{1,0:T(8,128)S(1)}, u32[]{:S(2)}, u32[]{:S(2)}) %collective-permute-start.6) | collective-permute-done | bytes 131104 | tf_op jit(solution)/shard_map/ppermute | solution.py:194
  18.6 3.9 %collective-permute-done.7.refs_5_ = bf16[1040,256]{1,0:T(8,128)(2,1)S(1)} collective-permute-done((bf16[1040,256]{1,0:T(8,128)(2,1)S(1)}, bf16[1040,256]{1,0:T(8,128)(2,1)S(1)}, u32[]{:S(2)}, u32[]{:S(2)}) %collective-permute-start.7) | collective-permute-done | bytes 532512 | tf_op jit(solution)/shard_map/ppermute | solution.py:183
  22.5 2.9 %shard_map.87.refs_0_ = f32[32,1024]{1,0:T(8,128)S(1)} custom-call(f32[32,1024]{1,0:T(8,128)S(1)} %shard_map.86.refs_0_, f32[32,1024]{1,0:T(8,128)S(1)} %collective-permute-done.3.refs_1_, f32[32,1024]{1,0:T(8,128)S(1)} %collective-permute-done.4.refs_2_, f32[32,1024]{1,0:T(8,128)S(1)} %collective-permute-done.6.refs_3_, bf16[1040,256]{1,0:T(8,128)(2,1)S(1)} %copy-done, ...), custom_call_target="tpu_custom_call" | custom-call | flops 134217728 | bytes 2785280 | tf_op jit(solution)/shard_map/pallas_call | solution.py:27
  25.4 0.0 collective-permute-start.10
  25.4 0.5 %collective-permute-start.11 = (f32[32,1024]{1,0:T(8,128)S(1)}, f32[32,1024]{1,0:T(8,128)S(1)}, u32[]{:S(2)}, u32[]{:S(2)}) collective-permute-start(f32[32,1024]{1,0:T(8,128)S(1)} %shard_map.87.refs_0_), channel_id=1, source_target_pairs={{8,14},{10,12},{12,10},{14,8},{17,23},{19,21},{21,19},{23,17},{0,1... | collective-permute-start | bytes 393224 | tf_op jit(solution)/shard_map/ppermute | solution.py:194
  25.9 0.1 collective-permute-start.9
  26.0 0.0 copy-start.1
  26.0 0.8 %collective-permute-done.10.refs_2_ = f32[32,1024]{1,0:T(8,128)S(1)} collective-permute-done((f32[32,1024]{1,0:T(8,128)S(1)}, f32[32,1024]{1,0:T(8,128)S(1)}, u32[]{:S(2)}, u32[]{:S(2)}) %collective-permute-start.10) | collective-permute-done | bytes 131104 | tf_op jit(solution)/shard_map/ppermute | solution.py:194
  26.8 0.2 collective-permute-done.11.refs_3_
  27.0 0.3 collective-permute-done.9.refs_1_
  27.3 1.8 %shard_map.88.refs_0_ = bf16[32,1536]{1,0:T(8,128)(2,1)S(1)} custom-call(f32[32,1024]{1,0:T(8,128)S(1)} %shard_map.87.refs_0_, f32[32,1024]{1,0:T(8,128)S(1)} %collective-permute-done.9.refs_1_, f32[32,1024]{1,0:T(8,128)S(1)} %collective-permute-done.10.refs_2_, f32[32,1024]{1,0:T(8,128)S(1)} %collective-permute-done.11.refs_3_, ...), custom_call_target="tpu_custom_call" | custom-call | flops 134217728 | bytes 2752512 | tf_op jit(solution)/shard_map/pallas_call | solution.py:27
  29.1 12.5 %collective-permute-start.12 = (bf16[32,1536]{1,0:T(8,128)(2,1)S(1)}, bf16[32,1536]{1,0:T(8,128)(2,1)S(1)}, u32[]{:S(2)}, u32[]{:S(2)}) collective-permute-start(bf16[32,1536]{1,0:T(8,128)(2,1)S(1)} %shard_map.88.refs_0_), channel_id=1, source_target_pairs={{8,24},{17,1},{1,0},{9,8},{16,17},{24,25},{0,9},{25,16},{10,26},{1... | collective-permute-start | bytes 294920 | tf_op jit(solution)/shard_map/ppermute | solution.py:183
  41.6 0.0 collective-permute-start.13
  41.6 0.5 %collective-permute-start.14 = (bf16[32,1536]{1,0:T(8,128)(2,1)S(1)}, bf16[32,1536]{1,0:T(8,128)(2,1)S(1)}, u32[]{:S(2)}, u32[]{:S(2)}) collective-permute-start(bf16[32,1536]{1,0:T(8,128)(2,1)S(1)} %shard_map.88.refs_0_), channel_id=1, source_target_pairs={{8,0},{17,25},{0,1},{9,8},{16,17},{25,24},{1,9},{24,16},{10,2},{19... | collective-permute-start | bytes 294920 | tf_op jit(solution)/shard_map/ppermute | solution.py:183
  42.1 0.1 pad_add_fusion.place
  42.2 0.0 copy-start.3
  42.2 2.4 %collective-permute-done.12.refs_1_ = bf16[32,1536]{1,0:T(8,128)(2,1)S(1)} collective-permute-done((bf16[32,1536]{1,0:T(8,128)(2,1)S(1)}, bf16[32,1536]{1,0:T(8,128)(2,1)S(1)}, u32[]{:S(2)}, u32[]{:S(2)}) %collective-permute-start.12) | collective-permute-done | bytes 98336 | tf_op jit(solution)/shard_map/ppermute | solution.py:183
  44.6 0.0 collective-permute-done.13.refs_2_
  44.6 1.6 %collective-permute-done.14.refs_3_ = bf16[32,1536]{1,0:T(8,128)(2,1)S(1)} collective-permute-done((bf16[32,1536]{1,0:T(8,128)(2,1)S(1)}, bf16[32,1536]{1,0:T(8,128)(2,1)S(1)}, u32[]{:S(2)}, u32[]{:S(2)}) %collective-permute-start.14) | collective-permute-done | bytes 98336 | tf_op jit(solution)/shard_map/ppermute | solution.py:183
  46.2 0.0 copy-done.1
  46.2 0.0 copy-done.3
  46.2 1.8 %shard_map.89 = (bf16[1024,256]{1,0:T(8,128)(2,1)}, f32[256,256]{1,0:T(8,128)}, f32[1,256]{1,0:T(1,128)}) custom-call(s32[2]{0:T(128)S(1)} %pad_add_fusion.place, bf16[1040,256]{1,0:T(8,128)(2,1)S(1)} %copy-done, f32[256,256]{1,0:T(8,128)S(1)} %bitcast.11, f32[1,256]{1,0:T(1,128)S(1)} %copy-done.3, bf16[32,1536]{1,0:T(8,128)(2,1)S(1)} %shard_map.88.refs_0_, ...), custom_call_target="tpu_custom_call" | custom-call | flops 33554432 | bytes 1976328 | tf_op jit(solution)/shard_map/pallas_call | solution.py:27
  (1 shorter events, 0.0 us)
Async XLA Ops:
  3.2 8.1 %copy-start = (bf16[1040,256]{1,0:T(8,128)(2,1)S(1)}, bf16[1040,256]{1,0:T(8,128)(2,1)}, u32[]{:S(2)}) copy-start(bf16[1040,256]{1,0:T(8,128)(2,1)} %get-tuple-element.13.refs_4_.merged) | copy-start | bytes 1597444
  3.2 5.4 %collective-permute-start = (f32[32,1024]{1,0:T(8,128)}, f32[32,1024]{1,0:T(8,128)S(1)}, u32[]{:S(2)}, u32[]{:S(2)}) collective-permute-start(f32[32,1024]{1,0:T(8,128)} %get-tuple-element.11.refs_0_), channel_id=1, source_target_pairs={{24,8},{1,17},{0,1},{8,9},{17,16},{25,24},{9,0},{16,25},{26,10},{3... | collective-permute-start | bytes 393224 | tf_op jit(solution)/shard_map/ppermute | solution.py:183
  3.7 4.9 %collective-permute-start.1 = (f32[32,1024]{1,0:T(8,128)}, f32[32,1024]{1,0:T(8,128)S(1)}, u32[]{:S(2)}, u32[]{:S(2)}) collective-permute-start(f32[32,1024]{1,0:T(8,128)} %get-tuple-element.11.refs_0_), channel_id=1, source_target_pairs={{16,8},{9,17},{0,1},{1,0},{8,9},{17,16},{24,25},{25,24},{18,10},{1... | collective-permute-start | bytes 393224 | tf_op jit(solution)/shard_map/ppermute | solution.py:183
  6.9 3.5 %collective-permute-start.2 = (f32[32,1024]{1,0:T(8,128)}, f32[32,1024]{1,0:T(8,128)S(1)}, u32[]{:S(2)}, u32[]{:S(2)}) collective-permute-start(f32[32,1024]{1,0:T(8,128)} %get-tuple-element.11.refs_0_), channel_id=1, source_target_pairs={{0,8},{25,17},{1,0},{8,9},{17,16},{24,25},{9,1},{16,24},{2,10},{27... | collective-permute-start | bytes 393224 | tf_op jit(solution)/shard_map/ppermute | solution.py:183
  6.9 10.4 %collective-permute-start.5 = (bf16[1040,256]{1,0:T(8,128)(2,1)}, bf16[1040,256]{1,0:T(8,128)(2,1)S(1)}, u32[]{:S(2)}, u32[]{:S(2)}) collective-permute-start(bf16[1040,256]{1,0:T(8,128)(2,1)} %get-tuple-element.13.refs_4_.merged), channel_id=1, source_target_pairs={{0,8},{25,17},{1,0},{8,9},{17,16},{24,25},{9,1},{16,24},{2,10},{27... | collective-permute-start | bytes 1597448 | tf_op jit(solution)/shard_map/ppermute | solution.py:183
  8.1 9.2 %collective-permute-start.8 = (bf16[1040,256]{1,0:T(8,128)(2,1)}, bf16[1040,256]{1,0:T(8,128)(2,1)S(1)}, u32[]{:S(2)}, u32[]{:S(2)}) collective-permute-start(bf16[1040,256]{1,0:T(8,128)(2,1)} %get-tuple-element.13.refs_4_.merged), channel_id=1, source_target_pairs={{16,8},{9,17},{0,1},{1,0},{8,9},{17,16},{24,25},{25,24},{18,10},{1... | collective-permute-start | bytes 1597448 | tf_op jit(solution)/shard_map/ppermute | solution.py:183
  10.4 0.9 %copy-start.2 = (f32[32,1024]{1,0:T(8,128)S(1)}, f32[32,1024]{1,0:T(8,128)}, u32[]{:S(2)}) copy-start(f32[32,1024]{1,0:T(8,128)} %get-tuple-element.11.refs_0_) | copy-start | bytes 393220
  11.3 11.2 %collective-permute-start.7 = (bf16[1040,256]{1,0:T(8,128)(2,1)S(1)}, bf16[1040,256]{1,0:T(8,128)(2,1)S(1)}, u32[]{:S(2)}, u32[]{:S(2)}) collective-permute-start(bf16[1040,256]{1,0:T(8,128)(2,1)S(1)} %copy-done), channel_id=1, source_target_pairs={{24,8},{1,17},{0,1},{8,9},{17,16},{25,24},{9,0},{16,25},{26,10},{3... | collective-permute-start | bytes 1597448 | tf_op jit(solution)/shard_map/ppermute | solution.py:183
  11.9 5.4 %collective-permute-start.3 = (f32[32,1024]{1,0:T(8,128)S(1)}, f32[32,1024]{1,0:T(8,128)S(1)}, u32[]{:S(2)}, u32[]{:S(2)}) collective-permute-start(f32[32,1024]{1,0:T(8,128)S(1)} %shard_map.86.refs_0_), channel_id=1, source_target_pairs={{8,10},{10,8},{12,14},{14,12},{17,19},{19,17},{21,23},{23,21},{0,1... | collective-permute-start | bytes 393224 | tf_op jit(solution)/shard_map/ppermute | solution.py:194
  14.3 3.0 %collective-permute-start.4 = (f32[32,1024]{1,0:T(8,128)S(1)}, f32[32,1024]{1,0:T(8,128)S(1)}, u32[]{:S(2)}, u32[]{:S(2)}) collective-permute-start(f32[32,1024]{1,0:T(8,128)S(1)} %shard_map.86.refs_0_), channel_id=1, source_target_pairs={{8,12},{10,14},{12,8},{14,10},{17,21},{19,23},{21,17},{23,19},{0,1... | collective-permute-start | bytes 393224 | tf_op jit(solution)/shard_map/ppermute | solution.py:194
  17.3 1.3 %collective-permute-start.6 = (f32[32,1024]{1,0:T(8,128)S(1)}, f32[32,1024]{1,0:T(8,128)S(1)}, u32[]{:S(2)}, u32[]{:S(2)}) collective-permute-start(f32[32,1024]{1,0:T(8,128)S(1)} %shard_map.86.refs_0_), channel_id=1, source_target_pairs={{8,14},{10,12},{12,10},{14,8},{17,23},{19,21},{21,19},{23,17},{0,1... | collective-permute-start | bytes 393224 | tf_op jit(solution)/shard_map/ppermute | solution.py:194
  25.4 1.4 %collective-permute-start.10 = (f32[32,1024]{1,0:T(8,128)S(1)}, f32[32,1024]{1,0:T(8,128)S(1)}, u32[]{:S(2)}, u32[]{:S(2)}) collective-permute-start(f32[32,1024]{1,0:T(8,128)S(1)} %shard_map.87.refs_0_), channel_id=1, source_target_pairs={{8,12},{10,14},{12,8},{14,10},{17,21},{19,23},{21,17},{23,19},{0,1... | collective-permute-start | bytes 393224 | tf_op jit(solution)/shard_map/ppermute | solution.py:194
  25.4 1.5 %collective-permute-start.11 = (f32[32,1024]{1,0:T(8,128)S(1)}, f32[32,1024]{1,0:T(8,128)S(1)}, u32[]{:S(2)}, u32[]{:S(2)}) collective-permute-start(f32[32,1024]{1,0:T(8,128)S(1)} %shard_map.87.refs_0_), channel_id=1, source_target_pairs={{8,14},{10,12},{12,10},{14,8},{17,23},{19,21},{21,19},{23,17},{0,1... | collective-permute-start | bytes 393224 | tf_op jit(solution)/shard_map/ppermute | solution.py:194
  25.9 1.3 %collective-permute-start.9 = (f32[32,1024]{1,0:T(8,128)S(1)}, f32[32,1024]{1,0:T(8,128)S(1)}, u32[]{:S(2)}, u32[]{:S(2)}) collective-permute-start(f32[32,1024]{1,0:T(8,128)S(1)} %shard_map.87.refs_0_), channel_id=1, source_target_pairs={{8,10},{10,8},{12,14},{14,12},{17,19},{19,17},{21,23},{23,21},{0,1... | collective-permute-start | bytes 393224 | tf_op jit(solution)/shard_map/ppermute | solution.py:194
  26.0 20.2 %copy-start.1 = (f32[1,256,256]{2,1,0:T(8,128)S(1)}, f32[1,256,256]{2,1,0:T(8,128)}, u32[]{:S(2)}) copy-start(f32[1,256,256]{2,1,0:T(8,128)} %param.9) | copy-start | bytes 786436
  29.1 15.5 %collective-permute-start.12 = (bf16[32,1536]{1,0:T(8,128)(2,1)S(1)}, bf16[32,1536]{1,0:T(8,128)(2,1)S(1)}, u32[]{:S(2)}, u32[]{:S(2)}) collective-permute-start(bf16[32,1536]{1,0:T(8,128)(2,1)S(1)} %shard_map.88.refs_0_), channel_id=1, source_target_pairs={{8,24},{17,1},{1,0},{9,8},{16,17},{24,25},{0,9},{25,16},{10,26},{1... | collective-permute-start | bytes 294920 | tf_op jit(solution)/shard_map/ppermute | solution.py:183
  41.6 3.0 %collective-permute-start.13 = (bf16[32,1536]{1,0:T(8,128)(2,1)S(1)}, bf16[32,1536]{1,0:T(8,128)(2,1)S(1)}, u32[]{:S(2)}, u32[]{:S(2)}) collective-permute-start(bf16[32,1536]{1,0:T(8,128)(2,1)S(1)} %shard_map.88.refs_0_), channel_id=1, source_target_pairs={{8,16},{17,9},{1,0},{0,1},{9,8},{16,17},{25,24},{24,25},{10,18},{1... | collective-permute-start | bytes 294920 | tf_op jit(solution)/shard_map/ppermute | solution.py:183
  41.6 4.6 %collective-permute-start.14 = (bf16[32,1536]{1,0:T(8,128)(2,1)S(1)}, bf16[32,1536]{1,0:T(8,128)(2,1)S(1)}, u32[]{:S(2)}, u32[]{:S(2)}) collective-permute-start(bf16[32,1536]{1,0:T(8,128)(2,1)S(1)} %shard_map.88.refs_0_), channel_id=1, source_target_pairs={{8,0},{17,25},{0,1},{9,8},{16,17},{25,24},{1,9},{24,16},{10,2},{19... | collective-permute-start | bytes 294920 | tf_op jit(solution)/shard_map/ppermute | solution.py:183
  42.2 4.0 %copy-start.3 = (f32[1,256]{1,0:T(1,128)S(1)}, f32[1,256]{1,0:T(1,128)}, u32[]{:S(2)}) copy-start(f32[1,256]{1,0:T(1,128)} %vec_momentum.1) | copy-start | bytes 3076

commit v3 on v2

--- a/solution.py
+++ b/solution.py
@@ -100,8 +100,13 @@
     refs[-1][...] = tree([r[...] for r in refs[:-1]])
 
 
-def factor_kernel(n_p, replicas, last, *refs):
-    p_parts, merged, out = refs[:n_p], refs[n_p:-1], refs[-1]
+def factor_kernel(n_p, replicas, last, owner, *refs):
+    @pl.when(lax.axis_index("replica") == owner[0] + lax.axis_index("section") * (owner[-1] - owner[0]))
+    def _():
+        factor_step(refs[:n_p], refs[n_p:-1], refs[-1], replicas, last)
+
+
+def factor_step(p_parts, merged, out, replicas, last):
     rows, cols = merged[0].shape[0] - PAD, merged[0].shape[1]
     p_sum = tree([p[...] for p in p_parts]) * (1.0 / replicas)
     inverse = inverse_factor(dot(p_sum, p_sum, 1, 1, HIGHEST))
@@ -118,14 +123,18 @@
     out[:, rows + cols :] = jnp.concatenate([*parts, jnp.zeros((out.shape[0] - 3, cols), F32)], axis=0).astype(BF16)
 
 
-def final_kernel(place, merged, momentum, vec_momentum, *refs):
+def final_kernel(sources, merged, momentum, vec_momentum, *refs):
     packs = refs[:-9]
     new_errors, new_momentum, new_vec, pack, p_rows, errors_out, momentum_out, vec_out, sems = refs[-9:]
     rows, cols = new_errors.shape
     own_rows = momentum.shape[0]
+    z, s = lax.axis_index("replica"), lax.axis_index("section")
+    came = sum(
+        jnp.where((z == row[j]) & (s == i), j + 1, 0) for i, row in enumerate(sources) for j in range(len(row))
+    )
     for i, candidate in enumerate(packs):
 
-        @pl.when(place[1] == i)
+        @pl.when(came == i)
         def _(candidate=candidate):
             pack[...] = candidate[...]
 
@@ -139,7 +148,7 @@
         errors_out[here, :] = (merged[here, :].astype(F32) - approx).astype(BF16)
         copies.append(pltpu.make_async_copy(errors_out.at[here], new_errors.at[here], sems.at[i]))
         copies[-1].start()
-    first = pl.multiple_of(place[0] * own_rows, own_rows)
+    first = pl.multiple_of(z * own_rows, own_rows)
     mine = dot(p_rows[pl.ds(first, own_rows), :], q_lo, 1, 0)
     momentum_out[...] = 0.9 * momentum[...] + mine
     copies.append(pltpu.make_async_copy(momentum_out, new_momentum, sems.at[CHUNKS]))
@@ -170,8 +179,9 @@
     rows, cols = grads.shape[2:]
     rank = q_start.shape[2]
     middle = (replicas - 1) // 2
+    distance = lambda z, o: (-(abs(2 * z - replicas + 1) <= 1), -abs(z - o))
     owner = [middle + s % min(2, replicas) for s in range(sections)]
-    sources = [sorted((z for z in range(replicas) if z != o), key=lambda z, o=o: (-abs(z - o), abs(2 * z - replicas + 1))) for o in owner]
+    sources = [sorted((z for z in range(replicas) if z != o), key=lambda z, o=o: distance(z, o)) for o in owner]
     places = [(z, s) for z in range(replicas) for s in range(sections)]
     inward = [
         completed([((sources[s][j], s), (owner[s], s)) for s in range(sections)], places) for j in range(replicas - 1)
@@ -182,14 +192,13 @@
     def along(x, perms):
         return [lax.ppermute(x, ("replica", "section"), [(number(a), number(b)) for a, b in p]) for p in perms]
 
-    def across(x, hold):
+    def across(x, steps):
         parts = [x]
-        for k in range(1, tensors):
-            if k == tensors - 1 and hold is not None:
-                x = lax.optimization_barrier((x, hold))[0]
-            needed = [((owner[s], i, s), (owner[s], i ^ k, s)) for s in range(sections) for i in range(tensors)]
-            idle = [p for p in places if p[0] != owner[p[1]]]
-            pairs = needed + [((a[0], i, a[1]), (b[0], i, b[1])) for a, b in completed([], idle) for i in range(tensors)]
+        for k in steps:
+            busy = [z for z in range(replicas) if z in owner]
+            idle = [p for p in places if p[0] not in busy]
+            pairs = [((z, i, s), (z, i ^ k, s)) for z in busy for s in range(sections) for i in range(tensors)]
+            pairs += [((a[0], i, a[1]), (b[0], i, b[1])) for a, b in completed([], idle) for i in range(tensors)]
             order = [((a[0] * tensors + a[1]) * sections + a[2], (b[0] * tensors + b[1]) * sections + b[2]) for a, b in pairs]
             parts.append(lax.ppermute(x, ("replica", "tensor", "section"), order))
         return parts
@@ -201,12 +210,9 @@
     merged, p_part = call(
         merge_kernel,
         [merged_shape, p_shape],
-        grads[0, 0],
-        errors[0, 0],
-        q_start[0].T,
-        vec_grads[0],
+        *(pltpu.with_memory_space_constraint(x, pltpu.HBM) for x in (grads[0, 0], errors[0, 0], q_start[0].T, vec_grads[0])),
         flops=work,
-        in_specs=[HBM] * 4, limit=60,
+        in_specs=[HBM] * 4,
         scratch=[
             pltpu.VMEM(block, BF16),
             pltpu.VMEM(block, BF16),
@@ -216,16 +222,23 @@
         ],
     )
     p_in = along(p_part, inward)
-    m_near = along(merged, inward[1:])
+    m_near = along(merged, inward[:1] + inward[2:])
     p_part = call(add_kernel, [p_shape], p_part, *p_in)[0]
     held = lax.optimization_barrier((merged, p_part))[0]
-    m_in = along(held, inward[:1]) + m_near
+    m_in = along(held, inward[1:2]) + m_near
     for round_no in range(ROUNDS):
         last = round_no == ROUNDS - 1
         shape = jax.ShapeDtypeStruct((rank, rows + 2 * cols), BF16) if last else p_shape
-        parts = across(p_part, None if round_no else m_in[-1])
+        if round_no:
+            parts = across(p_part, range(1, tensors))
+        else:
+            k = 1
+            while 2 * k < tensors:
+                p_part = tree(across(p_part, [k]))
+                k *= 2
+            parts = across(p_part, [k] if k < tensors else [])
         p_part = call(
-            functools.partial(factor_kernel, len(parts), replicas, last),
+            functools.partial(factor_kernel, len(parts), replicas, last, owner),
             [shape],
             *parts,
             merged,
@@ -233,25 +246,19 @@
             flops=2 * replicas * work,
         )[0]
     received = along(p_part, outward)
-    z, s = lax.axis_index("replica"), lax.axis_index("section")
-    came = sum(
-        jnp.where((z == sources[i][j]) & (s == i), j + 1, 0) for i in range(sections) for j in range(replicas - 1)
-    )
     new_errors, new_momentum, new_vec = call(
-        final_kernel,
+        functools.partial(final_kernel, sources),
         [
             jax.ShapeDtypeStruct(block, BF16),
             jax.ShapeDtypeStruct(momentum.shape[1:], F32),
             jax.ShapeDtypeStruct((1, cols), F32),
         ],
-        jnp.stack([z, came]).astype(jnp.int32),
         merged,
         momentum[0],
         vec_momentum,
         p_part,
         *received,
         flops=2 * work,
-        in_specs=[pl.BlockSpec(memory_space=pltpu.SMEM)] + [VMEM] * (replicas + 3),
         out_specs=[HBM] * 3,
         scratch=[
             pltpu.VMEM(p_part.shape, BF16),

time: 48.1 us -> 41.2 us (0.86)
  Pallas kernels: 9.04 us -> 3.15 us
  starting transfers between devices: 21.5 us -> 23.6 us
  waiting for transfers between devices: 15.7 us -> 13.7 us
  local copies, waits for them, and re-layouts: 0.92 us -> 0.01 us
    pallas_call x5, Pallas kernels: 9.04 us -> 3.15 us  [call(): pl.pallas_call(kernel, out_shape=outs, in_specs=in_specs or [VMEM] * len(...]
    ppermute x9, waiting for transfers between devices: 13.1 us -> 10.3 us  [along(): lax.ppermute(x, ('replica', 'section'), [(number(a), number(b)) for a, b...]
    ppermute x6 -> x5, starting transfers between devices: 3.04 us -> 4.11 us  [across(): parts.append(lax.ppermute(x, ('replica', 'tensor', 'section'), order))]
    ppermute x9, starting transfers between devices: 18.5 us -> 19.4 us  [along(): lax.ppermute(x, ('replica', 'section'), [(number(a), number(b)) for a, b...]
    unnamed x8 -> x4, local copies, waits for them, and re-layouts: 0.92 us -> 0.01 us
    ppermute x6 -> x5, waiting for transfers between devices: 2.6 us -> 3.32 us  [across(): parts.append(lax.ppermute(x, ('replica', 'tensor', 'section'), order))]
  transfers between devices with their start and end apart: 15 -> 14, of which waited for: 10 -> 10; matrix products, arithmetic and copies ran while one was open for 0% -> 0% of each run, Pallas kernels for 0% -> 0%
where the time goes in v3:
time: 41.2 us; the launch traced here: 41.1 us
  starting transfers between devices  23.6 us (57%)
  waiting for transfers between devices  13.7 us (33%)
  Pallas kernels  3.15 us (8%)
  between operations  0.67 us (2%)
    ppermute x9, starting transfers between devices, along(): lax.ppermute(x, ('replica', 'section'), [(number(a), number(b)) for a, b...  19.4 us
    ppermute x9, waiting for transfers between devices, along(): lax.ppermute(x, ('replica', 'section'), [(number(a), number(b)) for a, b...  10.3 us
    ppermute x5, starting transfers between devices, across(): parts.append(lax.ppermute(x, ('replica', 'tensor', 'section'), order))  4.11 us
    ppermute x5, waiting for transfers between devices, across(): parts.append(lax.ppermute(x, ('replica', 'tensor', 'section'), order))  3.32 us
    pallas_call x5, Pallas kernels, call(): pl.pallas_call(kernel, out_shape=outs, in_specs=in_specs or [VMEM] * len(...  3.15 us
  transfers between devices with their start and end apart: 14, of which 10 were waited for; matrix products, arithmetic and copies ran while one was open for 0% of the time, Pallas kernels for 0%

profile of v3, /device:TPU:0, one launch (start us, length us, event | category | flops | bytes accessed | tf_op | source)
XLA Modules:
  0.0 41.1 jit_solution(17453744930441071211)
XLA Ops:
  0.6 1.9 %shard_map.85 = (bf16[1040,256]{1,0:T(8,128)(2,1)S(1)}, f32[32,1024]{1,0:T(8,128)S(1)}) custom-call(bf16[1024,256]{1,0:T(8,128)(2,1)} %bitcast.10, bf16[1024,256]{1,0:T(8,128)(2,1)} %bitcast.11, f32[32,256]{1,0:T(8,128)} %bitcast.12, f32[1,256]{1,0:T(1,128)} %bitcast.13), custom_call_target="tpu_custom_call" | custom-call | flops 16777216 | bytes 1745920 | tf_op jit(solution)/shard_map/pallas_call | solution.py:27
  2.5 3.1 %collective-permute-start.2 = (f32[32,1024]{1,0:T(8,128)S(1)}, f32[32,1024]{1,0:T(8,128)S(1)}, u32[]{:S(2)}, u32[]{:S(2)}) collective-permute-start(f32[32,1024]{1,0:T(8,128)S(1)} %get-tuple-element.10.refs_0_), channel_id=1, source_target_pairs={{0,8},{25,17},{1,0},{8,9},{17,16},{24,25},{9,1},{16,24},{2,10},{27... | collective-permute-start | bytes 393224 | tf_op jit(solution)/shard_map/ppermute | solution.py:193
  5.6 0.0 collective-permute-start.1
  5.6 1.2 %collective-permute-start = (f32[32,1024]{1,0:T(8,128)S(1)}, f32[32,1024]{1,0:T(8,128)S(1)}, u32[]{:S(2)}, u32[]{:S(2)}) collective-permute-start(f32[32,1024]{1,0:T(8,128)S(1)} %get-tuple-element.10.refs_0_), channel_id=1, source_target_pairs={{16,8},{9,17},{0,1},{1,0},{8,9},{17,16},{24,25},{25,24},{18,10},{1... | collective-permute-start | bytes 393224 | tf_op jit(solution)/shard_map/ppermute | solution.py:193
  6.9 0.9 %collective-permute-start.7 = (bf16[1040,256]{1,0:T(8,128)(2,1)S(1)}, bf16[1040,256]{1,0:T(8,128)(2,1)S(1)}, u32[]{:S(2)}, u32[]{:S(2)}) collective-permute-start(bf16[1040,256]{1,0:T(8,128)(2,1)S(1)} %get-tuple-element.11.refs_2_.refs_4_.merged), channel_id=1, source_target_pairs={{0,8},{25,17},{1,0},{8,9},{17,16},{24,25},{9,1},{16,24},{2,10},{27... | collective-permute-start | bytes 1597448 | tf_op jit(solution)/shard_map/ppermute | solution.py:193
  7.7 0.0 collective-permute-start.6
  7.8 1.3 %collective-permute-done.2.refs_3_ = f32[32,1024]{1,0:T(8,128)S(1)} collective-permute-done((f32[32,1024]{1,0:T(8,128)S(1)}, f32[32,1024]{1,0:T(8,128)S(1)}, u32[]{:S(2)}, u32[]{:S(2)}) %collective-permute-start.2) | collective-permute-done | bytes 131104 | tf_op jit(solution)/shard_map/ppermute | solution.py:193
  9.0 1.0 %collective-permute-done.1.refs_2_ = f32[32,1024]{1,0:T(8,128)S(1)} collective-permute-done((f32[32,1024]{1,0:T(8,128)S(1)}, f32[32,1024]{1,0:T(8,128)S(1)}, u32[]{:S(2)}, u32[]{:S(2)}) %collective-permute-start.1) | collective-permute-done | bytes 131104 | tf_op jit(solution)/shard_map/ppermute | solution.py:193
  10.0 0.0 collective-permute-done.refs_1_
  10.0 0.2 collective-permute-start.5
  10.2 3.2 %collective-permute-start.3 = (f32[32,1024]{1,0:T(8,128)S(1)}, f32[32,1024]{1,0:T(8,128)S(1)}, u32[]{:S(2)}, u32[]{:S(2)}) collective-permute-start(f32[32,1024]{1,0:T(8,128)S(1)} %shard_map.86), channel_id=1, source_target_pairs={{8,10},{10,8},{12,14},{14,12},{9,11},{11,9},{13,15},{15,13},{16,18... | collective-permute-start | bytes 393224 | tf_op jit(solution)/shard_map/ppermute | solution.py:203
  13.4 1.0 %collective-permute-done.3 = f32[32,1024]{1,0:T(8,128)S(1)} collective-permute-done((f32[32,1024]{1,0:T(8,128)S(1)}, f32[32,1024]{1,0:T(8,128)S(1)}, u32[]{:S(2)}, u32[]{:S(2)}) %collective-permute-start.3) | collective-permute-done | bytes 131104 | tf_op jit(solution)/shard_map/ppermute | solution.py:203
  14.4 0.4 %collective-permute-start.4 = (f32[32,1024]{1,0:T(8,128)S(1)}, f32[32,1024]{1,0:T(8,128)S(1)}, u32[]{:S(2)}, u32[]{:S(2)}) collective-permute-start(f32[32,1024]{1,0:T(8,128)S(1)} %add.3.refs_0_), channel_id=1, source_target_pairs={{8,12},{10,14},{12,8},{14,10},{9,13},{11,15},{13,9},{15,11},{16,20... | collective-permute-start | bytes 393224 | tf_op jit(solution)/shard_map/ppermute | solution.py:203
  14.8 1.0 %collective-permute-done.4.refs_1_ = f32[32,1024]{1,0:T(8,128)S(1)} collective-permute-done((f32[32,1024]{1,0:T(8,128)S(1)}, f32[32,1024]{1,0:T(8,128)S(1)}, u32[]{:S(2)}, u32[]{:S(2)}) %collective-permute-start.4) | collective-permute-done | bytes 131104 | tf_op jit(solution)/shard_map/ppermute | solution.py:203
  15.8 0.8 %collective-permute-done.7.refs_5_.refs_7_ = bf16[1040,256]{1,0:T(8,128)(2,1)S(1)} collective-permute-done((bf16[1040,256]{1,0:T(8,128)(2,1)S(1)}, bf16[1040,256]{1,0:T(8,128)(2,1)S(1)}, u32[]{:S(2)}, u32[]{:S(2)}) %collective-permute-start.7) | collective-permute-done | bytes 532512 | tf_op jit(solution)/shard_map/ppermute | solution.py:193
  16.6 0.0 collective-permute-done.6.refs_4_.refs_6_
  16.6 4.8 %collective-permute-done.5.refs_3_.refs_5_ = bf16[1040,256]{1,0:T(8,128)(2,1)S(1)} collective-permute-done((bf16[1040,256]{1,0:T(8,128)(2,1)S(1)}, bf16[1040,256]{1,0:T(8,128)(2,1)S(1)}, u32[]{:S(2)}, u32[]{:S(2)}) %collective-permute-start.5) | collective-permute-done | bytes 532512 | tf_op jit(solution)/shard_map/ppermute | solution.py:193
  21.4 0.0 copy-start
  21.4 0.0 collective-permute-start.10
  21.4 0.5 %collective-permute-start.9 = (f32[32,1024]{1,0:T(8,128)S(1)}, f32[32,1024]{1,0:T(8,128)S(1)}, u32[]{:S(2)}, u32[]{:S(2)}) collective-permute-start(f32[32,1024]{1,0:T(8,128)S(1)} %shard_map.87.refs_0_), channel_id=1, source_target_pairs={{8,12},{10,14},{12,8},{14,10},{9,13},{11,15},{13,9},{15,11},{16,20... | collective-permute-start | bytes 393224 | tf_op jit(solution)/shard_map/ppermute | solution.py:203
  21.9 0.0 collective-permute-start.8
  21.9 0.8 %collective-permute-done.10.refs_3_ = f32[32,1024]{1,0:T(8,128)S(1)} collective-permute-done((f32[32,1024]{1,0:T(8,128)S(1)}, f32[32,1024]{1,0:T(8,128)S(1)}, u32[]{:S(2)}, u32[]{:S(2)}) %collective-permute-start.10) | collective-permute-done | bytes 131104 | tf_op jit(solution)/shard_map/ppermute | solution.py:203
  22.8 0.2 collective-permute-done.9.refs_2_
  22.9 0.3 collective-permute-done.8.refs_1_
  23.3 0.0 copy-start.1
  23.3 0.2 collective-permute-start.13
  23.5 13.9 %collective-permute-start.12 = (bf16[32,1536]{1,0:T(8,128)(2,1)S(1)}, bf16[32,1536]{1,0:T(8,128)(2,1)S(1)}, u32[]{:S(2)}, u32[]{:S(2)}) collective-permute-start(bf16[32,1536]{1,0:T(8,128)(2,1)S(1)} %shard_map.88.refs_0_), channel_id=1, source_target_pairs={{8,24},{17,1},{1,0},{9,8},{16,17},{24,25},{0,9},{25,16},{10,26},{1... | collective-permute-start | bytes 294920 | tf_op jit(solution)/shard_map/ppermute | solution.py:193
  37.3 0.0 collective-permute-start.11
  37.3 2.5 %collective-permute-done.13.refs_3_ = bf16[32,1536]{1,0:T(8,128)(2,1)S(1)} collective-permute-done((bf16[32,1536]{1,0:T(8,128)(2,1)S(1)}, bf16[32,1536]{1,0:T(8,128)(2,1)S(1)}, u32[]{:S(2)}, u32[]{:S(2)}) %collective-permute-start.13) | collective-permute-done | bytes 98336 | tf_op jit(solution)/shard_map/ppermute | solution.py:193
  39.8 0.0 collective-permute-done.12.refs_2_
  39.8 0.0 collective-permute-done.11.refs_1_
  39.8 0.0 copy-done
  39.8 0.0 copy-done.1
  39.8 1.2 %shard_map.89 = (bf16[1024,256]{1,0:T(8,128)(2,1)}, f32[256,256]{1,0:T(8,128)}, f32[1,256]{1,0:T(1,128)}) custom-call(bf16[1040,256]{1,0:T(8,128)(2,1)S(1)} %get-tuple-element.11.refs_2_.refs_4_.merged, f32[256,256]{1,0:T(8,128)S(1)} %bitcast.9, f32[1,256]{1,0:T(1,128)S(1)} %copy-done.1, bf16[32,1536]{1,0:T(8,128)(2,1)S(1)} %shard_map.88.refs_0_, ...), custom_call_target="tpu_custom_call" | custom-call | flops 33554432 | bytes 1976320 | tf_op jit(solution)/shard_map/pallas_call | solution.py:27
  (4 shorter events, 0.0 us)
Async XLA Ops:
  2.5 6.5 %collective-permute-start.2 = (f32[32,1024]{1,0:T(8,128)S(1)}, f32[32,1024]{1,0:T(8,128)S(1)}, u32[]{:S(2)}, u32[]{:S(2)}) collective-permute-start(f32[32,1024]{1,0:T(8,128)S(1)} %get-tuple-element.10.refs_0_), channel_id=1, source_target_pairs={{0,8},{25,17},{1,0},{8,9},{17,16},{24,25},{9,1},{16,24},{2,10},{27... | collective-permute-start | bytes 393224 | tf_op jit(solution)/shard_map/ppermute | solution.py:193
  5.6 4.4 %collective-permute-start.1 = (f32[32,1024]{1,0:T(8,128)S(1)}, f32[32,1024]{1,0:T(8,128)S(1)}, u32[]{:S(2)}, u32[]{:S(2)}) collective-permute-start(f32[32,1024]{1,0:T(8,128)S(1)} %get-tuple-element.10.refs_0_), channel_id=1, source_target_pairs={{24,8},{1,17},{0,1},{8,9},{17,16},{25,24},{9,0},{16,25},{26,10},{3... | collective-permute-start | bytes 393224 | tf_op jit(solution)/shard_map/ppermute | solution.py:193
  5.6 4.4 %collective-permute-start = (f32[32,1024]{1,0:T(8,128)S(1)}, f32[32,1024]{1,0:T(8,128)S(1)}, u32[]{:S(2)}, u32[]{:S(2)}) collective-permute-start(f32[32,1024]{1,0:T(8,128)S(1)} %get-tuple-element.10.refs_0_), channel_id=1, source_target_pairs={{16,8},{9,17},{0,1},{1,0},{8,9},{17,16},{24,25},{25,24},{18,10},{1... | collective-permute-start | bytes 393224 | tf_op jit(solution)/shard_map/ppermute | solution.py:193
  6.9 9.7 %collective-permute-start.7 = (bf16[1040,256]{1,0:T(8,128)(2,1)S(1)}, bf16[1040,256]{1,0:T(8,128)(2,1)S(1)}, u32[]{:S(2)}, u32[]{:S(2)}) collective-permute-start(bf16[1040,256]{1,0:T(8,128)(2,1)S(1)} %get-tuple-element.11.refs_2_.refs_4_.merged), channel_id=1, source_target_pairs={{0,8},{25,17},{1,0},{8,9},{17,16},{24,25},{9,1},{16,24},{2,10},{27... | collective-permute-start | bytes 1597448 | tf_op jit(solution)/shard_map/ppermute | solution.py:193
  7.7 8.8 %collective-permute-start.6 = (bf16[1040,256]{1,0:T(8,128)(2,1)S(1)}, bf16[1040,256]{1,0:T(8,128)(2,1)S(1)}, u32[]{:S(2)}, u32[]{:S(2)}) collective-permute-start(bf16[1040,256]{1,0:T(8,128)(2,1)S(1)} %get-tuple-element.11.refs_2_.refs_4_.merged), channel_id=1, source_target_pairs={{16,8},{9,17},{0,1},{1,0},{8,9},{17,16},{24,25},{25,24},{18,10},{1... | collective-permute-start | bytes 1597448 | tf_op jit(solution)/shard_map/ppermute | solution.py:193
  10.0 11.4 %collective-permute-start.5 = (bf16[1040,256]{1,0:T(8,128)(2,1)S(1)}, bf16[1040,256]{1,0:T(8,128)(2,1)S(1)}, u32[]{:S(2)}, u32[]{:S(2)}) collective-permute-start(bf16[1040,256]{1,0:T(8,128)(2,1)S(1)} %get-tuple-element.11.refs_2_.refs_4_.merged), channel_id=1, source_target_pairs={{24,8},{1,17},{0,1},{8,9},{17,16},{25,24},{9,0},{16,25},{26,10},{3... | collective-permute-start | bytes 1597448 | tf_op jit(solution)/shard_map/ppermute | solution.py:193
  10.2 4.2 %collective-permute-start.3 = (f32[32,1024]{1,0:T(8,128)S(1)}, f32[32,1024]{1,0:T(8,128)S(1)}, u32[]{:S(2)}, u32[]{:S(2)}) collective-permute-start(f32[32,1024]{1,0:T(8,128)S(1)} %shard_map.86), channel_id=1, source_target_pairs={{8,10},{10,8},{12,14},{14,12},{9,11},{11,9},{13,15},{15,13},{16,18... | collective-permute-start | bytes 393224 | tf_op jit(solution)/shard_map/ppermute | solution.py:203
  14.4 1.4 %collective-permute-start.4 = (f32[32,1024]{1,0:T(8,128)S(1)}, f32[32,1024]{1,0:T(8,128)S(1)}, u32[]{:S(2)}, u32[]{:S(2)}) collective-permute-start(f32[32,1024]{1,0:T(8,128)S(1)} %add.3.refs_0_), channel_id=1, source_target_pairs={{8,12},{10,14},{12,8},{14,10},{9,13},{11,15},{13,9},{15,11},{16,20... | collective-permute-start | bytes 393224 | tf_op jit(solution)/shard_map/ppermute | solution.py:203
  21.4 18.4 %copy-start = (f32[1,256,256]{2,1,0:T(8,128)S(1)}, f32[1,256,256]{2,1,0:T(8,128)}, u32[]{:S(2)}) copy-start(f32[1,256,256]{2,1,0:T(8,128)} %param.9) | copy-start | bytes 786436
  21.4 1.3 %collective-permute-start.10 = (f32[32,1024]{1,0:T(8,128)S(1)}, f32[32,1024]{1,0:T(8,128)S(1)}, u32[]{:S(2)}, u32[]{:S(2)}) collective-permute-start(f32[32,1024]{1,0:T(8,128)S(1)} %shard_map.87.refs_0_), channel_id=1, source_target_pairs={{8,14},{10,12},{12,10},{14,8},{9,15},{11,13},{13,11},{15,9},{16,22... | collective-permute-start | bytes 393224 | tf_op jit(solution)/shard_map/ppermute | solution.py:203
  21.4 1.5 %collective-permute-start.9 = (f32[32,1024]{1,0:T(8,128)S(1)}, f32[32,1024]{1,0:T(8,128)S(1)}, u32[]{:S(2)}, u32[]{:S(2)}) collective-permute-start(f32[32,1024]{1,0:T(8,128)S(1)} %shard_map.87.refs_0_), channel_id=1, source_target_pairs={{8,12},{10,14},{12,8},{14,10},{9,13},{11,15},{13,9},{15,11},{16,20... | collective-permute-start | bytes 393224 | tf_op jit(solution)/shard_map/ppermute | solution.py:203
  21.9 1.3 %collective-permute-start.8 = (f32[32,1024]{1,0:T(8,128)S(1)}, f32[32,1024]{1,0:T(8,128)S(1)}, u32[]{:S(2)}, u32[]{:S(2)}) collective-permute-start(f32[32,1024]{1,0:T(8,128)S(1)} %shard_map.87.refs_0_), channel_id=1, source_target_pairs={{8,10},{10,8},{12,14},{14,12},{9,11},{11,9},{13,15},{15,13},{16,18... | collective-permute-start | bytes 393224 | tf_op jit(solution)/shard_map/ppermute | solution.py:203
  23.3 16.6 %copy-start.1 = (f32[1,256]{1,0:T(1,128)S(1)}, f32[1,256]{1,0:T(1,128)}, u32[]{:S(2)}) copy-start(f32[1,256]{1,0:T(1,128)} %vec_momentum.1) | copy-start | bytes 3076
  23.3 16.5 %collective-permute-start.13 = (bf16[32,1536]{1,0:T(8,128)(2,1)S(1)}, bf16[32,1536]{1,0:T(8,128)(2,1)S(1)}, u32[]{:S(2)}, u32[]{:S(2)}) collective-permute-start(bf16[32,1536]{1,0:T(8,128)(2,1)S(1)} %shard_map.88.refs_0_), channel_id=1, source_target_pairs={{8,0},{17,25},{0,1},{9,8},{16,17},{25,24},{1,9},{24,16},{10,2},{19... | collective-permute-start | bytes 294920 | tf_op jit(solution)/shard_map/ppermute | solution.py:193
  23.5 16.4 %collective-permute-start.12 = (bf16[32,1536]{1,0:T(8,128)(2,1)S(1)}, bf16[32,1536]{1,0:T(8,128)(2,1)S(1)}, u32[]{:S(2)}, u32[]{:S(2)}) collective-permute-start(bf16[32,1536]{1,0:T(8,128)(2,1)S(1)} %shard_map.88.refs_0_), channel_id=1, source_target_pairs={{8,24},{17,1},{1,0},{9,8},{16,17},{24,25},{0,9},{25,16},{10,26},{1... | collective-permute-start | bytes 294920 | tf_op jit(solution)/shard_map/ppermute | solution.py:193
  37.3 2.5 %collective-permute-start.11 = (bf16[32,1536]{1,0:T(8,128)(2,1)S(1)}, bf16[32,1536]{1,0:T(8,128)(2,1)S(1)}, u32[]{:S(2)}, u32[]{:S(2)}) collective-permute-start(bf16[32,1536]{1,0:T(8,128)(2,1)S(1)} %shard_map.88.refs_0_), channel_id=1, source_target_pairs={{8,16},{17,9},{1,0},{0,1},{9,8},{16,17},{25,24},{24,25},{10,18},{1... | collective-permute-start | bytes 294920 | tf_op jit(solution)/shard_map/ppermute | solution.py:193

commit v4 on v3

--- a/solution.py
+++ b/solution.py
@@ -11,7 +11,7 @@
 GATHER_MAX = 8
 PAD = 16
 CHUNKS = 4
-STEP = 8
+STEP = 16
 HIGHEST = lax.Precision.HIGHEST
 F32, BF16 = jnp.float32, jnp.bfloat16
 VMEM = pl.BlockSpec(memory_space=pltpu.VMEM)
@@ -100,27 +100,34 @@
     refs[-1][...] = tree([r[...] for r in refs[:-1]])
 
 
-def factor_kernel(n_p, replicas, last, owner, *refs):
-    @pl.when(lax.axis_index("replica") == owner[0] + lax.axis_index("section") * (owner[-1] - owner[0]))
+def own_block(owner):
+    return lax.axis_index("replica") == owner[0] + lax.axis_index("section") * (owner[-1] - owner[0])
+
+
+def factor_kernel(replicas, owner, *refs):
+    @pl.when(own_block(owner))
     def _():
-        factor_step(refs[:n_p], refs[n_p:-1], refs[-1], replicas, last)
-
-
-def factor_step(p_parts, merged, out, replicas, last):
+        p_sum = tree([p[...] for p in refs[:-1]]) * (1.0 / replicas)
+        inverse = inverse_factor(dot(p_sum, p_sum, 1, 1, HIGHEST))
+        refs[-1][...] = dot(inverse, p_sum, 1, 0, HIGHEST).astype(BF16)
+
+
+def turn_kernel(replicas, last, owner, p_lo, *refs):
+    merged, out = refs[:-1], refs[-1]
     rows, cols = merged[0].shape[0] - PAD, merged[0].shape[1]
-    p_sum = tree([p[...] for p in p_parts]) * (1.0 / replicas)
-    inverse = inverse_factor(dot(p_sum, p_sum, 1, 1, HIGHEST))
-    p_lo = dot(inverse, p_sum, 1, 0, HIGHEST).astype(BF16)
-    q_sum = tree([dot(p_lo, m[:rows, :], 1, 0) for m in merged])
-    q_lo = (q_sum * (1.0 / replicas)).astype(BF16)
-    if not last:
-        out[...] = tree([dot(q_lo, m[:rows, :], 1, 1) for m in merged])
-        return
-    out[:, :rows] = p_lo
-    out[:, rows : rows + cols] = q_lo
-    vec = tree([jnp.sum(m[rows:, :].astype(F32), axis=0, keepdims=True) for m in merged]) * (1.0 / replicas)
-    parts = three_parts(vec)
-    out[:, rows + cols :] = jnp.concatenate([*parts, jnp.zeros((out.shape[0] - 3, cols), F32)], axis=0).astype(BF16)
+
+    @pl.when(own_block(owner))
+    def _():
+        q_sum = tree([dot(p_lo[...], m[:rows, :], 1, 0) for m in merged])
+        q_lo = (q_sum * (1.0 / replicas)).astype(BF16)
+        if not last:
+            out[...] = tree([dot(q_lo, m[:rows, :], 1, 1) for m in merged])
+            return
+        out[:, :rows] = p_lo[...]
+        out[:, rows : rows + cols] = q_lo
+        vec = tree([jnp.sum(m[rows:, :].astype(F32), axis=0, keepdims=True) for m in merged]) * (1.0 / replicas)
+        fill = jnp.zeros((out.shape[0] - 3, cols), F32)
+        out[:, rows + cols :] = jnp.concatenate([*three_parts(vec), fill], axis=0).astype(BF16)
 
 
 def final_kernel(sources, merged, momentum, vec_momentum, *refs):
@@ -192,12 +199,11 @@
     def along(x, perms):
         return [lax.ppermute(x, ("replica", "section"), [(number(a), number(b)) for a, b in p]) for p in perms]
 
-    def across(x, steps):
+    def across(x, steps, busy):
         parts = [x]
         for k in steps:
-            busy = [z for z in range(replicas) if z in owner]
-            idle = [p for p in places if p[0] not in busy]
-            pairs = [((z, i, s), (z, i ^ k, s)) for z in busy for s in range(sections) for i in range(tensors)]
+            idle = [p for p in places if p not in busy]
+            pairs = [((z, i, s), (z, i ^ k, s)) for z, s in busy for i in range(tensors)]
             pairs += [((a[0], i, a[1]), (b[0], i, b[1])) for a, b in completed([], idle) for i in range(tensors)]
             order = [((a[0] * tensors + a[1]) * sections + a[2], (b[0] * tensors + b[1]) * sections + b[2]) for a, b in pairs]
             parts.append(lax.ppermute(x, ("replica", "tensor", "section"), order))
@@ -221,6 +227,7 @@
             pltpu.SemaphoreType.DMA((3, CHUNKS)),
         ],
     )
+    planes = [p for p in places if p[0] in owner]
     p_in = along(p_part, inward)
     m_near = along(merged, inward[:1] + inward[2:])
     p_part = call(add_kernel, [p_shape], p_part, *p_in)[0]
@@ -230,17 +237,20 @@
         last = round_no == ROUNDS - 1
         shape = jax.ShapeDtypeStruct((rank, rows + 2 * cols), BF16) if last else p_shape
         if round_no:
-            parts = across(p_part, range(1, tensors))
+            parts = across(p_part, range(1, tensors), [(owner[s], s) for s in range(sections)])
         else:
             k = 1
             while 2 * k < tensors:
-                p_part = tree(across(p_part, [k]))
+                p_part = tree(across(p_part, [k], planes))
                 k *= 2
-            parts = across(p_part, [k] if k < tensors else [])
+            parts = across(p_part, [k] if k < tensors else [], planes)
+        p_lo = call(
+            functools.partial(factor_kernel, replicas, owner), [jax.ShapeDtypeStruct((rank, rows), BF16)], *parts
+        )[0]
         p_part = call(
-            functools.partial(factor_kernel, len(parts), replicas, last, owner),
+            functools.partial(turn_kernel, replicas, last, owner),
             [shape],
-            *parts,
+            p_lo,
             merged,
             *m_in,
             flops=2 * replicas * work,

time: 41.2 us -> 40 us (0.971)
  starting transfers between devices: 23.6 us -> 22.3 us
    ppermute x9, starting transfers between devices: 19.4 us -> 18.2 us  [along(): lax.ppermute(x, ('replica', 'section'), [(number(a), number(b)) for a, b...]
    pallas_call x5 -> x7, Pallas kernels: 3.15 us -> 3.14 us  [call(): pl.pallas_call(kernel, out_shape=outs, in_specs=in_specs or [VMEM] * len(...]
where the time goes in v4:
time: 40 us; the launch traced here: 39.9 us
  starting transfers between devices  22.3 us (56%)
  waiting for transfers between devices  13.7 us (34%)
  Pallas kernels  3.14 us (8%)
  between operations  0.68 us (2%)
    ppermute x9, starting transfers between devices, along(): lax.ppermute(x, ('replica', 'section'), [(number(a), number(b)) for a, b...  18.2 us
    ppermute x9, waiting for transfers between devices, along(): lax.ppermute(x, ('replica', 'section'), [(number(a), number(b)) for a, b...  10.3 us
    ppermute x5, starting transfers between devices, across(): parts.append(lax.ppermute(x, ('replica', 'tensor', 'section'), order))  4.11 us
    ppermute x5, waiting for transfers between devices, across(): parts.append(lax.ppermute(x, ('replica', 'tensor', 'section'), order))  3.32 us
    pallas_call x7, Pallas kernels, call(): pl.pallas_call(kernel, out_shape=outs, in_specs=in_specs or [VMEM] * len(...  3.14 us
  transfers between devices with their start and end apart: 14, of which 10 were waited for; matrix products, arithmetic and copies ran while one was open for 0% of the time, Pallas kernels for 0%

profile of v4, /device:TPU:0, one launch (start us, length us, event | category | flops | bytes accessed | tf_op | source)
XLA Modules:
  0.0 39.9 jit_solution(14603186201043169027)
XLA Ops:
  0.6 1.9 %shard_map.85 = (bf16[1040,256]{1,0:T(8,128)(2,1)S(1)}, f32[32,1024]{1,0:T(8,128)S(1)}) custom-call(bf16[1024,256]{1,0:T(8,128)(2,1)} %bitcast.10, bf16[1024,256]{1,0:T(8,128)(2,1)} %bitcast.11, f32[32,256]{1,0:T(8,128)} %bitcast.12, f32[1,256]{1,0:T(1,128)} %bitcast.13), custom_call_target="tpu_custom_call" | custom-call | flops 16777216 | bytes 1745920 | tf_op jit(solution)/shard_map/pallas_call | solution.py:27
  2.5 3.1 %collective-permute-start.2 = (f32[32,1024]{1,0:T(8,128)S(1)}, f32[32,1024]{1,0:T(8,128)S(1)}, u32[]{:S(2)}, u32[]{:S(2)}) collective-permute-start(f32[32,1024]{1,0:T(8,128)S(1)} %get-tuple-element.10.refs_0_), channel_id=1, source_target_pairs={{0,8},{25,17},{1,0},{8,9},{17,16},{24,25},{9,1},{16,24},{2,10},{27... | collective-permute-start | bytes 393224 | tf_op jit(solution)/shard_map/ppermute | solution.py:200
  5.6 0.0 collective-permute-start.1
  5.6 1.2 %collective-permute-start = (f32[32,1024]{1,0:T(8,128)S(1)}, f32[32,1024]{1,0:T(8,128)S(1)}, u32[]{:S(2)}, u32[]{:S(2)}) collective-permute-start(f32[32,1024]{1,0:T(8,128)S(1)} %get-tuple-element.10.refs_0_), channel_id=1, source_target_pairs={{16,8},{9,17},{0,1},{1,0},{8,9},{17,16},{24,25},{25,24},{18,10},{1... | collective-permute-start | bytes 393224 | tf_op jit(solution)/shard_map/ppermute | solution.py:200
  6.9 0.9 %collective-permute-start.7 = (bf16[1040,256]{1,0:T(8,128)(2,1)S(1)}, bf16[1040,256]{1,0:T(8,128)(2,1)S(1)}, u32[]{:S(2)}, u32[]{:S(2)}) collective-permute-start(bf16[1040,256]{1,0:T(8,128)(2,1)S(1)} %get-tuple-element.11.refs_0_.merged), channel_id=1, source_target_pairs={{0,8},{25,17},{1,0},{8,9},{17,16},{24,25},{9,1},{16,24},{2,10},{27... | collective-permute-start | bytes 1597448 | tf_op jit(solution)/shard_map/ppermute | solution.py:200
  7.7 0.0 collective-permute-start.6
  7.8 1.3 %collective-permute-done.2.refs_3_ = f32[32,1024]{1,0:T(8,128)S(1)} collective-permute-done((f32[32,1024]{1,0:T(8,128)S(1)}, f32[32,1024]{1,0:T(8,128)S(1)}, u32[]{:S(2)}, u32[]{:S(2)}) %collective-permute-start.2) | collective-permute-done | bytes 131104 | tf_op jit(solution)/shard_map/ppermute | solution.py:200
  9.0 1.0 %collective-permute-done.1.refs_2_ = f32[32,1024]{1,0:T(8,128)S(1)} collective-permute-done((f32[32,1024]{1,0:T(8,128)S(1)}, f32[32,1024]{1,0:T(8,128)S(1)}, u32[]{:S(2)}, u32[]{:S(2)}) %collective-permute-start.1) | collective-permute-done | bytes 131104 | tf_op jit(solution)/shard_map/ppermute | solution.py:200
  10.0 0.0 collective-permute-done.refs_1_
  10.0 0.2 collective-permute-start.5
  10.2 3.2 %collective-permute-start.3 = (f32[32,1024]{1,0:T(8,128)S(1)}, f32[32,1024]{1,0:T(8,128)S(1)}, u32[]{:S(2)}, u32[]{:S(2)}) collective-permute-start(f32[32,1024]{1,0:T(8,128)S(1)} %shard_map.86), channel_id=1, source_target_pairs={{8,10},{10,8},{12,14},{14,12},{9,11},{11,9},{13,15},{15,13},{16,18... | collective-permute-start | bytes 393224 | tf_op jit(solution)/shard_map/ppermute | solution.py:209
  13.4 1.0 %collective-permute-done.3 = f32[32,1024]{1,0:T(8,128)S(1)} collective-permute-done((f32[32,1024]{1,0:T(8,128)S(1)}, f32[32,1024]{1,0:T(8,128)S(1)}, u32[]{:S(2)}, u32[]{:S(2)}) %collective-permute-start.3) | collective-permute-done | bytes 131104 | tf_op jit(solution)/shard_map/ppermute | solution.py:209
  14.4 0.4 %collective-permute-start.4 = (f32[32,1024]{1,0:T(8,128)S(1)}, f32[32,1024]{1,0:T(8,128)S(1)}, u32[]{:S(2)}, u32[]{:S(2)}) collective-permute-start(f32[32,1024]{1,0:T(8,128)S(1)} %add.3.refs_0_), channel_id=1, source_target_pairs={{8,12},{10,14},{12,8},{14,10},{9,13},{11,15},{13,9},{15,11},{16,20... | collective-permute-start | bytes 393224 | tf_op jit(solution)/shard_map/ppermute | solution.py:209
  14.8 1.0 %collective-permute-done.4.refs_1_ = f32[32,1024]{1,0:T(8,128)S(1)} collective-permute-done((f32[32,1024]{1,0:T(8,128)S(1)}, f32[32,1024]{1,0:T(8,128)S(1)}, u32[]{:S(2)}, u32[]{:S(2)}) %collective-permute-start.4) | collective-permute-done | bytes 131104 | tf_op jit(solution)/shard_map/ppermute | solution.py:209
  15.8 0.8 %collective-permute-done.7.refs_3_ = bf16[1040,256]{1,0:T(8,128)(2,1)S(1)} collective-permute-done((bf16[1040,256]{1,0:T(8,128)(2,1)S(1)}, bf16[1040,256]{1,0:T(8,128)(2,1)S(1)}, u32[]{:S(2)}, u32[]{:S(2)}) %collective-permute-start.7) | collective-permute-done | bytes 532512 | tf_op jit(solution)/shard_map/ppermute | solution.py:200
  16.6 0.0 collective-permute-done.6.refs_2_
  16.6 4.8 %collective-permute-done.5.refs_1_ = bf16[1040,256]{1,0:T(8,128)(2,1)S(1)} collective-permute-done((bf16[1040,256]{1,0:T(8,128)(2,1)S(1)}, bf16[1040,256]{1,0:T(8,128)(2,1)S(1)}, u32[]{:S(2)}, u32[]{:S(2)}) %collective-permute-start.5) | collective-permute-done | bytes 532512 | tf_op jit(solution)/shard_map/ppermute | solution.py:200
  21.4 0.0 collective-permute-start.10
  21.4 0.5 %collective-permute-start.9 = (f32[32,1024]{1,0:T(8,128)S(1)}, f32[32,1024]{1,0:T(8,128)S(1)}, u32[]{:S(2)}, u32[]{:S(2)}) collective-permute-start(f32[32,1024]{1,0:T(8,128)S(1)} %shard_map.88.refs_0_), channel_id=1, source_target_pairs={{8,12},{10,14},{12,8},{14,10},{17,21},{19,23},{21,17},{23,19},{0,1... | collective-permute-start | bytes 393224 | tf_op jit(solution)/shard_map/ppermute | solution.py:209
  21.9 0.0 collective-permute-start.8
  21.9 0.8 %collective-permute-done.10.refs_3_ = f32[32,1024]{1,0:T(8,128)S(1)} collective-permute-done((f32[32,1024]{1,0:T(8,128)S(1)}, f32[32,1024]{1,0:T(8,128)S(1)}, u32[]{:S(2)}, u32[]{:S(2)}) %collective-permute-start.10) | collective-permute-done | bytes 131104 | tf_op jit(solution)/shard_map/ppermute | solution.py:209
  22.8 0.2 collective-permute-done.9.refs_2_
  22.9 0.3 collective-permute-done.8.refs_1_
  23.3 0.0 copy-start
  23.3 0.0 copy-start.1
  23.3 0.2 collective-permute-start.13
  23.5 12.7 %collective-permute-start.12 = (bf16[32,1536]{1,0:T(8,128)(2,1)S(1)}, bf16[32,1536]{1,0:T(8,128)(2,1)S(1)}, u32[]{:S(2)}, u32[]{:S(2)}) collective-permute-start(bf16[32,1536]{1,0:T(8,128)(2,1)S(1)} %shard_map.90.refs_0_), channel_id=1, source_target_pairs={{8,24},{17,1},{1,0},{9,8},{16,17},{24,25},{0,9},{25,16},{10,26},{1... | collective-permute-start | bytes 294920 | tf_op jit(solution)/shard_map/ppermute | solution.py:200
  36.1 0.0 collective-permute-start.11
  36.1 2.5 %collective-permute-done.13.refs_3_ = bf16[32,1536]{1,0:T(8,128)(2,1)S(1)} collective-permute-done((bf16[32,1536]{1,0:T(8,128)(2,1)S(1)}, bf16[32,1536]{1,0:T(8,128)(2,1)S(1)}, u32[]{:S(2)}, u32[]{:S(2)}) %collective-permute-start.13) | collective-permute-done | bytes 98336 | tf_op jit(solution)/shard_map/ppermute | solution.py:200
  38.6 0.0 collective-permute-done.12.refs_2_
  38.6 0.0 collective-permute-done.11.refs_1_
  38.6 0.0 copy-done
  38.6 0.0 copy-done.1
  38.6 1.2 %shard_map.91 = (bf16[1024,256]{1,0:T(8,128)(2,1)}, f32[256,256]{1,0:T(8,128)}, f32[1,256]{1,0:T(1,128)}) custom-call(bf16[1040,256]{1,0:T(8,128)(2,1)S(1)} %get-tuple-element.11.refs_0_.merged, f32[256,256]{1,0:T(8,128)S(1)} %bitcast.9, f32[1,256]{1,0:T(1,128)S(1)} %copy-done.1, bf16[32,1536]{1,0:T(8,128)(2,1)S(1)} %shard_map.90.refs_0_, ...), custom_call_target="tpu_custom_call" | custom-call | flops 33554432 | bytes 1976320 | tf_op jit(solution)/shard_map/pallas_call | solution.py:27
  (6 shorter events, 0.0 us)
Async XLA Ops:
  2.5 6.5 %collective-permute-start.2 = (f32[32,1024]{1,0:T(8,128)S(1)}, f32[32,1024]{1,0:T(8,128)S(1)}, u32[]{:S(2)}, u32[]{:S(2)}) collective-permute-start(f32[32,1024]{1,0:T(8,128)S(1)} %get-tuple-element.10.refs_0_), channel_id=1, source_target_pairs={{0,8},{25,17},{1,0},{8,9},{17,16},{24,25},{9,1},{16,24},{2,10},{27... | collective-permute-start | bytes 393224 | tf_op jit(solution)/shard_map/ppermute | solution.py:200
  5.6 4.4 %collective-permute-start.1 = (f32[32,1024]{1,0:T(8,128)S(1)}, f32[32,1024]{1,0:T(8,128)S(1)}, u32[]{:S(2)}, u32[]{:S(2)}) collective-permute-start(f32[32,1024]{1,0:T(8,128)S(1)} %get-tuple-element.10.refs_0_), channel_id=1, source_target_pairs={{24,8},{1,17},{0,1},{8,9},{17,16},{25,24},{9,0},{16,25},{26,10},{3... | collective-permute-start | bytes 393224 | tf_op jit(solution)/shard_map/ppermute | solution.py:200
  5.6 4.4 %collective-permute-start = (f32[32,1024]{1,0:T(8,128)S(1)}, f32[32,1024]{1,0:T(8,128)S(1)}, u32[]{:S(2)}, u32[]{:S(2)}) collective-permute-start(f32[32,1024]{1,0:T(8,128)S(1)} %get-tuple-element.10.refs_0_), channel_id=1, source_target_pairs={{16,8},{9,17},{0,1},{1,0},{8,9},{17,16},{24,25},{25,24},{18,10},{1... | collective-permute-start | bytes 393224 | tf_op jit(solution)/shard_map/ppermute | solution.py:200
  6.9 9.7 %collective-permute-start.7 = (bf16[1040,256]{1,0:T(8,128)(2,1)S(1)}, bf16[1040,256]{1,0:T(8,128)(2,1)S(1)}, u32[]{:S(2)}, u32[]{:S(2)}) collective-permute-start(bf16[1040,256]{1,0:T(8,128)(2,1)S(1)} %get-tuple-element.11.refs_0_.merged), channel_id=1, source_target_pairs={{0,8},{25,17},{1,0},{8,9},{17,16},{24,25},{9,1},{16,24},{2,10},{27... | collective-permute-start | bytes 1597448 | tf_op jit(solution)/shard_map/ppermute | solution.py:200
  7.7 8.8 %collective-permute-start.6 = (bf16[1040,256]{1,0:T(8,128)(2,1)S(1)}, bf16[1040,256]{1,0:T(8,128)(2,1)S(1)}, u32[]{:S(2)}, u32[]{:S(2)}) collective-permute-start(bf16[1040,256]{1,0:T(8,128)(2,1)S(1)} %get-tuple-element.11.refs_0_.merged), channel_id=1, source_target_pairs={{16,8},{9,17},{0,1},{1,0},{8,9},{17,16},{24,25},{25,24},{18,10},{1... | collective-permute-start | bytes 1597448 | tf_op jit(solution)/shard_map/ppermute | solution.py:200
  10.0 11.4 %collective-permute-start.5 = (bf16[1040,256]{1,0:T(8,128)(2,1)S(1)}, bf16[1040,256]{1,0:T(8,128)(2,1)S(1)}, u32[]{:S(2)}, u32[]{:S(2)}) collective-permute-start(bf16[1040,256]{1,0:T(8,128)(2,1)S(1)} %get-tuple-element.11.refs_0_.merged), channel_id=1, source_target_pairs={{24,8},{1,17},{0,1},{8,9},{17,16},{25,24},{9,0},{16,25},{26,10},{3... | collective-permute-start | bytes 1597448 | tf_op jit(solution)/shard_map/ppermute | solution.py:200
  10.2 4.2 %collective-permute-start.3 = (f32[32,1024]{1,0:T(8,128)S(1)}, f32[32,1024]{1,0:T(8,128)S(1)}, u32[]{:S(2)}, u32[]{:S(2)}) collective-permute-start(f32[32,1024]{1,0:T(8,128)S(1)} %shard_map.86), channel_id=1, source_target_pairs={{8,10},{10,8},{12,14},{14,12},{9,11},{11,9},{13,15},{15,13},{16,18... | collective-permute-start | bytes 393224 | tf_op jit(solution)/shard_map/ppermute | solution.py:209
  14.4 1.4 %collective-permute-start.4 = (f32[32,1024]{1,0:T(8,128)S(1)}, f32[32,1024]{1,0:T(8,128)S(1)}, u32[]{:S(2)}, u32[]{:S(2)}) collective-permute-start(f32[32,1024]{1,0:T(8,128)S(1)} %add.3.refs_0_), channel_id=1, source_target_pairs={{8,12},{10,14},{12,8},{14,10},{9,13},{11,15},{13,9},{15,11},{16,20... | collective-permute-start | bytes 393224 | tf_op jit(solution)/shard_map/ppermute | solution.py:209
  21.4 1.3 %collective-permute-start.10 = (f32[32,1024]{1,0:T(8,128)S(1)}, f32[32,1024]{1,0:T(8,128)S(1)}, u32[]{:S(2)}, u32[]{:S(2)}) collective-permute-start(f32[32,1024]{1,0:T(8,128)S(1)} %shard_map.88.refs_0_), channel_id=1, source_target_pairs={{8,14},{10,12},{12,10},{14,8},{17,23},{19,21},{21,19},{23,17},{0,1... | collective-permute-start | bytes 393224 | tf_op jit(solution)/shard_map/ppermute | solution.py:209
  21.4 1.5 %collective-permute-start.9 = (f32[32,1024]{1,0:T(8,128)S(1)}, f32[32,1024]{1,0:T(8,128)S(1)}, u32[]{:S(2)}, u32[]{:S(2)}) collective-permute-start(f32[32,1024]{1,0:T(8,128)S(1)} %shard_map.88.refs_0_), channel_id=1, source_target_pairs={{8,12},{10,14},{12,8},{14,10},{17,21},{19,23},{21,17},{23,19},{0,1... | collective-permute-start | bytes 393224 | tf_op jit(solution)/shard_map/ppermute | solution.py:209
  21.9 1.3 %collective-permute-start.8 = (f32[32,1024]{1,0:T(8,128)S(1)}, f32[32,1024]{1,0:T(8,128)S(1)}, u32[]{:S(2)}, u32[]{:S(2)}) collective-permute-start(f32[32,1024]{1,0:T(8,128)S(1)} %shard_map.88.refs_0_), channel_id=1, source_target_pairs={{8,10},{10,8},{12,14},{14,12},{17,19},{19,17},{21,23},{23,21},{0,1... | collective-permute-start | bytes 393224 | tf_op jit(solution)/shard_map/ppermute | solution.py:209
  23.3 15.3 %copy-start = (f32[1,256,256]{2,1,0:T(8,128)S(1)}, f32[1,256,256]{2,1,0:T(8,128)}, u32[]{:S(2)}) copy-start(f32[1,256,256]{2,1,0:T(8,128)} %param.9) | copy-start | bytes 786436
  23.3 15.3 %copy-start.1 = (f32[1,256]{1,0:T(1,128)S(1)}, f32[1,256]{1,0:T(1,128)}, u32[]{:S(2)}) copy-start(f32[1,256]{1,0:T(1,128)} %vec_momentum.1) | copy-start | bytes 3076
  23.3 15.3 %collective-permute-start.13 = (bf16[32,1536]{1,0:T(8,128)(2,1)S(1)}, bf16[32,1536]{1,0:T(8,128)(2,1)S(1)}, u32[]{:S(2)}, u32[]{:S(2)}) collective-permute-start(bf16[32,1536]{1,0:T(8,128)(2,1)S(1)} %shard_map.90.refs_0_), channel_id=1, source_target_pairs={{8,0},{17,25},{0,1},{9,8},{16,17},{25,24},{1,9},{24,16},{10,2},{19... | collective-permute-start | bytes 294920 | tf_op jit(solution)/shard_map/ppermute | solution.py:200
  23.5 15.1 %collective-permute-start.12 = (bf16[32,1536]{1,0:T(8,128)(2,1)S(1)}, bf16[32,1536]{1,0:T(8,128)(2,1)S(1)}, u32[]{:S(2)}, u32[]{:S(2)}) collective-permute-start(bf16[32,1536]{1,0:T(8,128)(2,1)S(1)} %shard_map.90.refs_0_), channel_id=1, source_target_pairs={{8,24},{17,1},{1,0},{9,8},{16,17},{24,25},{0,9},{25,16},{10,26},{1... | collective-permute-start | bytes 294920 | tf_op jit(solution)/shard_map/ppermute | solution.py:200
  36.1 2.5 %collective-permute-start.11 = (bf16[32,1536]{1,0:T(8,128)(2,1)S(1)}, bf16[32,1536]{1,0:T(8,128)(2,1)S(1)}, u32[]{:S(2)}, u32[]{:S(2)}) collective-permute-start(bf16[32,1536]{1,0:T(8,128)(2,1)S(1)} %shard_map.90.refs_0_), channel_id=1, source_target_pairs={{8,16},{17,9},{1,0},{0,1},{9,8},{16,17},{25,24},{24,25},{10,18},{1... | collective-permute-start | bytes 294920 | tf_op jit(solution)/shard_map/ppermute | solution.py:200

commit v5 on v4

--- a/solution.py
+++ b/solution.py
@@ -8,9 +8,9 @@
 from jax.sharding import PartitionSpec as P
 
 ROUNDS = 2
-GATHER_MAX = 8
+LANES = 128
 PAD = 16
-CHUNKS = 4
+CHUNKS_IN, CHUNKS_OUT = 2, 4
 STEP = 16
 HIGHEST = lax.Precision.HIGHEST
 F32, BF16 = jnp.float32, jnp.bfloat16
@@ -71,14 +71,14 @@
 
 def merge_kernel(grads, errors, q, vec, merged, p_part, grads_in, errors_in, q_in, vec_in, sems):
     rows, cols = grads.shape
-    step = rows // CHUNKS
+    step = rows // CHUNKS_IN
     small = [pltpu.make_async_copy(a, b, sems.at[2, i]) for i, (a, b) in enumerate([(q, q_in), (vec, vec_in)])]
     large = [
         [
             pltpu.make_async_copy(a.at[pl.ds(i * step, step)], b.at[pl.ds(i * step, step)], sems.at[j, i])
             for j, (a, b) in enumerate([(grads, grads_in), (errors, errors_in)])
         ]
-        for i in range(CHUNKS)
+        for i in range(CHUNKS_IN)
     ]
     for copy in small + sum(large, []):
         copy.start()
@@ -87,7 +87,7 @@
     q_lo = q_in[...].astype(BF16)
     parts = three_parts(vec_in[...])
     merged[rows:, :] = jnp.concatenate([*parts, jnp.zeros((PAD - 3, cols), F32)], axis=0).astype(BF16)
-    for i in range(CHUNKS):
+    for i in range(CHUNKS_IN):
         for copy in large[i]:
             copy.wait()
         here = slice(i * step, (i + 1) * step)
@@ -112,57 +112,78 @@
         refs[-1][...] = dot(inverse, p_sum, 1, 0, HIGHEST).astype(BF16)
 
 
-def turn_kernel(replicas, last, owner, p_lo, *refs):
-    merged, out = refs[:-1], refs[-1]
-    rows, cols = merged[0].shape[0] - PAD, merged[0].shape[1]
+def product(left, mean, here, axis):
+    high, low = mean
+    return dot(left, high[here, :], 1, axis) + dot(left, low[here, :], 1, axis)
+
+
+def turn_kernel(replicas, owner, p_lo, *refs):
+    *merged, high, low, vec_mean, out = refs
+    rows = high.shape[0]
 
     @pl.when(own_block(owner))
     def _():
-        q_sum = tree([dot(p_lo[...], m[:rows, :], 1, 0) for m in merged])
-        q_lo = (q_sum * (1.0 / replicas)).astype(BF16)
-        if not last:
-            out[...] = tree([dot(q_lo, m[:rows, :], 1, 1) for m in merged])
-            return
+        total = tree([m[:rows, :].astype(F32) for m in merged]) * (1.0 / replicas)
+        top = total.astype(BF16)
+        high[...] = top
+        low[...] = (total - top.astype(F32)).astype(BF16)
+        vec_mean[...] = tree([jnp.sum(m[rows:, :].astype(F32), axis=0, keepdims=True) for m in merged]) * (1.0 / replicas)
+        everything = slice(0, rows)
+        q_lo = product(p_lo[...], (high, low), everything, 0).astype(BF16)
+        out[...] = product(q_lo, (high, low), everything, 1)
+
+
+def last_kernel(owner, p_lo, high, low, vec_mean, out):
+    rows, cols = high.shape
+
+    @pl.when(own_block(owner))
+    def _():
+        q_lo = product(p_lo[...], (high, low), slice(0, rows), 0).astype(BF16)
+        vec = vec_mean[...]
+        parts = [part[:, i : i + LANES] for part in three_parts(vec) for i in range(0, cols, LANES)]
+        fill = jnp.zeros((out.shape[0] - len(parts), LANES), F32)
         out[:, :rows] = p_lo[...]
         out[:, rows : rows + cols] = q_lo
-        vec = tree([jnp.sum(m[rows:, :].astype(F32), axis=0, keepdims=True) for m in merged]) * (1.0 / replicas)
-        fill = jnp.zeros((out.shape[0] - 3, cols), F32)
-        out[:, rows + cols :] = jnp.concatenate([*three_parts(vec), fill], axis=0).astype(BF16)
+        out[:, rows + cols :] = jnp.concatenate([*parts, fill], axis=0).astype(BF16)
 
 
 def final_kernel(sources, merged, momentum, vec_momentum, *refs):
     packs = refs[:-9]
-    new_errors, new_momentum, new_vec, pack, p_rows, errors_out, momentum_out, vec_out, sems = refs[-9:]
+    new_errors, new_momentum, new_vec, rest, p_rows, errors_out, momentum_out, vec_out, sems = refs[-9:]
     rows, cols = new_errors.shape
     own_rows = momentum.shape[0]
     z, s = lax.axis_index("replica"), lax.axis_index("section")
     came = sum(
         jnp.where((z == row[j]) & (s == i), j + 1, 0) for i, row in enumerate(sources) for j in range(len(row))
     )
-    for i, candidate in enumerate(packs):
+    for i, pack in enumerate(packs):
 
         @pl.when(came == i)
-        def _(candidate=candidate):
-            pack[...] = candidate[...]
-
-    p_rows[...] = pack[:, :rows].T
-    q_lo = pack[:, rows : rows + cols]
+        def _(pack=pack):
+            p_rows[...] = pack[:, :rows].T
+            rest[...] = pack[:, rows:]
+
+    q_lo = rest[:, :cols]
     copies = []
-    step = rows // CHUNKS
-    for i in range(CHUNKS):
+    step = rows // CHUNKS_OUT
+    for i in range(CHUNKS_OUT):
         here = pl.ds(i * step, step)
         approx = dot(p_rows[here, :], q_lo, 1, 0)
         errors_out[here, :] = (merged[here, :].astype(F32) - approx).astype(BF16)
         copies.append(pltpu.make_async_copy(errors_out.at[here], new_errors.at[here], sems.at[i]))
         copies[-1].start()
-    first = pl.multiple_of(z * own_rows, own_rows)
-    mine = dot(p_rows[pl.ds(first, own_rows), :], q_lo, 1, 0)
+    start = pl.multiple_of(z * own_rows, own_rows)
+    mine = dot(p_rows[pl.ds(start, own_rows), :], q_lo, 1, 0)
     momentum_out[...] = 0.9 * momentum[...] + mine
-    copies.append(pltpu.make_async_copy(momentum_out, new_momentum, sems.at[CHUNKS]))
+    copies.append(pltpu.make_async_copy(momentum_out, new_momentum, sems.at[CHUNKS_OUT]))
     copies[-1].start()
-    vec = jnp.sum(pack[:, rows + cols :].astype(F32), axis=0, keepdims=True)
-    vec_out[...] = 0.9 * vec_momentum[...] + vec
-    copies.append(pltpu.make_async_copy(vec_out, new_vec, sems.at[CHUNKS + 1]))
+    parts = rest[:, cols:].astype(F32)
+    pieces = cols // LANES
+    for i in range(pieces):
+        vec = parts[i : i + 1] + parts[pieces + i : pieces + i + 1] + parts[2 * pieces + i : 2 * pieces + i + 1]
+        here = slice(i * LANES, (i + 1) * LANES)
+        vec_out[:, here] = 0.9 * vec_momentum[:, here] + vec
+    copies.append(pltpu.make_async_copy(vec_out, new_vec, sems.at[CHUNKS_OUT + 1]))
     copies[-1].start()
     for copy in copies:
         copy.wait()
@@ -224,7 +245,7 @@
             pltpu.VMEM(block, BF16),
             pltpu.VMEM((rank, cols), F32),
             pltpu.VMEM((1, cols), F32),
-            pltpu.SemaphoreType.DMA((3, CHUNKS)),
+            pltpu.SemaphoreType.DMA((3, CHUNKS_IN)),
         ],
     )
     planes = [p for p in places if p[0] in owner]
@@ -233,29 +254,32 @@
     p_part = call(add_kernel, [p_shape], p_part, *p_in)[0]
     held = lax.optimization_barrier((merged, p_part))[0]
     m_in = along(held, inward[1:2]) + m_near
-    for round_no in range(ROUNDS):
-        last = round_no == ROUNDS - 1
-        shape = jax.ShapeDtypeStruct((rank, rows + 2 * cols), BF16) if last else p_shape
-        if round_no:
-            parts = across(p_part, range(1, tensors), [(owner[s], s) for s in range(sections)])
-        else:
-            k = 1
-            while 2 * k < tensors:
-                p_part = tree(across(p_part, [k], planes))
-                k *= 2
-            parts = across(p_part, [k] if k < tensors else [], planes)
-        p_lo = call(
-            functools.partial(factor_kernel, replicas, owner), [jax.ShapeDtypeStruct((rank, rows), BF16)], *parts
-        )[0]
-        p_part = call(
-            functools.partial(turn_kernel, replicas, last, owner),
-            [shape],
+    k = 1
+    while 2 * k < tensors:
+        p_part = tree(across(p_part, [k], planes))
+        k *= 2
+    parts = across(p_part, [k] if k < tensors else [], planes)
+    lo_shape = jax.ShapeDtypeStruct((rank, rows), BF16)
+    for _ in range(ROUNDS - 1):
+        p_lo = call(functools.partial(factor_kernel, replicas, owner), [lo_shape], *parts)[0]
+        *mean, p_part = call(
+            functools.partial(turn_kernel, replicas, owner),
+            [jax.ShapeDtypeStruct(block, BF16)] * 2 + [jax.ShapeDtypeStruct((1, cols), F32), p_shape],
             p_lo,
             merged,
             *m_in,
-            flops=2 * replicas * work,
-        )[0]
-    received = along(p_part, outward)
+            flops=4 * work,
+        )
+        parts = across(p_part, range(1, tensors), [(owner[s], s) for s in range(sections)])
+    p_lo = call(functools.partial(factor_kernel, replicas, owner), [lo_shape], *parts)[0]
+    whole = call(
+        functools.partial(last_kernel, owner),
+        [jax.ShapeDtypeStruct((rank, rows + cols + LANES), BF16)],
+        p_lo,
+        *mean,
+        flops=2 * work,
+    )[0]
+    received = along(whole, outward)
     new_errors, new_momentum, new_vec = call(
         functools.partial(final_kernel, sources),
         [
@@ -266,17 +290,17 @@
         merged,
         momentum[0],
         vec_momentum,
-        p_part,
+        whole,
         *received,
         flops=2 * work,
         out_specs=[HBM] * 3,
         scratch=[
-            pltpu.VMEM(p_part.shape, BF16),
+            pltpu.VMEM((rank, cols + LANES), BF16),
             pltpu.VMEM((rows, rank), BF16),
             pltpu.VMEM(block, BF16),
             pltpu.VMEM(momentum.shape[1:], F32),
             pltpu.VMEM((1, cols), F32),
-            pltpu.SemaphoreType.DMA((CHUNKS + 2,)),
+            pltpu.SemaphoreType.DMA((CHUNKS_OUT + 2,)),
         ],
     )
     return new_errors[None, None], new_momentum[None], new_vec
@@ -304,7 +328,7 @@
 
 
 def solution(mesh):
-    few = mesh.shape["replica"] <= GATHER_MAX
+    few = mesh.shape["replica"] == 4
     wide = P("replica", "section", None, "tensor")
     outs = (wide, P("section", "replica", "tensor"), P("section", "tensor"))
     return jax.shard_map(

time: 40 us -> 39 us (0.975)
  starting transfers between devices: 22.3 us -> 21.8 us
    ppermute x9, starting transfers between devices: 18.2 us -> 17.7 us  [along(): lax.ppermute(x, ('replica', 'section'), [(number(a), number(b)) for a, b...]
where the time goes in v5:
time: 39 us; the launch traced here: 38.9 us
  starting transfers between devices  21.8 us (56%)
  waiting for transfers between devices  13.6 us (35%)
  Pallas kernels  2.82 us (7%)
  between operations  0.68 us (2%)
    ppermute x9, starting transfers between devices, along(): lax.ppermute(x, ('replica', 'section'), [(number(a), number(b)) for a, b...  17.7 us
    ppermute x9, waiting for transfers between devices, along(): lax.ppermute(x, ('replica', 'section'), [(number(a), number(b)) for a, b...  10.3 us
    ppermute x5, starting transfers between devices, across(): parts.append(lax.ppermute(x, ('replica', 'tensor', 'section'), order))  4.11 us
    ppermute x5, waiting for transfers between devices, across(): parts.append(lax.ppermute(x, ('replica', 'tensor', 'section'), order))  3.32 us
    pallas_call x7, Pallas kernels, call(): pl.pallas_call(kernel, out_shape=outs, in_specs=in_specs or [VMEM] * len(...  2.82 us
  transfers between devices with their start and end apart: 14, of which 10 were waited for; matrix products, arithmetic and copies ran while one was open for 0% of the time, Pallas kernels for 0%

profile of v5, /device:TPU:0, one launch (start us, length us, event | category | flops | bytes accessed | tf_op | source)
XLA Modules:
  0.0 38.9 jit_solution(13064363486797595065)
XLA Ops:
  0.6 1.5 %shard_map.85 = (bf16[1040,256]{1,0:T(8,128)(2,1)S(1)}, f32[32,1024]{1,0:T(8,128)S(1)}) custom-call(bf16[1024,256]{1,0:T(8,128)(2,1)} %bitcast.10, bf16[1024,256]{1,0:T(8,128)(2,1)} %bitcast.11, f32[32,256]{1,0:T(8,128)} %bitcast.12, f32[1,256]{1,0:T(1,128)} %bitcast.13), custom_call_target="tpu_custom_call" | custom-call | flops 16777216 | bytes 1745920 | tf_op jit(solution)/shard_map/pallas_call | solution.py:27
  2.1 3.1 %collective-permute-start.2 = (f32[32,1024]{1,0:T(8,128)S(1)}, f32[32,1024]{1,0:T(8,128)S(1)}, u32[]{:S(2)}, u32[]{:S(2)}) collective-permute-start(f32[32,1024]{1,0:T(8,128)S(1)} %get-tuple-element.14.refs_0_), channel_id=1, source_target_pairs={{0,8},{25,17},{1,0},{8,9},{17,16},{24,25},{9,1},{16,24},{2,10},{27... | collective-permute-start | bytes 393224 | tf_op jit(solution)/shard_map/ppermute | solution.py:221
  5.2 0.0 collective-permute-start.1
  5.2 1.2 %collective-permute-start = (f32[32,1024]{1,0:T(8,128)S(1)}, f32[32,1024]{1,0:T(8,128)S(1)}, u32[]{:S(2)}, u32[]{:S(2)}) collective-permute-start(f32[32,1024]{1,0:T(8,128)S(1)} %get-tuple-element.14.refs_0_), channel_id=1, source_target_pairs={{16,8},{9,17},{0,1},{1,0},{8,9},{17,16},{24,25},{25,24},{18,10},{1... | collective-permute-start | bytes 393224 | tf_op jit(solution)/shard_map/ppermute | solution.py:221
  6.5 0.9 %collective-permute-start.7 = (bf16[1040,256]{1,0:T(8,128)(2,1)S(1)}, bf16[1040,256]{1,0:T(8,128)(2,1)S(1)}, u32[]{:S(2)}, u32[]{:S(2)}) collective-permute-start(bf16[1040,256]{1,0:T(8,128)(2,1)S(1)} %get-tuple-element.15.refs_0_.merged), channel_id=1, source_target_pairs={{0,8},{25,17},{1,0},{8,9},{17,16},{24,25},{9,1},{16,24},{2,10},{27... | collective-permute-start | bytes 1597448 | tf_op jit(solution)/shard_map/ppermute | solution.py:221
  7.4 0.0 collective-permute-start.6
  7.4 1.3 %collective-permute-done.2.refs_3_ = f32[32,1024]{1,0:T(8,128)S(1)} collective-permute-done((f32[32,1024]{1,0:T(8,128)S(1)}, f32[32,1024]{1,0:T(8,128)S(1)}, u32[]{:S(2)}, u32[]{:S(2)}) %collective-permute-start.2) | collective-permute-done | bytes 131104 | tf_op jit(solution)/shard_map/ppermute | solution.py:221
  8.6 1.0 %collective-permute-done.1.refs_2_ = f32[32,1024]{1,0:T(8,128)S(1)} collective-permute-done((f32[32,1024]{1,0:T(8,128)S(1)}, f32[32,1024]{1,0:T(8,128)S(1)}, u32[]{:S(2)}, u32[]{:S(2)}) %collective-permute-start.1) | collective-permute-done | bytes 131104 | tf_op jit(solution)/shard_map/ppermute | solution.py:221
  9.6 0.0 collective-permute-done.refs_1_
  9.7 0.2 collective-permute-start.5
  9.8 3.2 %collective-permute-start.3 = (f32[32,1024]{1,0:T(8,128)S(1)}, f32[32,1024]{1,0:T(8,128)S(1)}, u32[]{:S(2)}, u32[]{:S(2)}) collective-permute-start(f32[32,1024]{1,0:T(8,128)S(1)} %shard_map.86), channel_id=1, source_target_pairs={{8,10},{10,8},{12,14},{14,12},{9,11},{11,9},{13,15},{15,13},{16,18... | collective-permute-start | bytes 393224 | tf_op jit(solution)/shard_map/ppermute | solution.py:230
  13.0 1.0 %collective-permute-done.3 = f32[32,1024]{1,0:T(8,128)S(1)} collective-permute-done((f32[32,1024]{1,0:T(8,128)S(1)}, f32[32,1024]{1,0:T(8,128)S(1)}, u32[]{:S(2)}, u32[]{:S(2)}) %collective-permute-start.3) | collective-permute-done | bytes 131104 | tf_op jit(solution)/shard_map/ppermute | solution.py:230
  14.0 0.4 %collective-permute-start.4 = (f32[32,1024]{1,0:T(8,128)S(1)}, f32[32,1024]{1,0:T(8,128)S(1)}, u32[]{:S(2)}, u32[]{:S(2)}) collective-permute-start(f32[32,1024]{1,0:T(8,128)S(1)} %add.3.refs_0_), channel_id=1, source_target_pairs={{8,12},{10,14},{12,8},{14,10},{9,13},{11,15},{13,9},{15,11},{16,20... | collective-permute-start | bytes 393224 | tf_op jit(solution)/shard_map/ppermute | solution.py:230
  14.4 1.0 %collective-permute-done.4.refs_1_ = f32[32,1024]{1,0:T(8,128)S(1)} collective-permute-done((f32[32,1024]{1,0:T(8,128)S(1)}, f32[32,1024]{1,0:T(8,128)S(1)}, u32[]{:S(2)}, u32[]{:S(2)}) %collective-permute-start.4) | collective-permute-done | bytes 131104 | tf_op jit(solution)/shard_map/ppermute | solution.py:230
  15.4 0.8 %collective-permute-done.7.refs_3_ = bf16[1040,256]{1,0:T(8,128)(2,1)S(1)} collective-permute-done((bf16[1040,256]{1,0:T(8,128)(2,1)S(1)}, bf16[1040,256]{1,0:T(8,128)(2,1)S(1)}, u32[]{:S(2)}, u32[]{:S(2)}) %collective-permute-start.7) | collective-permute-done | bytes 532512 | tf_op jit(solution)/shard_map/ppermute | solution.py:221
  16.2 0.0 collective-permute-done.6.refs_2_
  16.2 4.8 %collective-permute-done.5.refs_1_ = bf16[1040,256]{1,0:T(8,128)(2,1)S(1)} collective-permute-done((bf16[1040,256]{1,0:T(8,128)(2,1)S(1)}, bf16[1040,256]{1,0:T(8,128)(2,1)S(1)}, u32[]{:S(2)}, u32[]{:S(2)}) %collective-permute-start.5) | collective-permute-done | bytes 532512 | tf_op jit(solution)/shard_map/ppermute | solution.py:221
  21.0 0.0 collective-permute-start.10
  21.0 0.5 %collective-permute-start.9 = (f32[32,1024]{1,0:T(8,128)S(1)}, f32[32,1024]{1,0:T(8,128)S(1)}, u32[]{:S(2)}, u32[]{:S(2)}) collective-permute-start(f32[32,1024]{1,0:T(8,128)S(1)} %get-tuple-element.16.refs_0_), channel_id=1, source_target_pairs={{8,12},{10,14},{12,8},{14,10},{17,21},{19,23},{21,17},{23,19},{0,1... | collective-permute-start | bytes 393224 | tf_op jit(solution)/shard_map/ppermute | solution.py:230
  21.5 0.0 collective-permute-start.8
  21.6 0.8 %collective-permute-done.10.refs_3_ = f32[32,1024]{1,0:T(8,128)S(1)} collective-permute-done((f32[32,1024]{1,0:T(8,128)S(1)}, f32[32,1024]{1,0:T(8,128)S(1)}, u32[]{:S(2)}, u32[]{:S(2)}) %collective-permute-start.10) | collective-permute-done | bytes 131104 | tf_op jit(solution)/shard_map/ppermute | solution.py:230
  22.4 0.2 collective-permute-done.9.refs_2_
  22.6 0.3 collective-permute-done.8.refs_1_
  22.9 0.0 copy-start
  22.9 0.0 copy-start.1
  22.9 0.2 collective-permute-start.13
  23.1 12.1 %collective-permute-start.12 = (bf16[32,1408]{1,0:T(8,128)(2,1)S(1)}, bf16[32,1408]{1,0:T(8,128)(2,1)S(1)}, u32[]{:S(2)}, u32[]{:S(2)}) collective-permute-start(bf16[32,1408]{1,0:T(8,128)(2,1)S(1)} %shard_map.90.refs_0_), channel_id=1, source_target_pairs={{8,24},{17,1},{1,0},{9,8},{16,17},{24,25},{0,9},{25,16},{10,26},{1... | collective-permute-start | bytes 270344 | tf_op jit(solution)/shard_map/ppermute | solution.py:221
  35.2 0.0 collective-permute-start.11
  35.2 2.4 %collective-permute-done.13.refs_3_ = bf16[32,1408]{1,0:T(8,128)(2,1)S(1)} collective-permute-done((bf16[32,1408]{1,0:T(8,128)(2,1)S(1)}, bf16[32,1408]{1,0:T(8,128)(2,1)S(1)}, u32[]{:S(2)}, u32[]{:S(2)}) %collective-permute-start.13) | collective-permute-done | bytes 90144 | tf_op jit(solution)/shard_map/ppermute | solution.py:221
  37.6 0.0 collective-permute-done.12.refs_2_
  37.6 0.0 collective-permute-done.11.refs_1_
  37.6 0.0 copy-done
  37.6 0.0 copy-done.1
  37.6 1.3 %shard_map.91 = (bf16[1024,256]{1,0:T(8,128)(2,1)}, f32[256,256]{1,0:T(8,128)}, f32[1,256]{1,0:T(1,128)}) custom-call(bf16[1040,256]{1,0:T(8,128)(2,1)S(1)} %get-tuple-element.15.refs_0_.merged, f32[256,256]{1,0:T(8,128)S(1)} %bitcast.9, f32[1,256]{1,0:T(1,128)S(1)} %copy-done.1, bf16[32,1408]{1,0:T(8,128)(2,1)S(1)} %shard_map.90.refs_0_, ...), custom_call_target="tpu_custom_call" | custom-call | flops 33554432 | bytes 1943552 | tf_op jit(solution)/shard_map/pallas_call | solution.py:27
  (6 shorter events, 0.0 us)
Async XLA Ops:
  2.1 6.5 %collective-permute-start.2 = (f32[32,1024]{1,0:T(8,128)S(1)}, f32[32,1024]{1,0:T(8,128)S(1)}, u32[]{:S(2)}, u32[]{:S(2)}) collective-permute-start(f32[32,1024]{1,0:T(8,128)S(1)} %get-tuple-element.14.refs_0_), channel_id=1, source_target_pairs={{0,8},{25,17},{1,0},{8,9},{17,16},{24,25},{9,1},{16,24},{2,10},{27... | collective-permute-start | bytes 393224 | tf_op jit(solution)/shard_map/ppermute | solution.py:221
  5.2 4.4 %collective-permute-start.1 = (f32[32,1024]{1,0:T(8,128)S(1)}, f32[32,1024]{1,0:T(8,128)S(1)}, u32[]{:S(2)}, u32[]{:S(2)}) collective-permute-start(f32[32,1024]{1,0:T(8,128)S(1)} %get-tuple-element.14.refs_0_), channel_id=1, source_target_pairs={{24,8},{1,17},{0,1},{8,9},{17,16},{25,24},{9,0},{16,25},{26,10},{3... | collective-permute-start | bytes 393224 | tf_op jit(solution)/shard_map/ppermute | solution.py:221
  5.2 4.4 %collective-permute-start = (f32[32,1024]{1,0:T(8,128)S(1)}, f32[32,1024]{1,0:T(8,128)S(1)}, u32[]{:S(2)}, u32[]{:S(2)}) collective-permute-start(f32[32,1024]{1,0:T(8,128)S(1)} %get-tuple-element.14.refs_0_), channel_id=1, source_target_pairs={{16,8},{9,17},{0,1},{1,0},{8,9},{17,16},{24,25},{25,24},{18,10},{1... | collective-permute-start | bytes 393224 | tf_op jit(solution)/shard_map/ppermute | solution.py:221
  6.5 9.7 %collective-permute-start.7 = (bf16[1040,256]{1,0:T(8,128)(2,1)S(1)}, bf16[1040,256]{1,0:T(8,128)(2,1)S(1)}, u32[]{:S(2)}, u32[]{:S(2)}) collective-permute-start(bf16[1040,256]{1,0:T(8,128)(2,1)S(1)} %get-tuple-element.15.refs_0_.merged), channel_id=1, source_target_pairs={{0,8},{25,17},{1,0},{8,9},{17,16},{24,25},{9,1},{16,24},{2,10},{27... | collective-permute-start | bytes 1597448 | tf_op jit(solution)/shard_map/ppermute | solution.py:221
  7.4 8.8 %collective-permute-start.6 = (bf16[1040,256]{1,0:T(8,128)(2,1)S(1)}, bf16[1040,256]{1,0:T(8,128)(2,1)S(1)}, u32[]{:S(2)}, u32[]{:S(2)}) collective-permute-start(bf16[1040,256]{1,0:T(8,128)(2,1)S(1)} %get-tuple-element.15.refs_0_.merged), channel_id=1, source_target_pairs={{16,8},{9,17},{0,1},{1,0},{8,9},{17,16},{24,25},{25,24},{18,10},{1... | collective-permute-start | bytes 1597448 | tf_op jit(solution)/shard_map/ppermute | solution.py:221
  9.7 11.4 %collective-permute-start.5 = (bf16[1040,256]{1,0:T(8,128)(2,1)S(1)}, bf16[1040,256]{1,0:T(8,128)(2,1)S(1)}, u32[]{:S(2)}, u32[]{:S(2)}) collective-permute-start(bf16[1040,256]{1,0:T(8,128)(2,1)S(1)} %get-tuple-element.15.refs_0_.merged), channel_id=1, source_target_pairs={{24,8},{1,17},{0,1},{8,9},{17,16},{25,24},{9,0},{16,25},{26,10},{3... | collective-permute-start | bytes 1597448 | tf_op jit(solution)/shard_map/ppermute | solution.py:221
  9.8 4.2 %collective-permute-start.3 = (f32[32,1024]{1,0:T(8,128)S(1)}, f32[32,1024]{1,0:T(8,128)S(1)}, u32[]{:S(2)}, u32[]{:S(2)}) collective-permute-start(f32[32,1024]{1,0:T(8,128)S(1)} %shard_map.86), channel_id=1, source_target_pairs={{8,10},{10,8},{12,14},{14,12},{9,11},{11,9},{13,15},{15,13},{16,18... | collective-permute-start | bytes 393224 | tf_op jit(solution)/shard_map/ppermute | solution.py:230
  14.0 1.4 %collective-permute-start.4 = (f32[32,1024]{1,0:T(8,128)S(1)}, f32[32,1024]{1,0:T(8,128)S(1)}, u32[]{:S(2)}, u32[]{:S(2)}) collective-permute-start(f32[32,1024]{1,0:T(8,128)S(1)} %add.3.refs_0_), channel_id=1, source_target_pairs={{8,12},{10,14},{12,8},{14,10},{9,13},{11,15},{13,9},{15,11},{16,20... | collective-permute-start | bytes 393224 | tf_op jit(solution)/shard_map/ppermute | solution.py:230
  21.0 1.3 %collective-permute-start.10 = (f32[32,1024]{1,0:T(8,128)S(1)}, f32[32,1024]{1,0:T(8,128)S(1)}, u32[]{:S(2)}, u32[]{:S(2)}) collective-permute-start(f32[32,1024]{1,0:T(8,128)S(1)} %get-tuple-element.16.refs_0_), channel_id=1, source_target_pairs={{8,14},{10,12},{12,10},{14,8},{17,23},{19,21},{21,19},{23,17},{0,1... | collective-permute-start | bytes 393224 | tf_op jit(solution)/shard_map/ppermute | solution.py:230
  21.0 1.5 %collective-permute-start.9 = (f32[32,1024]{1,0:T(8,128)S(1)}, f32[32,1024]{1,0:T(8,128)S(1)}, u32[]{:S(2)}, u32[]{:S(2)}) collective-permute-start(f32[32,1024]{1,0:T(8,128)S(1)} %get-tuple-element.16.refs_0_), channel_id=1, source_target_pairs={{8,12},{10,14},{12,8},{14,10},{17,21},{19,23},{21,17},{23,19},{0,1... | collective-permute-start | bytes 393224 | tf_op jit(solution)/shard_map/ppermute | solution.py:230
  21.5 1.3 %collective-permute-start.8 = (f32[32,1024]{1,0:T(8,128)S(1)}, f32[32,1024]{1,0:T(8,128)S(1)}, u32[]{:S(2)}, u32[]{:S(2)}) collective-permute-start(f32[32,1024]{1,0:T(8,128)S(1)} %get-tuple-element.16.refs_0_), channel_id=1, source_target_pairs={{8,10},{10,8},{12,14},{14,12},{17,19},{19,17},{21,23},{23,21},{0,1... | collective-permute-start | bytes 393224 | tf_op jit(solution)/shard_map/ppermute | solution.py:230
  22.9 14.7 %copy-start = (f32[1,256,256]{2,1,0:T(8,128)S(1)}, f32[1,256,256]{2,1,0:T(8,128)}, u32[]{:S(2)}) copy-start(f32[1,256,256]{2,1,0:T(8,128)} %param.9) | copy-start | bytes 786436
  22.9 14.7 %copy-start.1 = (f32[1,256]{1,0:T(1,128)S(1)}, f32[1,256]{1,0:T(1,128)}, u32[]{:S(2)}) copy-start(f32[1,256]{1,0:T(1,128)} %vec_momentum.1) | copy-start | bytes 3076
  22.9 14.7 %collective-permute-start.13 = (bf16[32,1408]{1,0:T(8,128)(2,1)S(1)}, bf16[32,1408]{1,0:T(8,128)(2,1)S(1)}, u32[]{:S(2)}, u32[]{:S(2)}) collective-permute-start(bf16[32,1408]{1,0:T(8,128)(2,1)S(1)} %shard_map.90.refs_0_), channel_id=1, source_target_pairs={{8,0},{17,25},{0,1},{9,8},{16,17},{25,24},{1,9},{24,16},{10,2},{19... | collective-permute-start | bytes 270344 | tf_op jit(solution)/shard_map/ppermute | solution.py:221
  23.1 14.5 %collective-permute-start.12 = (bf16[32,1408]{1,0:T(8,128)(2,1)S(1)}, bf16[32,1408]{1,0:T(8,128)(2,1)S(1)}, u32[]{:S(2)}, u32[]{:S(2)}) collective-permute-start(bf16[32,1408]{1,0:T(8,128)(2,1)S(1)} %shard_map.90.refs_0_), channel_id=1, source_target_pairs={{8,24},{17,1},{1,0},{9,8},{16,17},{24,25},{0,9},{25,16},{10,26},{1... | collective-permute-start | bytes 270344 | tf_op jit(solution)/shard_map/ppermute | solution.py:221
  35.2 2.4 %collective-permute-start.11 = (bf16[32,1408]{1,0:T(8,128)(2,1)S(1)}, bf16[32,1408]{1,0:T(8,128)(2,1)S(1)}, u32[]{:S(2)}, u32[]{:S(2)}) collective-permute-start(bf16[32,1408]{1,0:T(8,128)(2,1)S(1)} %shard_map.90.refs_0_), channel_id=1, source_target_pairs={{8,16},{17,9},{1,0},{0,1},{9,8},{16,17},{25,24},{24,25},{10,18},{1... | collective-permute-start | bytes 270344 | tf_op jit(solution)/shard_map/ppermute | solution.py:221

commit v6 on v5

--- a/solution.py
+++ b/solution.py
@@ -154,7 +154,7 @@
     own_rows = momentum.shape[0]
     z, s = lax.axis_index("replica"), lax.axis_index("section")
     came = sum(
-        jnp.where((z == row[j]) & (s == i), j + 1, 0) for i, row in enumerate(sources) for j in range(len(row))
+        jnp.where((z == row[j]) & (s == i), (0, 1, 2)[j] + 1, 0) for i, row in enumerate(sources) for j in range(len(row))
     )
     for i, pack in enumerate(packs):
 
@@ -251,7 +251,7 @@
     planes = [p for p in places if p[0] in owner]
     p_in = along(p_part, inward)
     m_near = along(merged, inward[:1] + inward[2:])
-    p_part = call(add_kernel, [p_shape], p_part, *p_in)[0]
+    p_part = call(add_kernel, [p_shape], p_part, *(p_in[i] for i in (2, 0, 1)))[0]
     held = lax.optimization_barrier((merged, p_part))[0]
     m_in = along(held, inward[1:2]) + m_near
     k = 1
@@ -267,7 +267,7 @@
             [jax.ShapeDtypeStruct(block, BF16)] * 2 + [jax.ShapeDtypeStruct((1, cols), F32), p_shape],
             p_lo,
             merged,
-            *m_in,
+            *(m_in[i] for i in (1, 2, 0)),
             flops=4 * work,
         )
         parts = across(p_part, range(1, tensors), [(owner[s], s) for s in range(sections)])
@@ -291,7 +291,7 @@
         momentum[0],
         vec_momentum,
         whole,
-        *received,
+        *(received[i] for i in (0, 1, 2)),
         flops=2 * work,
         out_specs=[HBM] * 3,
         scratch=[

time: 39 us -> 38.7 us (level)
  starting transfers between devices: 21.8 us -> 20.7 us
  waiting for transfers between devices: 13.6 us -> 14.3 us
    ppermute x5, starting transfers between devices: 4.11 us -> 3.36 us  [across(): parts.append(lax.ppermute(x, ('replica', 'tensor', 'section'), order))]
    ppermute x9, waiting for transfers between devices: 10.3 us -> 11 us  [along(): lax.ppermute(x, ('replica', 'section'), [(number(a), number(b)) for a, b...]
where the time goes in v6:
time: 38.7 us; the launch traced here: 38.6 us
  starting transfers between devices  20.7 us (53%)
  waiting for transfers between devices  14.3 us (37%)
  Pallas kernels  2.82 us (7%)
  between operations  0.67 us (2%)
    ppermute x9, starting transfers between devices, along(): lax.ppermute(x, ('replica', 'section'), [(number(a), number(b)) for a, b...  17.4 us
    ppermute x9, waiting for transfers between devices, along(): lax.ppermute(x, ('replica', 'section'), [(number(a), number(b)) for a, b...  11 us
    ppermute x5, starting transfers between devices, across(): parts.append(lax.ppermute(x, ('replica', 'tensor', 'section'), order))  3.36 us
    ppermute x5, waiting for transfers between devices, across(): parts.append(lax.ppermute(x, ('replica', 'tensor', 'section'), order))  3.32 us
    pallas_call x7, Pallas kernels, call(): pl.pallas_call(kernel, out_shape=outs, in_specs=in_specs or [VMEM] * len(...  2.82 us
  transfers between devices with their start and end apart: 14, of which 10 were waited for; matrix products, arithmetic and copies ran while one was open for 0% of the time, Pallas kernels for 0%

profile of v6, /device:TPU:0, one launch (start us, length us, event | category | flops | bytes accessed | tf_op | source)
XLA Modules:
  0.0 38.6 jit_solution(4261202921495389092)
XLA Ops:
  0.6 1.5 %shard_map.85 = (bf16[1040,256]{1,0:T(8,128)(2,1)S(1)}, f32[32,1024]{1,0:T(8,128)S(1)}) custom-call(bf16[1024,256]{1,0:T(8,128)(2,1)} %bitcast.10, bf16[1024,256]{1,0:T(8,128)(2,1)} %bitcast.11, f32[32,256]{1,0:T(8,128)} %bitcast.12, f32[1,256]{1,0:T(1,128)} %bitcast.13), custom_call_target="tpu_custom_call" | custom-call | flops 16777216 | bytes 1745920 | tf_op jit(solution)/shard_map/pallas_call | solution.py:27
  2.1 0.5 %collective-permute-start.2 = (f32[32,1024]{1,0:T(8,128)S(1)}, f32[32,1024]{1,0:T(8,128)S(1)}, u32[]{:S(2)}, u32[]{:S(2)}) collective-permute-start(f32[32,1024]{1,0:T(8,128)S(1)} %get-tuple-element.14.refs_0_), channel_id=1, source_target_pairs={{24,8},{1,17},{0,1},{8,9},{17,16},{25,24},{9,0},{16,25},{26,10},{3... | collective-permute-start | bytes 393224 | tf_op jit(solution)/shard_map/ppermute | solution.py:221
  2.7 3.1 %collective-permute-start.1 = (f32[32,1024]{1,0:T(8,128)S(1)}, f32[32,1024]{1,0:T(8,128)S(1)}, u32[]{:S(2)}, u32[]{:S(2)}) collective-permute-start(f32[32,1024]{1,0:T(8,128)S(1)} %get-tuple-element.14.refs_0_), channel_id=1, source_target_pairs={{16,8},{9,17},{0,1},{1,0},{8,9},{17,16},{24,25},{25,24},{18,10},{1... | collective-permute-start | bytes 393224 | tf_op jit(solution)/shard_map/ppermute | solution.py:221
  5.8 0.0 collective-permute-start
  5.8 1.2 %collective-permute-start.6 = (bf16[1040,256]{1,0:T(8,128)(2,1)S(1)}, bf16[1040,256]{1,0:T(8,128)(2,1)S(1)}, u32[]{:S(2)}, u32[]{:S(2)}) collective-permute-start(bf16[1040,256]{1,0:T(8,128)(2,1)S(1)} %get-tuple-element.15.refs_0_.merged), channel_id=1, source_target_pairs={{0,8},{25,17},{1,0},{8,9},{17,16},{24,25},{9,1},{16,24},{2,10},{27... | collective-permute-start | bytes 1597448 | tf_op jit(solution)/shard_map/ppermute | solution.py:221
  7.0 0.0 collective-permute-start.5
  7.0 0.3 collective-permute-done.2.refs_3_
  7.3 0.0 collective-permute-done.1.refs_2_
  7.3 1.7 %collective-permute-done.refs_1_ = f32[32,1024]{1,0:T(8,128)S(1)} collective-permute-done((f32[32,1024]{1,0:T(8,128)S(1)}, f32[32,1024]{1,0:T(8,128)S(1)}, u32[]{:S(2)}, u32[]{:S(2)}) %collective-permute-start) | collective-permute-done | bytes 131104 | tf_op jit(solution)/shard_map/ppermute | solution.py:221
  9.0 0.7 %collective-permute-start.7 = (bf16[1040,256]{1,0:T(8,128)(2,1)S(1)}, bf16[1040,256]{1,0:T(8,128)(2,1)S(1)}, u32[]{:S(2)}, u32[]{:S(2)}) collective-permute-start(bf16[1040,256]{1,0:T(8,128)(2,1)S(1)} %get-tuple-element.15.refs_0_.merged), channel_id=1, source_target_pairs={{24,8},{1,17},{0,1},{8,9},{17,16},{25,24},{9,0},{16,25},{26,10},{3... | collective-permute-start | bytes 1597448 | tf_op jit(solution)/shard_map/ppermute | solution.py:221
  9.7 2.4 %collective-permute-start.3 = (f32[32,1024]{1,0:T(8,128)S(1)}, f32[32,1024]{1,0:T(8,128)S(1)}, u32[]{:S(2)}, u32[]{:S(2)}) collective-permute-start(f32[32,1024]{1,0:T(8,128)S(1)} %shard_map.86), channel_id=1, source_target_pairs={{8,10},{10,8},{12,14},{14,12},{9,11},{11,9},{13,15},{15,13},{16,18... | collective-permute-start | bytes 393224 | tf_op jit(solution)/shard_map/ppermute | solution.py:230
  12.1 1.0 %collective-permute-done.3 = f32[32,1024]{1,0:T(8,128)S(1)} collective-permute-done((f32[32,1024]{1,0:T(8,128)S(1)}, f32[32,1024]{1,0:T(8,128)S(1)}, u32[]{:S(2)}, u32[]{:S(2)}) %collective-permute-start.3) | collective-permute-done | bytes 131104 | tf_op jit(solution)/shard_map/ppermute | solution.py:230
  13.1 0.4 %collective-permute-start.4 = (f32[32,1024]{1,0:T(8,128)S(1)}, f32[32,1024]{1,0:T(8,128)S(1)}, u32[]{:S(2)}, u32[]{:S(2)}) collective-permute-start(f32[32,1024]{1,0:T(8,128)S(1)} %add.3.refs_0_), channel_id=1, source_target_pairs={{8,12},{10,14},{12,8},{14,10},{9,13},{11,15},{13,9},{15,11},{16,20... | collective-permute-start | bytes 393224 | tf_op jit(solution)/shard_map/ppermute | solution.py:230
  13.6 1.0 %collective-permute-done.4.refs_1_ = f32[32,1024]{1,0:T(8,128)S(1)} collective-permute-done((f32[32,1024]{1,0:T(8,128)S(1)}, f32[32,1024]{1,0:T(8,128)S(1)}, u32[]{:S(2)}, u32[]{:S(2)}) %collective-permute-start.4) | collective-permute-done | bytes 131104 | tf_op jit(solution)/shard_map/ppermute | solution.py:230
  14.6 2.3 %collective-permute-done.6.refs_2_ = bf16[1040,256]{1,0:T(8,128)(2,1)S(1)} collective-permute-done((bf16[1040,256]{1,0:T(8,128)(2,1)S(1)}, bf16[1040,256]{1,0:T(8,128)(2,1)S(1)}, u32[]{:S(2)}, u32[]{:S(2)}) %collective-permute-start.6) | collective-permute-done | bytes 532512 | tf_op jit(solution)/shard_map/ppermute | solution.py:221
  16.8 0.0 collective-permute-done.5.refs_1_
  16.8 4.4 %collective-permute-done.7.refs_3_ = bf16[1040,256]{1,0:T(8,128)(2,1)S(1)} collective-permute-done((bf16[1040,256]{1,0:T(8,128)(2,1)S(1)}, bf16[1040,256]{1,0:T(8,128)(2,1)S(1)}, u32[]{:S(2)}, u32[]{:S(2)}) %collective-permute-start.7) | collective-permute-done | bytes 532512 | tf_op jit(solution)/shard_map/ppermute | solution.py:221
  21.2 0.0 collective-permute-start.10
  21.2 0.5 %collective-permute-start.9 = (f32[32,1024]{1,0:T(8,128)S(1)}, f32[32,1024]{1,0:T(8,128)S(1)}, u32[]{:S(2)}, u32[]{:S(2)}) collective-permute-start(f32[32,1024]{1,0:T(8,128)S(1)} %get-tuple-element.16.refs_0_), channel_id=1, source_target_pairs={{8,12},{10,14},{12,8},{14,10},{17,21},{19,23},{21,17},{23,19},{0,1... | collective-permute-start | bytes 393224 | tf_op jit(solution)/shard_map/ppermute | solution.py:230
  21.7 0.0 collective-permute-start.8
  21.7 0.8 %collective-permute-done.10.refs_3_ = f32[32,1024]{1,0:T(8,128)S(1)} collective-permute-done((f32[32,1024]{1,0:T(8,128)S(1)}, f32[32,1024]{1,0:T(8,128)S(1)}, u32[]{:S(2)}, u32[]{:S(2)}) %collective-permute-start.10) | collective-permute-done | bytes 131104 | tf_op jit(solution)/shard_map/ppermute | solution.py:230
  22.6 0.2 collective-permute-done.9.refs_2_
  22.7 0.3 collective-permute-done.8.refs_1_
  23.1 0.0 copy-start
  23.1 0.0 copy-start.1
  23.1 0.2 collective-permute-start.13
  23.3 11.6 %collective-permute-start.12 = (bf16[32,1408]{1,0:T(8,128)(2,1)S(1)}, bf16[32,1408]{1,0:T(8,128)(2,1)S(1)}, u32[]{:S(2)}, u32[]{:S(2)}) collective-permute-start(bf16[32,1408]{1,0:T(8,128)(2,1)S(1)} %shard_map.90.refs_0_), channel_id=1, source_target_pairs={{8,24},{17,1},{1,0},{9,8},{16,17},{24,25},{0,9},{25,16},{10,26},{1... | collective-permute-start | bytes 270344 | tf_op jit(solution)/shard_map/ppermute | solution.py:221
  34.9 0.0 collective-permute-start.11
  34.9 2.4 %collective-permute-done.13.refs_3_ = bf16[32,1408]{1,0:T(8,128)(2,1)S(1)} collective-permute-done((bf16[32,1408]{1,0:T(8,128)(2,1)S(1)}, bf16[32,1408]{1,0:T(8,128)(2,1)S(1)}, u32[]{:S(2)}, u32[]{:S(2)}) %collective-permute-start.13) | collective-permute-done | bytes 90144 | tf_op jit(solution)/shard_map/ppermute | solution.py:221
  37.2 0.0 collective-permute-done.12.refs_2_
  37.2 0.0 collective-permute-done.11.refs_1_
  37.3 0.0 copy-done
  37.3 0.0 copy-done.1
  37.3 1.3 %shard_map.91 = (bf16[1024,256]{1,0:T(8,128)(2,1)}, f32[256,256]{1,0:T(8,128)}, f32[1,256]{1,0:T(1,128)}) custom-call(bf16[1040,256]{1,0:T(8,128)(2,1)S(1)} %get-tuple-element.15.refs_0_.merged, f32[256,256]{1,0:T(8,128)S(1)} %bitcast.9, f32[1,256]{1,0:T(1,128)S(1)} %copy-done.1, bf16[32,1408]{1,0:T(8,128)(2,1)S(1)} %shard_map.90.refs_0_, ...), custom_call_target="tpu_custom_call" | custom-call | flops 33554432 | bytes 1943552 | tf_op jit(solution)/shard_map/pallas_call | solution.py:27
  (6 shorter events, 0.0 us)
Async XLA Ops:
  2.1 5.2 %collective-permute-start.2 = (f32[32,1024]{1,0:T(8,128)S(1)}, f32[32,1024]{1,0:T(8,128)S(1)}, u32[]{:S(2)}, u32[]{:S(2)}) collective-permute-start(f32[32,1024]{1,0:T(8,128)S(1)} %get-tuple-element.14.refs_0_), channel_id=1, source_target_pairs={{24,8},{1,17},{0,1},{8,9},{17,16},{25,24},{9,0},{16,25},{26,10},{3... | collective-permute-start | bytes 393224 | tf_op jit(solution)/shard_map/ppermute | solution.py:221
  2.7 4.7 %collective-permute-start.1 = (f32[32,1024]{1,0:T(8,128)S(1)}, f32[32,1024]{1,0:T(8,128)S(1)}, u32[]{:S(2)}, u32[]{:S(2)}) collective-permute-start(f32[32,1024]{1,0:T(8,128)S(1)} %get-tuple-element.14.refs_0_), channel_id=1, source_target_pairs={{16,8},{9,17},{0,1},{1,0},{8,9},{17,16},{24,25},{25,24},{18,10},{1... | collective-permute-start | bytes 393224 | tf_op jit(solution)/shard_map/ppermute | solution.py:221
  5.8 3.2 %collective-permute-start = (f32[32,1024]{1,0:T(8,128)S(1)}, f32[32,1024]{1,0:T(8,128)S(1)}, u32[]{:S(2)}, u32[]{:S(2)}) collective-permute-start(f32[32,1024]{1,0:T(8,128)S(1)} %get-tuple-element.14.refs_0_), channel_id=1, source_target_pairs={{0,8},{25,17},{1,0},{8,9},{17,16},{24,25},{9,1},{16,24},{2,10},{27... | collective-permute-start | bytes 393224 | tf_op jit(solution)/shard_map/ppermute | solution.py:221
  5.8 11.0 %collective-permute-start.6 = (bf16[1040,256]{1,0:T(8,128)(2,1)S(1)}, bf16[1040,256]{1,0:T(8,128)(2,1)S(1)}, u32[]{:S(2)}, u32[]{:S(2)}) collective-permute-start(bf16[1040,256]{1,0:T(8,128)(2,1)S(1)} %get-tuple-element.15.refs_0_.merged), channel_id=1, source_target_pairs={{0,8},{25,17},{1,0},{8,9},{17,16},{24,25},{9,1},{16,24},{2,10},{27... | collective-permute-start | bytes 1597448 | tf_op jit(solution)/shard_map/ppermute | solution.py:221
  7.0 9.8 %collective-permute-start.5 = (bf16[1040,256]{1,0:T(8,128)(2,1)S(1)}, bf16[1040,256]{1,0:T(8,128)(2,1)S(1)}, u32[]{:S(2)}, u32[]{:S(2)}) collective-permute-start(bf16[1040,256]{1,0:T(8,128)(2,1)S(1)} %get-tuple-element.15.refs_0_.merged), channel_id=1, source_target_pairs={{16,8},{9,17},{0,1},{1,0},{8,9},{17,16},{24,25},{25,24},{18,10},{1... | collective-permute-start | bytes 1597448 | tf_op jit(solution)/shard_map/ppermute | solution.py:221
  9.0 12.2 %collective-permute-start.7 = (bf16[1040,256]{1,0:T(8,128)(2,1)S(1)}, bf16[1040,256]{1,0:T(8,128)(2,1)S(1)}, u32[]{:S(2)}, u32[]{:S(2)}) collective-permute-start(bf16[1040,256]{1,0:T(8,128)(2,1)S(1)} %get-tuple-element.15.refs_0_.merged), channel_id=1, source_target_pairs={{24,8},{1,17},{0,1},{8,9},{17,16},{25,24},{9,0},{16,25},{26,10},{3... | collective-permute-start | bytes 1597448 | tf_op jit(solution)/shard_map/ppermute | solution.py:221
  9.7 3.4 %collective-permute-start.3 = (f32[32,1024]{1,0:T(8,128)S(1)}, f32[32,1024]{1,0:T(8,128)S(1)}, u32[]{:S(2)}, u32[]{:S(2)}) collective-permute-start(f32[32,1024]{1,0:T(8,128)S(1)} %shard_map.86), channel_id=1, source_target_pairs={{8,10},{10,8},{12,14},{14,12},{9,11},{11,9},{13,15},{15,13},{16,18... | collective-permute-start | bytes 393224 | tf_op jit(solution)/shard_map/ppermute | solution.py:230
  13.1 1.4 %collective-permute-start.4 = (f32[32,1024]{1,0:T(8,128)S(1)}, f32[32,1024]{1,0:T(8,128)S(1)}, u32[]{:S(2)}, u32[]{:S(2)}) collective-permute-start(f32[32,1024]{1,0:T(8,128)S(1)} %add.3.refs_0_), channel_id=1, source_target_pairs={{8,12},{10,14},{12,8},{14,10},{9,13},{11,15},{13,9},{15,11},{16,20... | collective-permute-start | bytes 393224 | tf_op jit(solution)/shard_map/ppermute | solution.py:230
  21.2 1.3 %collective-permute-start.10 = (f32[32,1024]{1,0:T(8,128)S(1)}, f32[32,1024]{1,0:T(8,128)S(1)}, u32[]{:S(2)}, u32[]{:S(2)}) collective-permute-start(f32[32,1024]{1,0:T(8,128)S(1)} %get-tuple-element.16.refs_0_), channel_id=1, source_target_pairs={{8,14},{10,12},{12,10},{14,8},{17,23},{19,21},{21,19},{23,17},{0,1... | collective-permute-start | bytes 393224 | tf_op jit(solution)/shard_map/ppermute | solution.py:230
  21.2 1.5 %collective-permute-start.9 = (f32[32,1024]{1,0:T(8,128)S(1)}, f32[32,1024]{1,0:T(8,128)S(1)}, u32[]{:S(2)}, u32[]{:S(2)}) collective-permute-start(f32[32,1024]{1,0:T(8,128)S(1)} %get-tuple-element.16.refs_0_), channel_id=1, source_target_pairs={{8,12},{10,14},{12,8},{14,10},{17,21},{19,23},{21,17},{23,19},{0,1... | collective-permute-start | bytes 393224 | tf_op jit(solution)/shard_map/ppermute | solution.py:230
  21.7 1.3 %collective-permute-start.8 = (f32[32,1024]{1,0:T(8,128)S(1)}, f32[32,1024]{1,0:T(8,128)S(1)}, u32[]{:S(2)}, u32[]{:S(2)}) collective-permute-start(f32[32,1024]{1,0:T(8,128)S(1)} %get-tuple-element.16.refs_0_), channel_id=1, source_target_pairs={{8,10},{10,8},{12,14},{14,12},{17,19},{19,17},{21,23},{23,21},{0,1... | collective-permute-start | bytes 393224 | tf_op jit(solution)/shard_map/ppermute | solution.py:230
  23.1 14.2 %copy-start = (f32[1,256,256]{2,1,0:T(8,128)S(1)}, f32[1,256,256]{2,1,0:T(8,128)}, u32[]{:S(2)}) copy-start(f32[1,256,256]{2,1,0:T(8,128)} %param.9) | copy-start | bytes 786436
  23.1 14.2 %copy-start.1 = (f32[1,256]{1,0:T(1,128)S(1)}, f32[1,256]{1,0:T(1,128)}, u32[]{:S(2)}) copy-start(f32[1,256]{1,0:T(1,128)} %vec_momentum.1) | copy-start | bytes 3076
  23.1 14.2 %collective-permute-start.13 = (bf16[32,1408]{1,0:T(8,128)(2,1)S(1)}, bf16[32,1408]{1,0:T(8,128)(2,1)S(1)}, u32[]{:S(2)}, u32[]{:S(2)}) collective-permute-start(bf16[32,1408]{1,0:T(8,128)(2,1)S(1)} %shard_map.90.refs_0_), channel_id=1, source_target_pairs={{8,0},{17,25},{0,1},{9,8},{16,17},{25,24},{1,9},{24,16},{10,2},{19... | collective-permute-start | bytes 270344 | tf_op jit(solution)/shard_map/ppermute | solution.py:221
  23.3 14.0 %collective-permute-start.12 = (bf16[32,1408]{1,0:T(8,128)(2,1)S(1)}, bf16[32,1408]{1,0:T(8,128)(2,1)S(1)}, u32[]{:S(2)}, u32[]{:S(2)}) collective-permute-start(bf16[32,1408]{1,0:T(8,128)(2,1)S(1)} %shard_map.90.refs_0_), channel_id=1, source_target_pairs={{8,24},{17,1},{1,0},{9,8},{16,17},{24,25},{0,9},{25,16},{10,26},{1... | collective-permute-start | bytes 270344 | tf_op jit(solution)/shard_map/ppermute | solution.py:221
  34.9 2.4 %collective-permute-start.11 = (bf16[32,1408]{1,0:T(8,128)(2,1)S(1)}, bf16[32,1408]{1,0:T(8,128)(2,1)S(1)}, u32[]{:S(2)}, u32[]{:S(2)}) collective-permute-start(bf16[32,1408]{1,0:T(8,128)(2,1)S(1)} %shard_map.90.refs_0_), channel_id=1, source_target_pairs={{8,16},{17,9},{1,0},{0,1},{9,8},{16,17},{25,24},{24,25},{10,18},{1... | collective-permute-start | bytes 270344 | tf_op jit(solution)/shard_map/ppermute | solution.py:221

commit v7 on v6

--- a/solution.py
+++ b/solution.py
@@ -216,6 +216,7 @@
     ]
     outward = [[(b, a) for a, b in pairs] for pairs in inward]
     number = lambda place: place[0] * sections + place[1]
+    device = lambda place: (place[0] * tensors + place[1]) * sections + place[2]
 
     def along(x, perms):
         return [lax.ppermute(x, ("replica", "section"), [(number(a), number(b)) for a, b in p]) for p in perms]
@@ -228,6 +229,23 @@
             pairs += [((a[0], i, a[1]), (b[0], i, b[1])) for a, b in completed([], idle) for i in range(tensors)]
             order = [((a[0] * tensors + a[1]) * sections + a[2], (b[0] * tensors + b[1]) * sections + b[2]) for a, b in pairs]
             parts.append(lax.ppermute(x, ("replica", "tensor", "section"), order))
+        return parts
+
+    def to_mates(x):
+        parts = []
+        for k in range(1, tensors):
+            pairs = []
+            for s in range(sections):
+                mate, outer = sections - 1 - s, sources[s][-1]
+                ring = [(owner[s], mate), (outer, s), (outer, mate), (owner[s], s)]
+                if k < tensors - 1:
+                    rest = [(ring[0], ring[3]), (ring[1], ring[2]), (ring[2], ring[1])]
+                else:
+                    rest = list(zip(ring, ring[1:]))
+                for i in range(tensors):
+                    pairs.append(((owner[s], i, s), (owner[s], i ^ k, mate)))
+                    pairs += [((a[0], i, a[1]), (b[0], i, b[1])) for a, b in rest]
+            parts.append(lax.ppermute(x, ("replica", "tensor", "section"), [(device(a), device(b)) for a, b in pairs]))
         return parts
 
     p_shape = jax.ShapeDtypeStruct((rank, rows), F32)
@@ -270,7 +288,8 @@
             *(m_in[i] for i in (1, 2, 0)),
             flops=4 * work,
         )
-        parts = across(p_part, range(1, tensors), [(owner[s], s) for s in range(sections)])
+        p_other = call(add_kernel, [p_shape], *to_mates(p_part))[0]
+        parts = [p_part, lax.ppermute(p_other, "section", [(s, sections - 1 - s) for s in range(sections)])]
     p_lo = call(functools.partial(factor_kernel, replicas, owner), [lo_shape], *parts)[0]
     whole = call(
         functools.partial(last_kernel, owner),

time: 38.7 us -> 38.6 us (level)
  starting transfers between devices: 20.7 us -> 18.6 us
  waiting for transfers between devices: 14.3 us -> 16.3 us
    ppermute x9, starting transfers between devices: 17.4 us -> 11.1 us  [along(): lax.ppermute(x, ('replica', 'section'), [(number(a), number(b)) for a, b...]
    ppermute x0 -> x4, starting transfers between devices: none -> 4.67 us  [the longest x3 4 us: to_mates(): lax.ppermute(x, ('replica', 'tensor', 'section'), [(device(a), device(b))...]
    ppermute x0 -> x4, waiting for transfers between devices: none -> 2.33 us  [the longest x3 1.34 us: to_mates(): lax.ppermute(x, ('replica', 'tensor', 'section'), [(device(a), device(b))...]
    ppermute x5 -> x2, waiting for transfers between devices: 3.32 us -> 1.97 us  [across(): parts.append(lax.ppermute(x, ('replica', 'tensor', 'section'), order))]
    ppermute x9, waiting for transfers between devices: 11 us -> 12 us  [along(): lax.ppermute(x, ('replica', 'section'), [(number(a), number(b)) for a, b...]
    ppermute x5 -> x2, starting transfers between devices: 3.36 us -> 2.85 us  [across(): parts.append(lax.ppermute(x, ('replica', 'tensor', 'section'), order))]
    pallas_call x7 -> x8, Pallas kernels: 2.82 us -> 2.83 us  [call(): pl.pallas_call(kernel, out_shape=outs, in_specs=in_specs or [VMEM] * len(...]
  transfers between devices with their start and end apart: 14 -> 15, of which waited for: 10 -> 11; matrix products, arithmetic and copies ran while one was open for 0% -> 0% of each run, Pallas kernels for 0% -> 0%
where the time goes in v7:
time: 38.6 us; the launch traced here: 38.4 us
  starting transfers between devices  18.6 us (48%)
  waiting for transfers between devices  16.3 us (42%)
  Pallas kernels  2.83 us (7%)
  between operations  0.68 us (2%)
    ppermute x9, waiting for transfers between devices, along(): lax.ppermute(x, ('replica', 'section'), [(number(a), number(b)) for a, b...  12 us
    ppermute x9, starting transfers between devices, along(): lax.ppermute(x, ('replica', 'section'), [(number(a), number(b)) for a, b...  11.1 us
    ppermute x3, starting transfers between devices, to_mates(): lax.ppermute(x, ('replica', 'tensor', 'section'), [(device(a), device(b))...  4 us
    ppermute x2, starting transfers between devices, across(): parts.append(lax.ppermute(x, ('replica', 'tensor', 'section'), order))  2.85 us
    pallas_call x8, Pallas kernels, call(): pl.pallas_call(kernel, out_shape=outs, in_specs=in_specs or [VMEM] * len(...  2.83 us
    ppermute x2, waiting for transfers between devices, across(): parts.append(lax.ppermute(x, ('replica', 'tensor', 'section'), order))  1.97 us
    ppermute x3, waiting for transfers between devices, to_mates(): lax.ppermute(x, ('replica', 'tensor', 'section'), [(device(a), device(b))...  1.34 us
    ppermute x1, waiting for transfers between devices, gathered(): lax.ppermute(p_other, 'section', [(s, sections - 1 - s) for s in range(se...  0.99 us
  transfers between devices with their start and end apart: 15, of which 11 were waited for; matrix products, arithmetic and copies ran while one was open for 0% of the time, Pallas kernels for 0%

profile of v7, /device:TPU:0, one launch (start us, length us, event | category | flops | bytes accessed | tf_op | source)
XLA Modules:
  0.0 38.4 jit_solution(269624075838550097)
XLA Ops:
  0.6 1.5 %shard_map.85 = (bf16[1040,256]{1,0:T(8,128)(2,1)S(1)}, f32[32,1024]{1,0:T(8,128)S(1)}) custom-call(bf16[1024,256]{1,0:T(8,128)(2,1)} %bitcast.10, bf16[1024,256]{1,0:T(8,128)(2,1)} %bitcast.11, f32[32,256]{1,0:T(8,128)} %bitcast.12, f32[1,256]{1,0:T(1,128)} %bitcast.13), custom_call_target="tpu_custom_call" | custom-call | flops 16777216 | bytes 1745920 | tf_op jit(solution)/shard_map/pallas_call | solution.py:27
  2.1 0.5 %collective-permute-start.2 = (f32[32,1024]{1,0:T(8,128)S(1)}, f32[32,1024]{1,0:T(8,128)S(1)}, u32[]{:S(2)}, u32[]{:S(2)}) collective-permute-start(f32[32,1024]{1,0:T(8,128)S(1)} %get-tuple-element.14.refs_0_), channel_id=1, source_target_pairs={{24,8},{1,17},{0,1},{8,9},{17,16},{25,24},{9,0},{16,25},{26,10},{3... | collective-permute-start | bytes 393224 | tf_op jit(solution)/shard_map/ppermute | solution.py:222
  2.7 3.1 %collective-permute-start.1 = (f32[32,1024]{1,0:T(8,128)S(1)}, f32[32,1024]{1,0:T(8,128)S(1)}, u32[]{:S(2)}, u32[]{:S(2)}) collective-permute-start(f32[32,1024]{1,0:T(8,128)S(1)} %get-tuple-element.14.refs_0_), channel_id=1, source_target_pairs={{16,8},{9,17},{0,1},{1,0},{8,9},{17,16},{24,25},{25,24},{18,10},{1... | collective-permute-start | bytes 393224 | tf_op jit(solution)/shard_map/ppermute | solution.py:222
  5.8 0.0 collective-permute-start
  5.8 1.2 %collective-permute-start.6 = (bf16[1040,256]{1,0:T(8,128)(2,1)S(1)}, bf16[1040,256]{1,0:T(8,128)(2,1)S(1)}, u32[]{:S(2)}, u32[]{:S(2)}) collective-permute-start(bf16[1040,256]{1,0:T(8,128)(2,1)S(1)} %get-tuple-element.15.refs_0_.merged), channel_id=1, source_target_pairs={{0,8},{25,17},{1,0},{8,9},{17,16},{24,25},{9,1},{16,24},{2,10},{27... | collective-permute-start | bytes 1597448 | tf_op jit(solution)/shard_map/ppermute | solution.py:222
  7.0 0.0 collective-permute-start.5
  7.0 0.3 collective-permute-done.2.refs_3_
  7.3 0.0 collective-permute-done.1.refs_2_
  7.3 1.7 %collective-permute-done.refs_1_ = f32[32,1024]{1,0:T(8,128)S(1)} collective-permute-done((f32[32,1024]{1,0:T(8,128)S(1)}, f32[32,1024]{1,0:T(8,128)S(1)}, u32[]{:S(2)}, u32[]{:S(2)}) %collective-permute-start) | collective-permute-done | bytes 131104 | tf_op jit(solution)/shard_map/ppermute | solution.py:222
  9.0 0.7 %collective-permute-start.7 = (bf16[1040,256]{1,0:T(8,128)(2,1)S(1)}, bf16[1040,256]{1,0:T(8,128)(2,1)S(1)}, u32[]{:S(2)}, u32[]{:S(2)}) collective-permute-start(bf16[1040,256]{1,0:T(8,128)(2,1)S(1)} %get-tuple-element.15.refs_0_.merged), channel_id=1, source_target_pairs={{24,8},{1,17},{0,1},{8,9},{17,16},{25,24},{9,0},{16,25},{26,10},{3... | collective-permute-start | bytes 1597448 | tf_op jit(solution)/shard_map/ppermute | solution.py:222
  9.7 2.4 %collective-permute-start.3 = (f32[32,1024]{1,0:T(8,128)S(1)}, f32[32,1024]{1,0:T(8,128)S(1)}, u32[]{:S(2)}, u32[]{:S(2)}) collective-permute-start(f32[32,1024]{1,0:T(8,128)S(1)} %shard_map.86), channel_id=1, source_target_pairs={{8,10},{10,8},{12,14},{14,12},{9,11},{11,9},{13,15},{15,13},{16,18... | collective-permute-start | bytes 393224 | tf_op jit(solution)/shard_map/ppermute | solution.py:231
  12.1 1.0 %collective-permute-done.3 = f32[32,1024]{1,0:T(8,128)S(1)} collective-permute-done((f32[32,1024]{1,0:T(8,128)S(1)}, f32[32,1024]{1,0:T(8,128)S(1)}, u32[]{:S(2)}, u32[]{:S(2)}) %collective-permute-start.3) | collective-permute-done | bytes 131104 | tf_op jit(solution)/shard_map/ppermute | solution.py:231
  13.1 0.4 %collective-permute-start.4 = (f32[32,1024]{1,0:T(8,128)S(1)}, f32[32,1024]{1,0:T(8,128)S(1)}, u32[]{:S(2)}, u32[]{:S(2)}) collective-permute-start(f32[32,1024]{1,0:T(8,128)S(1)} %add.3.refs_0_), channel_id=1, source_target_pairs={{8,12},{10,14},{12,8},{14,10},{9,13},{11,15},{13,9},{15,11},{16,20... | collective-permute-start | bytes 393224 | tf_op jit(solution)/shard_map/ppermute | solution.py:231
  13.6 1.0 %collective-permute-done.4.refs_1_ = f32[32,1024]{1,0:T(8,128)S(1)} collective-permute-done((f32[32,1024]{1,0:T(8,128)S(1)}, f32[32,1024]{1,0:T(8,128)S(1)}, u32[]{:S(2)}, u32[]{:S(2)}) %collective-permute-start.4) | collective-permute-done | bytes 131104 | tf_op jit(solution)/shard_map/ppermute | solution.py:231
  14.6 2.3 %collective-permute-done.6.refs_2_ = bf16[1040,256]{1,0:T(8,128)(2,1)S(1)} collective-permute-done((bf16[1040,256]{1,0:T(8,128)(2,1)S(1)}, bf16[1040,256]{1,0:T(8,128)(2,1)S(1)}, u32[]{:S(2)}, u32[]{:S(2)}) %collective-permute-start.6) | collective-permute-done | bytes 532512 | tf_op jit(solution)/shard_map/ppermute | solution.py:222
  16.8 0.0 collective-permute-done.5.refs_1_
  16.8 4.4 %collective-permute-done.7.refs_3_ = bf16[1040,256]{1,0:T(8,128)(2,1)S(1)} collective-permute-done((bf16[1040,256]{1,0:T(8,128)(2,1)S(1)}, bf16[1040,256]{1,0:T(8,128)(2,1)S(1)}, u32[]{:S(2)}, u32[]{:S(2)}) %collective-permute-start.7) | collective-permute-done | bytes 532512 | tf_op jit(solution)/shard_map/ppermute | solution.py:222
  21.2 0.0 collective-permute-start.10
  21.2 4.0 %collective-permute-start.9 = (f32[32,1024]{1,0:T(8,128)S(1)}, f32[32,1024]{1,0:T(8,128)S(1)}, u32[]{:S(2)}, u32[]{:S(2)}) collective-permute-start(f32[32,1024]{1,0:T(8,128)S(1)} %get-tuple-element.16.refs_0_), channel_id=1, source_target_pairs={{8,13},{9,8},{0,1},{1,0},{10,15},{11,10},{2,3},{3,2},{12,9},{13,12... | collective-permute-start | bytes 393224 | tf_op jit(solution)/shard_map/ppermute | solution.py:248
  25.2 0.0 collective-permute-start.8
  25.2 0.4 %collective-permute-done.10.refs_2_ = f32[32,1024]{1,0:T(8,128)S(1)} collective-permute-done((f32[32,1024]{1,0:T(8,128)S(1)}, f32[32,1024]{1,0:T(8,128)S(1)}, u32[]{:S(2)}, u32[]{:S(2)}) %collective-permute-start.10) | collective-permute-done | bytes 131104 | tf_op jit(solution)/shard_map/ppermute | solution.py:248
  25.6 0.6 %collective-permute-done.9.refs_1_ = f32[32,1024]{1,0:T(8,128)S(1)} collective-permute-done((f32[32,1024]{1,0:T(8,128)S(1)}, f32[32,1024]{1,0:T(8,128)S(1)}, u32[]{:S(2)}, u32[]{:S(2)}) %collective-permute-start.9) | collective-permute-done | bytes 131104 | tf_op jit(solution)/shard_map/ppermute | solution.py:248
  26.2 0.4 collective-permute-done.8.refs_0_
  26.6 0.7 %collective-permute-start.11 = (f32[32,1024]{1,0:T(8,128)S(1)}, f32[32,1024]{1,0:T(8,128)S(1)}, u32[]{:S(2)}, u32[]{:S(2)}) collective-permute-start(f32[32,1024]{1,0:T(8,128)S(1)} %shard_map.89), channel_id=1, source_target_pairs={{0,1},{1,0},{2,3},{3,2},{4,5},{5,4},{6,7},{7,6},{8,9},{9,8},{10,11... | collective-permute-start | bytes 393224 | tf_op jit(solution)/shard_map/ppermute | solution.py:292
  27.3 1.0 %collective-permute-done.11.refs_1_ = f32[32,1024]{1,0:T(8,128)S(1)} collective-permute-done((f32[32,1024]{1,0:T(8,128)S(1)}, f32[32,1024]{1,0:T(8,128)S(1)}, u32[]{:S(2)}, u32[]{:S(2)}) %collective-permute-start.11) | collective-permute-done | bytes 131104 | tf_op jit(solution)/shard_map/ppermute | solution.py:292
  28.2 0.0 copy-start
  28.2 0.0 copy-start.1
  28.3 0.4 collective-permute-start.14
  28.6 5.1 %collective-permute-start.13 = (bf16[32,1408]{1,0:T(8,128)(2,1)S(1)}, bf16[32,1408]{1,0:T(8,128)(2,1)S(1)}, u32[]{:S(2)}, u32[]{:S(2)}) collective-permute-start(bf16[32,1408]{1,0:T(8,128)(2,1)S(1)} %shard_map.91.refs_0_), channel_id=1, source_target_pairs={{8,24},{17,1},{1,0},{9,8},{16,17},{24,25},{0,9},{25,16},{10,26},{1... | collective-permute-start | bytes 270344 | tf_op jit(solution)/shard_map/ppermute | solution.py:222
  33.8 0.0 collective-permute-start.12
  33.8 3.4 %collective-permute-done.14.refs_3_ = bf16[32,1408]{1,0:T(8,128)(2,1)S(1)} collective-permute-done((bf16[32,1408]{1,0:T(8,128)(2,1)S(1)}, bf16[32,1408]{1,0:T(8,128)(2,1)S(1)}, u32[]{:S(2)}, u32[]{:S(2)}) %collective-permute-start.14) | collective-permute-done | bytes 90144 | tf_op jit(solution)/shard_map/ppermute | solution.py:222
  37.1 0.0 collective-permute-done.13.refs_2_
  37.1 0.0 collective-permute-done.12.refs_1_
  37.1 0.0 copy-done
  37.1 0.0 copy-done.1
  37.1 1.3 %shard_map.92 = (bf16[1024,256]{1,0:T(8,128)(2,1)}, f32[256,256]{1,0:T(8,128)}, f32[1,256]{1,0:T(1,128)}) custom-call(bf16[1040,256]{1,0:T(8,128)(2,1)S(1)} %get-tuple-element.15.refs_0_.merged, f32[256,256]{1,0:T(8,128)S(1)} %bitcast.9, f32[1,256]{1,0:T(1,128)S(1)} %copy-done.1, bf16[32,1408]{1,0:T(8,128)(2,1)S(1)} %shard_map.91.refs_0_, ...), custom_call_target="tpu_custom_call" | custom-call | flops 33554432 | bytes 1943552 | tf_op jit(solution)/shard_map/pallas_call | solution.py:27
  (7 shorter events, 0.1 us)
Async XLA Ops:
  2.1 5.2 %collective-permute-start.2 = (f32[32,1024]{1,0:T(8,128)S(1)}, f32[32,1024]{1,0:T(8,128)S(1)}, u32[]{:S(2)}, u32[]{:S(2)}) collective-permute-start(f32[32,1024]{1,0:T(8,128)S(1)} %get-tuple-element.14.refs_0_), channel_id=1, source_target_pairs={{24,8},{1,17},{0,1},{8,9},{17,16},{25,24},{9,0},{16,25},{26,10},{3... | collective-permute-start | bytes 393224 | tf_op jit(solution)/shard_map/ppermute | solution.py:222
  2.7 4.7 %collective-permute-start.1 = (f32[32,1024]{1,0:T(8,128)S(1)}, f32[32,1024]{1,0:T(8,128)S(1)}, u32[]{:S(2)}, u32[]{:S(2)}) collective-permute-start(f32[32,1024]{1,0:T(8,128)S(1)} %get-tuple-element.14.refs_0_), channel_id=1, source_target_pairs={{16,8},{9,17},{0,1},{1,0},{8,9},{17,16},{24,25},{25,24},{18,10},{1... | collective-permute-start | bytes 393224 | tf_op jit(solution)/shard_map/ppermute | solution.py:222
  5.8 3.2 %collective-permute-start = (f32[32,1024]{1,0:T(8,128)S(1)}, f32[32,1024]{1,0:T(8,128)S(1)}, u32[]{:S(2)}, u32[]{:S(2)}) collective-permute-start(f32[32,1024]{1,0:T(8,128)S(1)} %get-tuple-element.14.refs_0_), channel_id=1, source_target_pairs={{0,8},{25,17},{1,0},{8,9},{17,16},{24,25},{9,1},{16,24},{2,10},{27... | collective-permute-start | bytes 393224 | tf_op jit(solution)/shard_map/ppermute | solution.py:222
  5.8 11.0 %collective-permute-start.6 = (bf16[1040,256]{1,0:T(8,128)(2,1)S(1)}, bf16[1040,256]{1,0:T(8,128)(2,1)S(1)}, u32[]{:S(2)}, u32[]{:S(2)}) collective-permute-start(bf16[1040,256]{1,0:T(8,128)(2,1)S(1)} %get-tuple-element.15.refs_0_.merged), channel_id=1, source_target_pairs={{0,8},{25,17},{1,0},{8,9},{17,16},{24,25},{9,1},{16,24},{2,10},{27... | collective-permute-start | bytes 1597448 | tf_op jit(solution)/shard_map/ppermute | solution.py:222
  7.0 9.8 %collective-permute-start.5 = (bf16[1040,256]{1,0:T(8,128)(2,1)S(1)}, bf16[1040,256]{1,0:T(8,128)(2,1)S(1)}, u32[]{:S(2)}, u32[]{:S(2)}) collective-permute-start(bf16[1040,256]{1,0:T(8,128)(2,1)S(1)} %get-tuple-element.15.refs_0_.merged), channel_id=1, source_target_pairs={{16,8},{9,17},{0,1},{1,0},{8,9},{17,16},{24,25},{25,24},{18,10},{1... | collective-permute-start | bytes 1597448 | tf_op jit(solution)/shard_map/ppermute | solution.py:222
  9.0 12.2 %collective-permute-start.7 = (bf16[1040,256]{1,0:T(8,128)(2,1)S(1)}, bf16[1040,256]{1,0:T(8,128)(2,1)S(1)}, u32[]{:S(2)}, u32[]{:S(2)}) collective-permute-start(bf16[1040,256]{1,0:T(8,128)(2,1)S(1)} %get-tuple-element.15.refs_0_.merged), channel_id=1, source_target_pairs={{24,8},{1,17},{0,1},{8,9},{17,16},{25,24},{9,0},{16,25},{26,10},{3... | collective-permute-start | bytes 1597448 | tf_op jit(solution)/shard_map/ppermute | solution.py:222
  9.7 3.4 %collective-permute-start.3 = (f32[32,1024]{1,0:T(8,128)S(1)}, f32[32,1024]{1,0:T(8,128)S(1)}, u32[]{:S(2)}, u32[]{:S(2)}) collective-permute-start(f32[32,1024]{1,0:T(8,128)S(1)} %shard_map.86), channel_id=1, source_target_pairs={{8,10},{10,8},{12,14},{14,12},{9,11},{11,9},{13,15},{15,13},{16,18... | collective-permute-start | bytes 393224 | tf_op jit(solution)/shard_map/ppermute | solution.py:231
  13.1 1.4 %collective-permute-start.4 = (f32[32,1024]{1,0:T(8,128)S(1)}, f32[32,1024]{1,0:T(8,128)S(1)}, u32[]{:S(2)}, u32[]{:S(2)}) collective-permute-start(f32[32,1024]{1,0:T(8,128)S(1)} %add.3.refs_0_), channel_id=1, source_target_pairs={{8,12},{10,14},{12,8},{14,10},{9,13},{11,15},{13,9},{15,11},{16,20... | collective-permute-start | bytes 393224 | tf_op jit(solution)/shard_map/ppermute | solution.py:231
  21.2 4.4 %collective-permute-start.10 = (f32[32,1024]{1,0:T(8,128)S(1)}, f32[32,1024]{1,0:T(8,128)S(1)}, u32[]{:S(2)}, u32[]{:S(2)}) collective-permute-start(f32[32,1024]{1,0:T(8,128)S(1)} %get-tuple-element.16.refs_0_), channel_id=1, source_target_pairs={{8,15},{9,0},{0,1},{1,8},{10,13},{11,2},{2,3},{3,10},{12,11},{13,4... | collective-permute-start | bytes 393224 | tf_op jit(solution)/shard_map/ppermute | solution.py:248
  21.2 5.0 %collective-permute-start.9 = (f32[32,1024]{1,0:T(8,128)S(1)}, f32[32,1024]{1,0:T(8,128)S(1)}, u32[]{:S(2)}, u32[]{:S(2)}) collective-permute-start(f32[32,1024]{1,0:T(8,128)S(1)} %get-tuple-element.16.refs_0_), channel_id=1, source_target_pairs={{8,13},{9,8},{0,1},{1,0},{10,15},{11,10},{2,3},{3,2},{12,9},{13,12... | collective-permute-start | bytes 393224 | tf_op jit(solution)/shard_map/ppermute | solution.py:248
  25.2 1.3 %collective-permute-start.8 = (f32[32,1024]{1,0:T(8,128)S(1)}, f32[32,1024]{1,0:T(8,128)S(1)}, u32[]{:S(2)}, u32[]{:S(2)}) collective-permute-start(f32[32,1024]{1,0:T(8,128)S(1)} %get-tuple-element.16.refs_0_), channel_id=1, source_target_pairs={{8,11},{9,8},{0,1},{1,0},{10,9},{11,10},{2,3},{3,2},{12,15},{13,12... | collective-permute-start | bytes 393224 | tf_op jit(solution)/shard_map/ppermute | solution.py:248
  26.6 1.7 %collective-permute-start.11 = (f32[32,1024]{1,0:T(8,128)S(1)}, f32[32,1024]{1,0:T(8,128)S(1)}, u32[]{:S(2)}, u32[]{:S(2)}) collective-permute-start(f32[32,1024]{1,0:T(8,128)S(1)} %shard_map.89), channel_id=1, source_target_pairs={{0,1},{1,0},{2,3},{3,2},{4,5},{5,4},{6,7},{7,6},{8,9},{9,8},{10,11... | collective-permute-start | bytes 393224 | tf_op jit(solution)/shard_map/ppermute | solution.py:292
  28.2 8.9 %copy-start = (f32[1,256,256]{2,1,0:T(8,128)S(1)}, f32[1,256,256]{2,1,0:T(8,128)}, u32[]{:S(2)}) copy-start(f32[1,256,256]{2,1,0:T(8,128)} %param.9) | copy-start | bytes 786436
  28.2 8.9 %copy-start.1 = (f32[1,256]{1,0:T(1,128)S(1)}, f32[1,256]{1,0:T(1,128)}, u32[]{:S(2)}) copy-start(f32[1,256]{1,0:T(1,128)} %vec_momentum.1) | copy-start | bytes 3076
  28.3 8.9 %collective-permute-start.14 = (bf16[32,1408]{1,0:T(8,128)(2,1)S(1)}, bf16[32,1408]{1,0:T(8,128)(2,1)S(1)}, u32[]{:S(2)}, u32[]{:S(2)}) collective-permute-start(bf16[32,1408]{1,0:T(8,128)(2,1)S(1)} %shard_map.91.refs_0_), channel_id=1, source_target_pairs={{8,0},{17,25},{0,1},{9,8},{16,17},{25,24},{1,9},{24,16},{10,2},{19... | collective-permute-start | bytes 270344 | tf_op jit(solution)/shard_map/ppermute | solution.py:222
  28.6 8.5 %collective-permute-start.13 = (bf16[32,1408]{1,0:T(8,128)(2,1)S(1)}, bf16[32,1408]{1,0:T(8,128)(2,1)S(1)}, u32[]{:S(2)}, u32[]{:S(2)}) collective-permute-start(bf16[32,1408]{1,0:T(8,128)(2,1)S(1)} %shard_map.91.refs_0_), channel_id=1, source_target_pairs={{8,24},{17,1},{1,0},{9,8},{16,17},{24,25},{0,9},{25,16},{10,26},{1... | collective-permute-start | bytes 270344 | tf_op jit(solution)/shard_map/ppermute | solution.py:222
  33.8 3.4 %collective-permute-start.12 = (bf16[32,1408]{1,0:T(8,128)(2,1)S(1)}, bf16[32,1408]{1,0:T(8,128)(2,1)S(1)}, u32[]{:S(2)}, u32[]{:S(2)}) collective-permute-start(bf16[32,1408]{1,0:T(8,128)(2,1)S(1)} %shard_map.91.refs_0_), channel_id=1, source_target_pairs={{8,16},{17,9},{1,0},{0,1},{9,8},{16,17},{25,24},{24,25},{10,18},{1... | collective-permute-start | bytes 270344 | tf_op jit(solution)/shard_map/ppermute | solution.py:222

commit v8 on v7

--- a/solution.py
+++ b/solution.py
@@ -80,13 +80,11 @@
         ]
         for i in range(CHUNKS_IN)
     ]
-    for copy in small + sum(large, []):
+    for copy in large[0] + small + sum(large[1:], []):
         copy.start()
     for copy in small:
         copy.wait()
     q_lo = q_in[...].astype(BF16)
-    parts = three_parts(vec_in[...])
-    merged[rows:, :] = jnp.concatenate([*parts, jnp.zeros((PAD - 3, cols), F32)], axis=0).astype(BF16)
     for i in range(CHUNKS_IN):
         for copy in large[i]:
             copy.wait()
@@ -94,6 +92,8 @@
         total = (grads_in[here, :].astype(F32) + errors_in[here, :].astype(F32)).astype(BF16)
         merged[here, :] = total
         p_part[:, here] = dot(q_lo, total, 1, 1)
+    parts = three_parts(vec_in[...])
+    merged[rows:, :] = jnp.concatenate([*parts, jnp.zeros((PAD - 3, cols), F32)], axis=0).astype(BF16)
 
 
 def add_kernel(*refs):
@@ -148,19 +148,19 @@
 
 
 def final_kernel(sources, merged, momentum, vec_momentum, *refs):
-    packs = refs[:-9]
-    new_errors, new_momentum, new_vec, rest, p_rows, errors_out, momentum_out, vec_out, sems = refs[-9:]
+    packs = refs[:-10]
+    new_errors, new_momentum, new_vec, rest, left, p_rows, errors_out, momentum_out, vec_out, sems = refs[-10:]
     rows, cols = new_errors.shape
     own_rows = momentum.shape[0]
     z, s = lax.axis_index("replica"), lax.axis_index("section")
     came = sum(
-        jnp.where((z == row[j]) & (s == i), (0, 1, 2)[j] + 1, 0) for i, row in enumerate(sources) for j in range(len(row))
+        jnp.where((z == row[j]) & (s == i), (0, 2, 1)[j] + 1, 0) for i, row in enumerate(sources) for j in range(len(row))
     )
     for i, pack in enumerate(packs):
 
         @pl.when(came == i)
         def _(pack=pack):
-            p_rows[...] = pack[:, :rows].T
+            left[...] = pack[:, :rows]
             rest[...] = pack[:, rows:]
 
     q_lo = rest[:, :cols]
@@ -168,6 +168,7 @@
     step = rows // CHUNKS_OUT
     for i in range(CHUNKS_OUT):
         here = pl.ds(i * step, step)
+        p_rows[here, :] = left[:, i * step : (i + 1) * step].T
         approx = dot(p_rows[here, :], q_lo, 1, 0)
         errors_out[here, :] = (merged[here, :].astype(F32) - approx).astype(BF16)
         copies.append(pltpu.make_async_copy(errors_out.at[here], new_errors.at[here], sems.at[i]))
@@ -310,11 +311,12 @@
         momentum[0],
         vec_momentum,
         whole,
-        *(received[i] for i in (0, 1, 2)),
+        *(received[i] for i in (0, 2, 1)),
         flops=2 * work,
         out_specs=[HBM] * 3,
         scratch=[
             pltpu.VMEM((rank, cols + LANES), BF16),
+            pltpu.VMEM((rank, rows), BF16),
             pltpu.VMEM((rows, rank), BF16),
             pltpu.VMEM(block, BF16),
             pltpu.VMEM(momentum.shape[1:], F32),

time: 38.6 us -> 37.8 us (0.979)
  waiting for transfers between devices: 16.3 us -> 15.5 us
    ppermute x9, waiting for transfers between devices: 12 us -> 11.2 us  [along(): lax.ppermute(x, ('replica', 'section'), [(number(a), number(b)) for a, b...]
  transfers between devices with their start and end apart: 15 -> 15, of which waited for: 11 -> 12; matrix products, arithmetic and copies ran while one was open for 0% -> 0% of each run, Pallas kernels for 0% -> 0%
where the time goes in v8:
time: 37.8 us; the launch traced here: 37.6 us
  starting transfers between devices  18.7 us (49%)
  waiting for transfers between devices  15.5 us (41%)
  Pallas kernels  2.76 us (7%)
  between operations  0.67 us (2%)
    ppermute x9, starting transfers between devices, along(): lax.ppermute(x, ('replica', 'section'), [(number(a), number(b)) for a, b...  11.2 us
    ppermute x9, waiting for transfers between devices, along(): lax.ppermute(x, ('replica', 'section'), [(number(a), number(b)) for a, b...  11.2 us
    ppermute x3, starting transfers between devices, to_mates(): lax.ppermute(x, ('replica', 'tensor', 'section'), [(device(a), device(b))...  4 us
    ppermute x2, starting transfers between devices, across(): parts.append(lax.ppermute(x, ('replica', 'tensor', 'section'), order))  2.85 us
    pallas_call x8, Pallas kernels, call(): pl.pallas_call(kernel, out_shape=outs, in_specs=in_specs or [VMEM] * len(...  2.76 us
    ppermute x2, waiting for transfers between devices, across(): parts.append(lax.ppermute(x, ('replica', 'tensor', 'section'), order))  1.97 us
    ppermute x3, waiting for transfers between devices, to_mates(): lax.ppermute(x, ('replica', 'tensor', 'section'), [(device(a), device(b))...  1.34 us
    ppermute x1, waiting for transfers between devices, gathered(): lax.ppermute(p_other, 'section', [(s, sections - 1 - s) for s in range(se...  0.99 us
  transfers between devices with their start and end apart: 15, of which 12 were waited for; matrix products, arithmetic and copies ran while one was open for 0% of the time, Pallas kernels for 0%

profile of v8, /device:TPU:0, one launch (start us, length us, event | category | flops | bytes accessed | tf_op | source)
XLA Modules:
  0.0 37.6 jit_solution(6320717960304609057)
XLA Ops:
  0.6 1.5 %shard_map.85 = (bf16[1040,256]{1,0:T(8,128)(2,1)S(1)}, f32[32,1024]{1,0:T(8,128)S(1)}) custom-call(bf16[1024,256]{1,0:T(8,128)(2,1)} %bitcast.10, bf16[1024,256]{1,0:T(8,128)(2,1)} %bitcast.11, f32[32,256]{1,0:T(8,128)} %bitcast.12, f32[1,256]{1,0:T(1,128)} %bitcast.13), custom_call_target="tpu_custom_call" | custom-call | flops 16777216 | bytes 1745920 | tf_op jit(solution)/shard_map/pallas_call | solution.py:27
  2.1 0.5 %collective-permute-start.2 = (f32[32,1024]{1,0:T(8,128)S(1)}, f32[32,1024]{1,0:T(8,128)S(1)}, u32[]{:S(2)}, u32[]{:S(2)}) collective-permute-start(f32[32,1024]{1,0:T(8,128)S(1)} %get-tuple-element.14.refs_0_), channel_id=1, source_target_pairs={{24,8},{1,17},{0,1},{8,9},{17,16},{25,24},{9,0},{16,25},{26,10},{3... | collective-permute-start | bytes 393224 | tf_op jit(solution)/shard_map/ppermute | solution.py:223
  2.6 3.1 %collective-permute-start.1 = (f32[32,1024]{1,0:T(8,128)S(1)}, f32[32,1024]{1,0:T(8,128)S(1)}, u32[]{:S(2)}, u32[]{:S(2)}) collective-permute-start(f32[32,1024]{1,0:T(8,128)S(1)} %get-tuple-element.14.refs_0_), channel_id=1, source_target_pairs={{16,8},{9,17},{0,1},{1,0},{8,9},{17,16},{24,25},{25,24},{18,10},{1... | collective-permute-start | bytes 393224 | tf_op jit(solution)/shard_map/ppermute | solution.py:223
  5.8 0.0 collective-permute-start
  5.8 1.2 %collective-permute-start.6 = (bf16[1040,256]{1,0:T(8,128)(2,1)S(1)}, bf16[1040,256]{1,0:T(8,128)(2,1)S(1)}, u32[]{:S(2)}, u32[]{:S(2)}) collective-permute-start(bf16[1040,256]{1,0:T(8,128)(2,1)S(1)} %get-tuple-element.15.refs_0_.merged), channel_id=1, source_target_pairs={{0,8},{25,17},{1,0},{8,9},{17,16},{24,25},{9,1},{16,24},{2,10},{27... | collective-permute-start | bytes 1597448 | tf_op jit(solution)/shard_map/ppermute | solution.py:223
  7.0 0.0 collective-permute-start.5
  7.0 0.3 collective-permute-done.2.refs_3_
  7.3 0.0 collective-permute-done.1.refs_2_
  7.3 1.7 %collective-permute-done.refs_1_ = f32[32,1024]{1,0:T(8,128)S(1)} collective-permute-done((f32[32,1024]{1,0:T(8,128)S(1)}, f32[32,1024]{1,0:T(8,128)S(1)}, u32[]{:S(2)}, u32[]{:S(2)}) %collective-permute-start) | collective-permute-done | bytes 131104 | tf_op jit(solution)/shard_map/ppermute | solution.py:223
  9.0 0.7 %collective-permute-start.7 = (bf16[1040,256]{1,0:T(8,128)(2,1)S(1)}, bf16[1040,256]{1,0:T(8,128)(2,1)S(1)}, u32[]{:S(2)}, u32[]{:S(2)}) collective-permute-start(bf16[1040,256]{1,0:T(8,128)(2,1)S(1)} %get-tuple-element.15.refs_0_.merged), channel_id=1, source_target_pairs={{24,8},{1,17},{0,1},{8,9},{17,16},{25,24},{9,0},{16,25},{26,10},{3... | collective-permute-start | bytes 1597448 | tf_op jit(solution)/shard_map/ppermute | solution.py:223
  9.7 2.4 %collective-permute-start.3 = (f32[32,1024]{1,0:T(8,128)S(1)}, f32[32,1024]{1,0:T(8,128)S(1)}, u32[]{:S(2)}, u32[]{:S(2)}) collective-permute-start(f32[32,1024]{1,0:T(8,128)S(1)} %shard_map.86), channel_id=1, source_target_pairs={{8,10},{10,8},{12,14},{14,12},{9,11},{11,9},{13,15},{15,13},{16,18... | collective-permute-start | bytes 393224 | tf_op jit(solution)/shard_map/ppermute | solution.py:232
  12.1 1.0 %collective-permute-done.3 = f32[32,1024]{1,0:T(8,128)S(1)} collective-permute-done((f32[32,1024]{1,0:T(8,128)S(1)}, f32[32,1024]{1,0:T(8,128)S(1)}, u32[]{:S(2)}, u32[]{:S(2)}) %collective-permute-start.3) | collective-permute-done | bytes 131104 | tf_op jit(solution)/shard_map/ppermute | solution.py:232
  13.1 0.4 %collective-permute-start.4 = (f32[32,1024]{1,0:T(8,128)S(1)}, f32[32,1024]{1,0:T(8,128)S(1)}, u32[]{:S(2)}, u32[]{:S(2)}) collective-permute-start(f32[32,1024]{1,0:T(8,128)S(1)} %add.3.refs_0_), channel_id=1, source_target_pairs={{8,12},{10,14},{12,8},{14,10},{9,13},{11,15},{13,9},{15,11},{16,20... | collective-permute-start | bytes 393224 | tf_op jit(solution)/shard_map/ppermute | solution.py:232
  13.5 1.0 %collective-permute-done.4.refs_1_ = f32[32,1024]{1,0:T(8,128)S(1)} collective-permute-done((f32[32,1024]{1,0:T(8,128)S(1)}, f32[32,1024]{1,0:T(8,128)S(1)}, u32[]{:S(2)}, u32[]{:S(2)}) %collective-permute-start.4) | collective-permute-done | bytes 131104 | tf_op jit(solution)/shard_map/ppermute | solution.py:232
  14.5 2.3 %collective-permute-done.6.refs_2_ = bf16[1040,256]{1,0:T(8,128)(2,1)S(1)} collective-permute-done((bf16[1040,256]{1,0:T(8,128)(2,1)S(1)}, bf16[1040,256]{1,0:T(8,128)(2,1)S(1)}, u32[]{:S(2)}, u32[]{:S(2)}) %collective-permute-start.6) | collective-permute-done | bytes 532512 | tf_op jit(solution)/shard_map/ppermute | solution.py:223
  16.8 0.0 collective-permute-done.5.refs_1_
  16.8 4.4 %collective-permute-done.7.refs_3_ = bf16[1040,256]{1,0:T(8,128)(2,1)S(1)} collective-permute-done((bf16[1040,256]{1,0:T(8,128)(2,1)S(1)}, bf16[1040,256]{1,0:T(8,128)(2,1)S(1)}, u32[]{:S(2)}, u32[]{:S(2)}) %collective-permute-start.7) | collective-permute-done | bytes 532512 | tf_op jit(solution)/shard_map/ppermute | solution.py:223
  21.2 0.0 collective-permute-start.10
  21.2 4.0 %collective-permute-start.9 = (f32[32,1024]{1,0:T(8,128)S(1)}, f32[32,1024]{1,0:T(8,128)S(1)}, u32[]{:S(2)}, u32[]{:S(2)}) collective-permute-start(f32[32,1024]{1,0:T(8,128)S(1)} %get-tuple-element.16.refs_0_), channel_id=1, source_target_pairs={{8,13},{9,8},{0,1},{1,0},{10,15},{11,10},{2,3},{3,2},{12,9},{13,12... | collective-permute-start | bytes 393224 | tf_op jit(solution)/shard_map/ppermute | solution.py:249
  25.2 0.0 collective-permute-start.8
  25.2 0.4 %collective-permute-done.10.refs_2_ = f32[32,1024]{1,0:T(8,128)S(1)} collective-permute-done((f32[32,1024]{1,0:T(8,128)S(1)}, f32[32,1024]{1,0:T(8,128)S(1)}, u32[]{:S(2)}, u32[]{:S(2)}) %collective-permute-start.10) | collective-permute-done | bytes 131104 | tf_op jit(solution)/shard_map/ppermute | solution.py:249
  25.6 0.6 %collective-permute-done.9.refs_1_ = f32[32,1024]{1,0:T(8,128)S(1)} collective-permute-done((f32[32,1024]{1,0:T(8,128)S(1)}, f32[32,1024]{1,0:T(8,128)S(1)}, u32[]{:S(2)}, u32[]{:S(2)}) %collective-permute-start.9) | collective-permute-done | bytes 131104 | tf_op jit(solution)/shard_map/ppermute | solution.py:249
  26.2 0.4 collective-permute-done.8.refs_0_
  26.6 0.7 %collective-permute-start.11 = (f32[32,1024]{1,0:T(8,128)S(1)}, f32[32,1024]{1,0:T(8,128)S(1)}, u32[]{:S(2)}, u32[]{:S(2)}) collective-permute-start(f32[32,1024]{1,0:T(8,128)S(1)} %shard_map.89), channel_id=1, source_target_pairs={{0,1},{1,0},{2,3},{3,2},{4,5},{5,4},{6,7},{7,6},{8,9},{9,8},{10,11... | collective-permute-start | bytes 393224 | tf_op jit(solution)/shard_map/ppermute | solution.py:293
  27.2 1.0 %collective-permute-done.11.refs_1_ = f32[32,1024]{1,0:T(8,128)S(1)} collective-permute-done((f32[32,1024]{1,0:T(8,128)S(1)}, f32[32,1024]{1,0:T(8,128)S(1)}, u32[]{:S(2)}, u32[]{:S(2)}) %collective-permute-start.11) | collective-permute-done | bytes 131104 | tf_op jit(solution)/shard_map/ppermute | solution.py:293
  28.2 0.0 copy-start
  28.2 0.0 copy-start.1
  28.2 3.6 %collective-permute-start.14 = (bf16[32,1408]{1,0:T(8,128)(2,1)S(1)}, bf16[32,1408]{1,0:T(8,128)(2,1)S(1)}, u32[]{:S(2)}, u32[]{:S(2)}) collective-permute-start(bf16[32,1408]{1,0:T(8,128)(2,1)S(1)} %shard_map.91.refs_0_), channel_id=1, source_target_pairs={{8,24},{17,1},{1,0},{9,8},{16,17},{24,25},{0,9},{25,16},{10,26},{1... | collective-permute-start | bytes 270344 | tf_op jit(solution)/shard_map/ppermute | solution.py:223
  31.9 0.0 collective-permute-start.13
  31.9 2.0 %collective-permute-start.12 = (bf16[32,1408]{1,0:T(8,128)(2,1)S(1)}, bf16[32,1408]{1,0:T(8,128)(2,1)S(1)}, u32[]{:S(2)}, u32[]{:S(2)}) collective-permute-start(bf16[32,1408]{1,0:T(8,128)(2,1)S(1)} %shard_map.91.refs_0_), channel_id=1, source_target_pairs={{8,16},{17,9},{1,0},{0,1},{9,8},{16,17},{25,24},{24,25},{10,18},{1... | collective-permute-start | bytes 270344 | tf_op jit(solution)/shard_map/ppermute | solution.py:223
  33.8 0.2 collective-permute-done.14.refs_3_
  34.0 2.4 %collective-permute-done.13.refs_2_ = bf16[32,1408]{1,0:T(8,128)(2,1)S(1)} collective-permute-done((bf16[32,1408]{1,0:T(8,128)(2,1)S(1)}, bf16[32,1408]{1,0:T(8,128)(2,1)S(1)}, u32[]{:S(2)}, u32[]{:S(2)}) %collective-permute-start.13) | collective-permute-done | bytes 90144 | tf_op jit(solution)/shard_map/ppermute | solution.py:223
  36.4 0.0 collective-permute-done.12.refs_1_
  36.4 0.0 copy-done
  36.4 0.0 copy-done.1
  36.4 1.2 %shard_map.92 = (bf16[1024,256]{1,0:T(8,128)(2,1)}, f32[256,256]{1,0:T(8,128)}, f32[1,256]{1,0:T(1,128)}) custom-call(bf16[1040,256]{1,0:T(8,128)(2,1)S(1)} %get-tuple-element.15.refs_0_.merged, f32[256,256]{1,0:T(8,128)S(1)} %bitcast.9, f32[1,256]{1,0:T(1,128)S(1)} %copy-done.1, bf16[32,1408]{1,0:T(8,128)(2,1)S(1)} %shard_map.91.refs_0_, ...), custom_call_target="tpu_custom_call" | custom-call | flops 33554432 | bytes 1943552 | tf_op jit(solution)/shard_map/pallas_call | solution.py:27
  (7 shorter events, 0.1 us)
Async XLA Ops:
  2.1 5.2 %collective-permute-start.2 = (f32[32,1024]{1,0:T(8,128)S(1)}, f32[32,1024]{1,0:T(8,128)S(1)}, u32[]{:S(2)}, u32[]{:S(2)}) collective-permute-start(f32[32,1024]{1,0:T(8,128)S(1)} %get-tuple-element.14.refs_0_), channel_id=1, source_target_pairs={{24,8},{1,17},{0,1},{8,9},{17,16},{25,24},{9,0},{16,25},{26,10},{3... | collective-permute-start | bytes 393224 | tf_op jit(solution)/shard_map/ppermute | solution.py:223
  2.6 4.7 %collective-permute-start.1 = (f32[32,1024]{1,0:T(8,128)S(1)}, f32[32,1024]{1,0:T(8,128)S(1)}, u32[]{:S(2)}, u32[]{:S(2)}) collective-permute-start(f32[32,1024]{1,0:T(8,128)S(1)} %get-tuple-element.14.refs_0_), channel_id=1, source_target_pairs={{16,8},{9,17},{0,1},{1,0},{8,9},{17,16},{24,25},{25,24},{18,10},{1... | collective-permute-start | bytes 393224 | tf_op jit(solution)/shard_map/ppermute | solution.py:223
  5.8 3.2 %collective-permute-start = (f32[32,1024]{1,0:T(8,128)S(1)}, f32[32,1024]{1,0:T(8,128)S(1)}, u32[]{:S(2)}, u32[]{:S(2)}) collective-permute-start(f32[32,1024]{1,0:T(8,128)S(1)} %get-tuple-element.14.refs_0_), channel_id=1, source_target_pairs={{0,8},{25,17},{1,0},{8,9},{17,16},{24,25},{9,1},{16,24},{2,10},{27... | collective-permute-start | bytes 393224 | tf_op jit(solution)/shard_map/ppermute | solution.py:223
  5.8 11.0 %collective-permute-start.6 = (bf16[1040,256]{1,0:T(8,128)(2,1)S(1)}, bf16[1040,256]{1,0:T(8,128)(2,1)S(1)}, u32[]{:S(2)}, u32[]{:S(2)}) collective-permute-start(bf16[1040,256]{1,0:T(8,128)(2,1)S(1)} %get-tuple-element.15.refs_0_.merged), channel_id=1, source_target_pairs={{0,8},{25,17},{1,0},{8,9},{17,16},{24,25},{9,1},{16,24},{2,10},{27... | collective-permute-start | bytes 1597448 | tf_op jit(solution)/shard_map/ppermute | solution.py:223
  7.0 9.8 %collective-permute-start.5 = (bf16[1040,256]{1,0:T(8,128)(2,1)S(1)}, bf16[1040,256]{1,0:T(8,128)(2,1)S(1)}, u32[]{:S(2)}, u32[]{:S(2)}) collective-permute-start(bf16[1040,256]{1,0:T(8,128)(2,1)S(1)} %get-tuple-element.15.refs_0_.merged), channel_id=1, source_target_pairs={{16,8},{9,17},{0,1},{1,0},{8,9},{17,16},{24,25},{25,24},{18,10},{1... | collective-permute-start | bytes 1597448 | tf_op jit(solution)/shard_map/ppermute | solution.py:223
  9.0 12.2 %collective-permute-start.7 = (bf16[1040,256]{1,0:T(8,128)(2,1)S(1)}, bf16[1040,256]{1,0:T(8,128)(2,1)S(1)}, u32[]{:S(2)}, u32[]{:S(2)}) collective-permute-start(bf16[1040,256]{1,0:T(8,128)(2,1)S(1)} %get-tuple-element.15.refs_0_.merged), channel_id=1, source_target_pairs={{24,8},{1,17},{0,1},{8,9},{17,16},{25,24},{9,0},{16,25},{26,10},{3... | collective-permute-start | bytes 1597448 | tf_op jit(solution)/shard_map/ppermute | solution.py:223
  9.7 3.4 %collective-permute-start.3 = (f32[32,1024]{1,0:T(8,128)S(1)}, f32[32,1024]{1,0:T(8,128)S(1)}, u32[]{:S(2)}, u32[]{:S(2)}) collective-permute-start(f32[32,1024]{1,0:T(8,128)S(1)} %shard_map.86), channel_id=1, source_target_pairs={{8,10},{10,8},{12,14},{14,12},{9,11},{11,9},{13,15},{15,13},{16,18... | collective-permute-start | bytes 393224 | tf_op jit(solution)/shard_map/ppermute | solution.py:232
  13.1 1.4 %collective-permute-start.4 = (f32[32,1024]{1,0:T(8,128)S(1)}, f32[32,1024]{1,0:T(8,128)S(1)}, u32[]{:S(2)}, u32[]{:S(2)}) collective-permute-start(f32[32,1024]{1,0:T(8,128)S(1)} %add.3.refs_0_), channel_id=1, source_target_pairs={{8,12},{10,14},{12,8},{14,10},{9,13},{11,15},{13,9},{15,11},{16,20... | collective-permute-start | bytes 393224 | tf_op jit(solution)/shard_map/ppermute | solution.py:232
  21.2 4.4 %collective-permute-start.10 = (f32[32,1024]{1,0:T(8,128)S(1)}, f32[32,1024]{1,0:T(8,128)S(1)}, u32[]{:S(2)}, u32[]{:S(2)}) collective-permute-start(f32[32,1024]{1,0:T(8,128)S(1)} %get-tuple-element.16.refs_0_), channel_id=1, source_target_pairs={{8,15},{9,0},{0,1},{1,8},{10,13},{11,2},{2,3},{3,10},{12,11},{13,4... | collective-permute-start | bytes 393224 | tf_op jit(solution)/shard_map/ppermute | solution.py:249
  21.2 5.0 %collective-permute-start.9 = (f32[32,1024]{1,0:T(8,128)S(1)}, f32[32,1024]{1,0:T(8,128)S(1)}, u32[]{:S(2)}, u32[]{:S(2)}) collective-permute-start(f32[32,1024]{1,0:T(8,128)S(1)} %get-tuple-element.16.refs_0_), channel_id=1, source_target_pairs={{8,13},{9,8},{0,1},{1,0},{10,15},{11,10},{2,3},{3,2},{12,9},{13,12... | collective-permute-start | bytes 393224 | tf_op jit(solution)/shard_map/ppermute | solution.py:249
  25.2 1.3 %collective-permute-start.8 = (f32[32,1024]{1,0:T(8,128)S(1)}, f32[32,1024]{1,0:T(8,128)S(1)}, u32[]{:S(2)}, u32[]{:S(2)}) collective-permute-start(f32[32,1024]{1,0:T(8,128)S(1)} %get-tuple-element.16.refs_0_), channel_id=1, source_target_pairs={{8,11},{9,8},{0,1},{1,0},{10,9},{11,10},{2,3},{3,2},{12,15},{13,12... | collective-permute-start | bytes 393224 | tf_op jit(solution)/shard_map/ppermute | solution.py:249
  26.6 1.7 %collective-permute-start.11 = (f32[32,1024]{1,0:T(8,128)S(1)}, f32[32,1024]{1,0:T(8,128)S(1)}, u32[]{:S(2)}, u32[]{:S(2)}) collective-permute-start(f32[32,1024]{1,0:T(8,128)S(1)} %shard_map.89), channel_id=1, source_target_pairs={{0,1},{1,0},{2,3},{3,2},{4,5},{5,4},{6,7},{7,6},{8,9},{9,8},{10,11... | collective-permute-start | bytes 393224 | tf_op jit(solution)/shard_map/ppermute | solution.py:293
  28.2 8.2 %copy-start = (f32[1,256,256]{2,1,0:T(8,128)S(1)}, f32[1,256,256]{2,1,0:T(8,128)}, u32[]{:S(2)}) copy-start(f32[1,256,256]{2,1,0:T(8,128)} %param.9) | copy-start | bytes 786436
  28.2 8.2 %copy-start.1 = (f32[1,256]{1,0:T(1,128)S(1)}, f32[1,256]{1,0:T(1,128)}, u32[]{:S(2)}) copy-start(f32[1,256]{1,0:T(1,128)} %vec_momentum.1) | copy-start | bytes 3076
  28.2 5.8 %collective-permute-start.14 = (bf16[32,1408]{1,0:T(8,128)(2,1)S(1)}, bf16[32,1408]{1,0:T(8,128)(2,1)S(1)}, u32[]{:S(2)}, u32[]{:S(2)}) collective-permute-start(bf16[32,1408]{1,0:T(8,128)(2,1)S(1)} %shard_map.91.refs_0_), channel_id=1, source_target_pairs={{8,24},{17,1},{1,0},{9,8},{16,17},{24,25},{0,9},{25,16},{10,26},{1... | collective-permute-start | bytes 270344 | tf_op jit(solution)/shard_map/ppermute | solution.py:223
  31.9 4.5 %collective-permute-start.13 = (bf16[32,1408]{1,0:T(8,128)(2,1)S(1)}, bf16[32,1408]{1,0:T(8,128)(2,1)S(1)}, u32[]{:S(2)}, u32[]{:S(2)}) collective-permute-start(bf16[32,1408]{1,0:T(8,128)(2,1)S(1)} %shard_map.91.refs_0_), channel_id=1, source_target_pairs={{8,0},{17,25},{0,1},{9,8},{16,17},{25,24},{1,9},{24,16},{10,2},{19... | collective-permute-start | bytes 270344 | tf_op jit(solution)/shard_map/ppermute | solution.py:223
  31.9 4.5 %collective-permute-start.12 = (bf16[32,1408]{1,0:T(8,128)(2,1)S(1)}, bf16[32,1408]{1,0:T(8,128)(2,1)S(1)}, u32[]{:S(2)}, u32[]{:S(2)}) collective-permute-start(bf16[32,1408]{1,0:T(8,128)(2,1)S(1)} %shard_map.91.refs_0_), channel_id=1, source_target_pairs={{8,16},{17,9},{1,0},{0,1},{9,8},{16,17},{25,24},{24,25},{10,18},{1... | collective-permute-start | bytes 270344 | tf_op jit(solution)/shard_map/ppermute | solution.py:223

commit v9 on v8

--- a/solution.py
+++ b/solution.py
@@ -154,7 +154,7 @@
     own_rows = momentum.shape[0]
     z, s = lax.axis_index("replica"), lax.axis_index("section")
     came = sum(
-        jnp.where((z == row[j]) & (s == i), (0, 2, 1)[j] + 1, 0) for i, row in enumerate(sources) for j in range(len(row))
+        jnp.where((z == row[j]) & (s == i), (1, 2, 0)[j] + 1, 0) for i, row in enumerate(sources) for j in range(len(row))
     )
     for i, pack in enumerate(packs):
 
@@ -215,7 +215,11 @@
     inward = [
         completed([((sources[s][j], s), (owner[s], s)) for s in range(sections)], places) for j in range(replicas - 1)
     ]
-    outward = [[(b, a) for a, b in pairs] for pairs in inward]
+    leaving = [[sources[0][0], sources[0][2], sources[0][1]], sources[1]]
+    outward = [
+        [(b, a) for a, b in completed([((leaving[s][j], s), (owner[s], s)) for s in range(sections)], places)]
+        for j in range(replicas - 1)
+    ]
     number = lambda place: place[0] * sections + place[1]
     device = lambda place: (place[0] * tensors + place[1]) * sections + place[2]
 
@@ -301,7 +305,7 @@
     )[0]
     received = along(whole, outward)
     new_errors, new_momentum, new_vec = call(
-        functools.partial(final_kernel, sources),
+        functools.partial(final_kernel, leaving),
         [
             jax.ShapeDtypeStruct(block, BF16),
             jax.ShapeDtypeStruct(momentum.shape[1:], F32),
@@ -311,7 +315,7 @@
         momentum[0],
         vec_momentum,
         whole,
-        *(received[i] for i in (0, 2, 1)),
+        *(received[i] for i in (2, 0, 1)),
         flops=2 * work,
         out_specs=[HBM] * 3,
         scratch=[

time: 37.8 us -> 37.7 us (level)
  starting transfers between devices: 18.7 us -> 17.1 us
  waiting for transfers between devices: 15.5 us -> 17 us
    ppermute x9, starting transfers between devices: 11.2 us -> 9.55 us  [along(): lax.ppermute(x, ('replica', 'section'), [(number(a), number(b)) for a, b...]
    ppermute x9, waiting for transfers between devices: 11.2 us -> 12.7 us  [along(): lax.ppermute(x, ('replica', 'section'), [(number(a), number(b)) for a, b...]
  transfers between devices with their start and end apart: 15 -> 15, of which waited for: 12 -> 11; matrix products, arithmetic and copies ran while one was open for 0% -> 0% of each run, Pallas kernels for 0% -> 0%
where the time goes in v9:
time: 37.7 us; the launch traced here: 37.6 us
  starting transfers between devices  17.1 us (45%)
  waiting for transfers between devices  17 us (45%)
  Pallas kernels  2.76 us (7%)
  between operations  0.68 us (2%)
    ppermute x9, waiting for transfers between devices, along(): lax.ppermute(x, ('replica', 'section'), [(number(a), number(b)) for a, b...  12.7 us
    ppermute x9, starting transfers between devices, along(): lax.ppermute(x, ('replica', 'section'), [(number(a), number(b)) for a, b...  9.55 us
    ppermute x3, starting transfers between devices, to_mates(): lax.ppermute(x, ('replica', 'tensor', 'section'), [(device(a), device(b))...  4 us
    ppermute x2, starting transfers between devices, across(): parts.append(lax.ppermute(x, ('replica', 'tensor', 'section'), order))  2.85 us
    pallas_call x8, Pallas kernels, call(): pl.pallas_call(kernel, out_shape=outs, in_specs=in_specs or [VMEM] * len(...  2.76 us
    ppermute x2, waiting for transfers between devices, across(): parts.append(lax.ppermute(x, ('replica', 'tensor', 'section'), order))  1.97 us
    ppermute x3, waiting for transfers between devices, to_mates(): lax.ppermute(x, ('replica', 'tensor', 'section'), [(device(a), device(b))...  1.34 us
    ppermute x1, waiting for transfers between devices, gathered(): lax.ppermute(p_other, 'section', [(s, sections - 1 - s) for s in range(se...  0.99 us
  transfers between devices with their start and end apart: 15, of which 11 were waited for; matrix products, arithmetic and copies ran while one was open for 0% of the time, Pallas kernels for 0%

profile of v9, /device:TPU:0, one launch (start us, length us, event | category | flops | bytes accessed | tf_op | source)
XLA Modules:
  0.0 37.6 jit_solution(1182949528237607761)
XLA Ops:
  0.6 1.5 %shard_map.85 = (bf16[1040,256]{1,0:T(8,128)(2,1)S(1)}, f32[32,1024]{1,0:T(8,128)S(1)}) custom-call(bf16[1024,256]{1,0:T(8,128)(2,1)} %bitcast.10, bf16[1024,256]{1,0:T(8,128)(2,1)} %bitcast.11, f32[32,256]{1,0:T(8,128)} %bitcast.12, f32[1,256]{1,0:T(1,128)} %bitcast.13), custom_call_target="tpu_custom_call" | custom-call | flops 16777216 | bytes 1745920 | tf_op jit(solution)/shard_map/pallas_call | solution.py:27
  2.1 0.5 %collective-permute-start.2 = (f32[32,1024]{1,0:T(8,128)S(1)}, f32[32,1024]{1,0:T(8,128)S(1)}, u32[]{:S(2)}, u32[]{:S(2)}) collective-permute-start(f32[32,1024]{1,0:T(8,128)S(1)} %get-tuple-element.14.refs_0_), channel_id=1, source_target_pairs={{24,8},{1,17},{0,1},{8,9},{17,16},{25,24},{9,0},{16,25},{26,10},{3... | collective-permute-start | bytes 393224 | tf_op jit(solution)/shard_map/ppermute | solution.py:227
  2.6 3.1 %collective-permute-start.1 = (f32[32,1024]{1,0:T(8,128)S(1)}, f32[32,1024]{1,0:T(8,128)S(1)}, u32[]{:S(2)}, u32[]{:S(2)}) collective-permute-start(f32[32,1024]{1,0:T(8,128)S(1)} %get-tuple-element.14.refs_0_), channel_id=1, source_target_pairs={{16,8},{9,17},{0,1},{1,0},{8,9},{17,16},{24,25},{25,24},{18,10},{1... | collective-permute-start | bytes 393224 | tf_op jit(solution)/shard_map/ppermute | solution.py:227
  5.8 0.0 collective-permute-start
  5.8 1.2 %collective-permute-start.6 = (bf16[1040,256]{1,0:T(8,128)(2,1)S(1)}, bf16[1040,256]{1,0:T(8,128)(2,1)S(1)}, u32[]{:S(2)}, u32[]{:S(2)}) collective-permute-start(bf16[1040,256]{1,0:T(8,128)(2,1)S(1)} %get-tuple-element.15.refs_0_.merged), channel_id=1, source_target_pairs={{0,8},{25,17},{1,0},{8,9},{17,16},{24,25},{9,1},{16,24},{2,10},{27... | collective-permute-start | bytes 1597448 | tf_op jit(solution)/shard_map/ppermute | solution.py:227
  7.0 0.0 collective-permute-start.5
  7.0 0.3 collective-permute-done.2.refs_3_
  7.3 0.0 collective-permute-done.1.refs_2_
  7.3 1.7 %collective-permute-done.refs_1_ = f32[32,1024]{1,0:T(8,128)S(1)} collective-permute-done((f32[32,1024]{1,0:T(8,128)S(1)}, f32[32,1024]{1,0:T(8,128)S(1)}, u32[]{:S(2)}, u32[]{:S(2)}) %collective-permute-start) | collective-permute-done | bytes 131104 | tf_op jit(solution)/shard_map/ppermute | solution.py:227
  9.0 0.7 %collective-permute-start.7 = (bf16[1040,256]{1,0:T(8,128)(2,1)S(1)}, bf16[1040,256]{1,0:T(8,128)(2,1)S(1)}, u32[]{:S(2)}, u32[]{:S(2)}) collective-permute-start(bf16[1040,256]{1,0:T(8,128)(2,1)S(1)} %get-tuple-element.15.refs_0_.merged), channel_id=1, source_target_pairs={{24,8},{1,17},{0,1},{8,9},{17,16},{25,24},{9,0},{16,25},{26,10},{3... | collective-permute-start | bytes 1597448 | tf_op jit(solution)/shard_map/ppermute | solution.py:227
  9.7 2.4 %collective-permute-start.3 = (f32[32,1024]{1,0:T(8,128)S(1)}, f32[32,1024]{1,0:T(8,128)S(1)}, u32[]{:S(2)}, u32[]{:S(2)}) collective-permute-start(f32[32,1024]{1,0:T(8,128)S(1)} %shard_map.86), channel_id=1, source_target_pairs={{8,10},{10,8},{12,14},{14,12},{9,11},{11,9},{13,15},{15,13},{16,18... | collective-permute-start | bytes 393224 | tf_op jit(solution)/shard_map/ppermute | solution.py:236
  12.1 1.0 %collective-permute-done.3 = f32[32,1024]{1,0:T(8,128)S(1)} collective-permute-done((f32[32,1024]{1,0:T(8,128)S(1)}, f32[32,1024]{1,0:T(8,128)S(1)}, u32[]{:S(2)}, u32[]{:S(2)}) %collective-permute-start.3) | collective-permute-done | bytes 131104 | tf_op jit(solution)/shard_map/ppermute | solution.py:236
  13.1 0.4 %collective-permute-start.4 = (f32[32,1024]{1,0:T(8,128)S(1)}, f32[32,1024]{1,0:T(8,128)S(1)}, u32[]{:S(2)}, u32[]{:S(2)}) collective-permute-start(f32[32,1024]{1,0:T(8,128)S(1)} %add.3.refs_0_), channel_id=1, source_target_pairs={{8,12},{10,14},{12,8},{14,10},{9,13},{11,15},{13,9},{15,11},{16,20... | collective-permute-start | bytes 393224 | tf_op jit(solution)/shard_map/ppermute | solution.py:236
  13.5 1.0 %collective-permute-done.4.refs_1_ = f32[32,1024]{1,0:T(8,128)S(1)} collective-permute-done((f32[32,1024]{1,0:T(8,128)S(1)}, f32[32,1024]{1,0:T(8,128)S(1)}, u32[]{:S(2)}, u32[]{:S(2)}) %collective-permute-start.4) | collective-permute-done | bytes 131104 | tf_op jit(solution)/shard_map/ppermute | solution.py:236
  14.5 2.3 %collective-permute-done.6.refs_2_ = bf16[1040,256]{1,0:T(8,128)(2,1)S(1)} collective-permute-done((bf16[1040,256]{1,0:T(8,128)(2,1)S(1)}, bf16[1040,256]{1,0:T(8,128)(2,1)S(1)}, u32[]{:S(2)}, u32[]{:S(2)}) %collective-permute-start.6) | collective-permute-done | bytes 532512 | tf_op jit(solution)/shard_map/ppermute | solution.py:227
  16.8 0.0 collective-permute-done.5.refs_1_
  16.8 4.4 %collective-permute-done.7.refs_3_ = bf16[1040,256]{1,0:T(8,128)(2,1)S(1)} collective-permute-done((bf16[1040,256]{1,0:T(8,128)(2,1)S(1)}, bf16[1040,256]{1,0:T(8,128)(2,1)S(1)}, u32[]{:S(2)}, u32[]{:S(2)}) %collective-permute-start.7) | collective-permute-done | bytes 532512 | tf_op jit(solution)/shard_map/ppermute | solution.py:227
  21.2 0.0 collective-permute-start.10
  21.2 4.0 %collective-permute-start.9 = (f32[32,1024]{1,0:T(8,128)S(1)}, f32[32,1024]{1,0:T(8,128)S(1)}, u32[]{:S(2)}, u32[]{:S(2)}) collective-permute-start(f32[32,1024]{1,0:T(8,128)S(1)} %get-tuple-element.16.refs_0_), channel_id=1, source_target_pairs={{8,13},{9,8},{0,1},{1,0},{10,15},{11,10},{2,3},{3,2},{12,9},{13,12... | collective-permute-start | bytes 393224 | tf_op jit(solution)/shard_map/ppermute | solution.py:253
  25.2 0.0 collective-permute-start.8
  25.2 0.4 %collective-permute-done.10.refs_2_ = f32[32,1024]{1,0:T(8,128)S(1)} collective-permute-done((f32[32,1024]{1,0:T(8,128)S(1)}, f32[32,1024]{1,0:T(8,128)S(1)}, u32[]{:S(2)}, u32[]{:S(2)}) %collective-permute-start.10) | collective-permute-done | bytes 131104 | tf_op jit(solution)/shard_map/ppermute | solution.py:253
  25.6 0.6 %collective-permute-done.9.refs_1_ = f32[32,1024]{1,0:T(8,128)S(1)} collective-permute-done((f32[32,1024]{1,0:T(8,128)S(1)}, f32[32,1024]{1,0:T(8,128)S(1)}, u32[]{:S(2)}, u32[]{:S(2)}) %collective-permute-start.9) | collective-permute-done | bytes 131104 | tf_op jit(solution)/shard_map/ppermute | solution.py:253
  26.2 0.4 collective-permute-done.8.refs_0_
  26.6 0.7 %collective-permute-start.11 = (f32[32,1024]{1,0:T(8,128)S(1)}, f32[32,1024]{1,0:T(8,128)S(1)}, u32[]{:S(2)}, u32[]{:S(2)}) collective-permute-start(f32[32,1024]{1,0:T(8,128)S(1)} %shard_map.89), channel_id=1, source_target_pairs={{0,1},{1,0},{2,3},{3,2},{4,5},{5,4},{6,7},{7,6},{8,9},{9,8},{10,11... | collective-permute-start | bytes 393224 | tf_op jit(solution)/shard_map/ppermute | solution.py:297
  27.2 1.0 %collective-permute-done.11.refs_1_ = f32[32,1024]{1,0:T(8,128)S(1)} collective-permute-done((f32[32,1024]{1,0:T(8,128)S(1)}, f32[32,1024]{1,0:T(8,128)S(1)}, u32[]{:S(2)}, u32[]{:S(2)}) %collective-permute-start.11) | collective-permute-done | bytes 131104 | tf_op jit(solution)/shard_map/ppermute | solution.py:297
  28.2 0.0 copy-start
  28.2 0.0 copy-start.1
  28.2 3.5 %collective-permute-start.14 = (bf16[32,1408]{1,0:T(8,128)(2,1)S(1)}, bf16[32,1408]{1,0:T(8,128)(2,1)S(1)}, u32[]{:S(2)}, u32[]{:S(2)}) collective-permute-start(bf16[32,1408]{1,0:T(8,128)(2,1)S(1)} %shard_map.91.refs_0_), channel_id=1, source_target_pairs={{8,0},{17,1},{9,8},{16,17},{25,24},{24,25},{1,9},{0,16},{10,2},{19... | collective-permute-start | bytes 270344 | tf_op jit(solution)/shard_map/ppermute | solution.py:227
  31.7 0.3 collective-permute-start.13
  32.0 0.2 collective-permute-start.12
  32.2 4.1 %collective-permute-done.14.refs_3_ = bf16[32,1408]{1,0:T(8,128)(2,1)S(1)} collective-permute-done((bf16[32,1408]{1,0:T(8,128)(2,1)S(1)}, bf16[32,1408]{1,0:T(8,128)(2,1)S(1)}, u32[]{:S(2)}, u32[]{:S(2)}) %collective-permute-start.14) | collective-permute-done | bytes 90144 | tf_op jit(solution)/shard_map/ppermute | solution.py:227
  36.3 0.0 collective-permute-done.13.refs_2_
  36.3 0.0 collective-permute-done.12.refs_1_
  36.3 0.0 copy-done
  36.3 0.0 copy-done.1
  36.3 1.2 %shard_map.92 = (bf16[1024,256]{1,0:T(8,128)(2,1)}, f32[256,256]{1,0:T(8,128)}, f32[1,256]{1,0:T(1,128)}) custom-call(bf16[1040,256]{1,0:T(8,128)(2,1)S(1)} %get-tuple-element.15.refs_0_.merged, f32[256,256]{1,0:T(8,128)S(1)} %bitcast.9, f32[1,256]{1,0:T(1,128)S(1)} %copy-done.1, bf16[32,1408]{1,0:T(8,128)(2,1)S(1)} %shard_map.91.refs_0_, ...), custom_call_target="tpu_custom_call" | custom-call | flops 33554432 | bytes 1943552 | tf_op jit(solution)/shard_map/pallas_call | solution.py:27
  (7 shorter events, 0.1 us)
Async XLA Ops:
  2.1 5.2 %collective-permute-start.2 = (f32[32,1024]{1,0:T(8,128)S(1)}, f32[32,1024]{1,0:T(8,128)S(1)}, u32[]{:S(2)}, u32[]{:S(2)}) collective-permute-start(f32[32,1024]{1,0:T(8,128)S(1)} %get-tuple-element.14.refs_0_), channel_id=1, source_target_pairs={{24,8},{1,17},{0,1},{8,9},{17,16},{25,24},{9,0},{16,25},{26,10},{3... | collective-permute-start | bytes 393224 | tf_op jit(solution)/shard_map/ppermute | solution.py:227
  2.6 4.7 %collective-permute-start.1 = (f32[32,1024]{1,0:T(8,128)S(1)}, f32[32,1024]{1,0:T(8,128)S(1)}, u32[]{:S(2)}, u32[]{:S(2)}) collective-permute-start(f32[32,1024]{1,0:T(8,128)S(1)} %get-tuple-element.14.refs_0_), channel_id=1, source_target_pairs={{16,8},{9,17},{0,1},{1,0},{8,9},{17,16},{24,25},{25,24},{18,10},{1... | collective-permute-start | bytes 393224 | tf_op jit(solution)/shard_map/ppermute | solution.py:227
  5.8 3.2 %collective-permute-start = (f32[32,1024]{1,0:T(8,128)S(1)}, f32[32,1024]{1,0:T(8,128)S(1)}, u32[]{:S(2)}, u32[]{:S(2)}) collective-permute-start(f32[32,1024]{1,0:T(8,128)S(1)} %get-tuple-element.14.refs_0_), channel_id=1, source_target_pairs={{0,8},{25,17},{1,0},{8,9},{17,16},{24,25},{9,1},{16,24},{2,10},{27... | collective-permute-start | bytes 393224 | tf_op jit(solution)/shard_map/ppermute | solution.py:227
  5.8 11.0 %collective-permute-start.6 = (bf16[1040,256]{1,0:T(8,128)(2,1)S(1)}, bf16[1040,256]{1,0:T(8,128)(2,1)S(1)}, u32[]{:S(2)}, u32[]{:S(2)}) collective-permute-start(bf16[1040,256]{1,0:T(8,128)(2,1)S(1)} %get-tuple-element.15.refs_0_.merged), channel_id=1, source_target_pairs={{0,8},{25,17},{1,0},{8,9},{17,16},{24,25},{9,1},{16,24},{2,10},{27... | collective-permute-start | bytes 1597448 | tf_op jit(solution)/shard_map/ppermute | solution.py:227
  7.0 9.8 %collective-permute-start.5 = (bf16[1040,256]{1,0:T(8,128)(2,1)S(1)}, bf16[1040,256]{1,0:T(8,128)(2,1)S(1)}, u32[]{:S(2)}, u32[]{:S(2)}) collective-permute-start(bf16[1040,256]{1,0:T(8,128)(2,1)S(1)} %get-tuple-element.15.refs_0_.merged), channel_id=1, source_target_pairs={{16,8},{9,17},{0,1},{1,0},{8,9},{17,16},{24,25},{25,24},{18,10},{1... | collective-permute-start | bytes 1597448 | tf_op jit(solution)/shard_map/ppermute | solution.py:227
  9.0 12.2 %collective-permute-start.7 = (bf16[1040,256]{1,0:T(8,128)(2,1)S(1)}, bf16[1040,256]{1,0:T(8,128)(2,1)S(1)}, u32[]{:S(2)}, u32[]{:S(2)}) collective-permute-start(bf16[1040,256]{1,0:T(8,128)(2,1)S(1)} %get-tuple-element.15.refs_0_.merged), channel_id=1, source_target_pairs={{24,8},{1,17},{0,1},{8,9},{17,16},{25,24},{9,0},{16,25},{26,10},{3... | collective-permute-start | bytes 1597448 | tf_op jit(solution)/shard_map/ppermute | solution.py:227
  9.7 3.4 %collective-permute-start.3 = (f32[32,1024]{1,0:T(8,128)S(1)}, f32[32,1024]{1,0:T(8,128)S(1)}, u32[]{:S(2)}, u32[]{:S(2)}) collective-permute-start(f32[32,1024]{1,0:T(8,128)S(1)} %shard_map.86), channel_id=1, source_target_pairs={{8,10},{10,8},{12,14},{14,12},{9,11},{11,9},{13,15},{15,13},{16,18... | collective-permute-start | bytes 393224 | tf_op jit(solution)/shard_map/ppermute | solution.py:236
  13.1 1.4 %collective-permute-start.4 = (f32[32,1024]{1,0:T(8,128)S(1)}, f32[32,1024]{1,0:T(8,128)S(1)}, u32[]{:S(2)}, u32[]{:S(2)}) collective-permute-start(f32[32,1024]{1,0:T(8,128)S(1)} %add.3.refs_0_), channel_id=1, source_target_pairs={{8,12},{10,14},{12,8},{14,10},{9,13},{11,15},{13,9},{15,11},{16,20... | collective-permute-start | bytes 393224 | tf_op jit(solution)/shard_map/ppermute | solution.py:236
  21.2 4.4 %collective-permute-start.10 = (f32[32,1024]{1,0:T(8,128)S(1)}, f32[32,1024]{1,0:T(8,128)S(1)}, u32[]{:S(2)}, u32[]{:S(2)}) collective-permute-start(f32[32,1024]{1,0:T(8,128)S(1)} %get-tuple-element.16.refs_0_), channel_id=1, source_target_pairs={{8,15},{9,0},{0,1},{1,8},{10,13},{11,2},{2,3},{3,10},{12,11},{13,4... | collective-permute-start | bytes 393224 | tf_op jit(solution)/shard_map/ppermute | solution.py:253
  21.2 5.0 %collective-permute-start.9 = (f32[32,1024]{1,0:T(8,128)S(1)}, f32[32,1024]{1,0:T(8,128)S(1)}, u32[]{:S(2)}, u32[]{:S(2)}) collective-permute-start(f32[32,1024]{1,0:T(8,128)S(1)} %get-tuple-element.16.refs_0_), channel_id=1, source_target_pairs={{8,13},{9,8},{0,1},{1,0},{10,15},{11,10},{2,3},{3,2},{12,9},{13,12... | collective-permute-start | bytes 393224 | tf_op jit(solution)/shard_map/ppermute | solution.py:253
  25.2 1.3 %collective-permute-start.8 = (f32[32,1024]{1,0:T(8,128)S(1)}, f32[32,1024]{1,0:T(8,128)S(1)}, u32[]{:S(2)}, u32[]{:S(2)}) collective-permute-start(f32[32,1024]{1,0:T(8,128)S(1)} %get-tuple-element.16.refs_0_), channel_id=1, source_target_pairs={{8,11},{9,8},{0,1},{1,0},{10,9},{11,10},{2,3},{3,2},{12,15},{13,12... | collective-permute-start | bytes 393224 | tf_op jit(solution)/shard_map/ppermute | solution.py:253
  26.6 1.7 %collective-permute-start.11 = (f32[32,1024]{1,0:T(8,128)S(1)}, f32[32,1024]{1,0:T(8,128)S(1)}, u32[]{:S(2)}, u32[]{:S(2)}) collective-permute-start(f32[32,1024]{1,0:T(8,128)S(1)} %shard_map.89), channel_id=1, source_target_pairs={{0,1},{1,0},{2,3},{3,2},{4,5},{5,4},{6,7},{7,6},{8,9},{9,8},{10,11... | collective-permute-start | bytes 393224 | tf_op jit(solution)/shard_map/ppermute | solution.py:297
  28.2 8.1 %copy-start = (f32[1,256,256]{2,1,0:T(8,128)S(1)}, f32[1,256,256]{2,1,0:T(8,128)}, u32[]{:S(2)}) copy-start(f32[1,256,256]{2,1,0:T(8,128)} %param.9) | copy-start | bytes 786436
  28.2 8.1 %copy-start.1 = (f32[1,256]{1,0:T(1,128)S(1)}, f32[1,256]{1,0:T(1,128)}, u32[]{:S(2)}) copy-start(f32[1,256]{1,0:T(1,128)} %vec_momentum.1) | copy-start | bytes 3076
  28.2 8.1 %collective-permute-start.14 = (bf16[32,1408]{1,0:T(8,128)(2,1)S(1)}, bf16[32,1408]{1,0:T(8,128)(2,1)S(1)}, u32[]{:S(2)}, u32[]{:S(2)}) collective-permute-start(bf16[32,1408]{1,0:T(8,128)(2,1)S(1)} %shard_map.91.refs_0_), channel_id=1, source_target_pairs={{8,0},{17,1},{9,8},{16,17},{25,24},{24,25},{1,9},{0,16},{10,2},{19... | collective-permute-start | bytes 270344 | tf_op jit(solution)/shard_map/ppermute | solution.py:227
  31.7 4.6 %collective-permute-start.13 = (bf16[32,1408]{1,0:T(8,128)(2,1)S(1)}, bf16[32,1408]{1,0:T(8,128)(2,1)S(1)}, u32[]{:S(2)}, u32[]{:S(2)}) collective-permute-start(bf16[32,1408]{1,0:T(8,128)(2,1)S(1)} %shard_map.91.refs_0_), channel_id=1, source_target_pairs={{8,16},{17,9},{1,0},{0,1},{9,8},{16,17},{25,24},{24,25},{10,18},{1... | collective-permute-start | bytes 270344 | tf_op jit(solution)/shard_map/ppermute | solution.py:227
  32.0 4.3 %collective-permute-start.12 = (bf16[32,1408]{1,0:T(8,128)(2,1)S(1)}, bf16[32,1408]{1,0:T(8,128)(2,1)S(1)}, u32[]{:S(2)}, u32[]{:S(2)}) collective-permute-start(bf16[32,1408]{1,0:T(8,128)(2,1)S(1)} %shard_map.91.refs_0_), channel_id=1, source_target_pairs={{8,24},{17,25},{1,0},{0,1},{9,8},{16,17},{24,16},{25,9},{10,26},{1... | collective-permute-start | bytes 270344 | tf_op jit(solution)/shard_map/ppermute | solution.py:227
